TPU v7x, 32 devices: a whole 2x2x4 slice. The times are simulated.
32 devices in a mesh: dp: 4 (over z), fsdp: 8 (over y, x, core).
Axes of the slice: x: 2, y: 2, z: 4, core: 2. Of those that a mesh axis runs over, the one named last changes fastest.
Arguments:
- frames: bfloat16 [2, 32, 384, 512], P(None, ('dp', 'fsdp')), may hold values from -6 to 6
- upstream: bfloat16 [2, 32, 384, 512], P(None, ('dp', 'fsdp')), may hold values from -6 to 6
- utterance: int32 [2, 32, 24], P(None, ('dp', 'fsdp')), may hold values from 0 to 5, never falling along the last dimension, each value on 1 to 8 neighbouring positions
- first_gain: bfloat16 [512], P('fsdp'), may hold values from 0.099609375 to 1.8984375
- first_shift: bfloat16 [512], P('fsdp'), may hold values from -3 to 3
- project_in: bfloat16 [512, 1536], P('fsdp'), may hold values from -0.25 to 0.25
- query_bias: bfloat16 [512], P('fsdp'), may hold values from -3 to 3
- value_bias: bfloat16 [512], P('fsdp'), may hold values from -3 to 3
- project_out: bfloat16 [512, 512], P('fsdp'), may hold values from -0.75 to 0.75
- out_bias: bfloat16 [512], P('fsdp'), may hold values from -3 to 3
- second_gain: bfloat16 [512], P('fsdp'), may hold values from 0.099609375 to 1.8984375
- second_shift: bfloat16 [512], P('fsdp'), may hold values from -3 to 3
- up_weight: bfloat16 [512, 2048], P('fsdp'), may hold values from -0.25 to 0.25
- up_bias: bfloat16 [2048], P('fsdp'), may hold values from -3 to 3
- down_weight: bfloat16 [2048, 512], P('fsdp'), may hold values from -0.1875 to 0.1875
- down_bias: bfloat16 [512], P('fsdp'), may hold values from -3 to 3
Outputs:
- output: bfloat16 [2, 32, 384, 512], P(None, ('dp', 'fsdp'))
- grad_frames: float32 [2, 32, 384, 512], P(None, ('dp', 'fsdp'))
- grad_first_gain: float32 [512], P('fsdp')
- grad_first_shift: float32 [512], P('fsdp')
- grad_project_in: float32 [512, 1536], P('fsdp')
- grad_query_bias: float32 [512], P('fsdp')
- grad_value_bias: float32 [512], P('fsdp')
- grad_project_out: float32 [512, 512], P('fsdp')
- grad_out_bias: float32 [512], P('fsdp')
- grad_second_gain: float32 [512], P('fsdp')
- grad_second_shift: float32 [512], P('fsdp')
- grad_up_weight: float32 [512, 2048], P('fsdp')
- grad_up_bias: float32 [2048], P('fsdp')
- grad_down_weight: float32 [2048, 512], P('fsdp')
- grad_down_bias: float32 [512], P('fsdp')
Inputs may be any that keep to these rules, and one draw needn't show every extreme that they name: In each packed row the utterance numbers never fall, every utterance covers 1 to 8 consecutive segments, and some utterance covers exactly 8.
All inputs are finite; a program needn't handle non-finite values.
Results may differ from a plain program's by a relative error of at most 0.023.
Values may be sent and summed in bfloat16 or wider, within the bound.
No kernel may reach another device: no remote copies, remote signals or barrier semaphores. Data moves between devices by JAX's collectives and lax.ppermute only.
A program may use at most 192 MiB of HBM per device.

v0:
```python
import functools

import jax
import jax.numpy as jnp
from jax import lax
from jax.experimental import pallas as pl
from jax.experimental.pallas import tpu as pltpu
from jax.sharding import PartitionSpec as P

HEADS = 8
SEG = 16
RIGHT = 4
LEFT = 30
MEMS = 4
QB = 128
WIN = 176
SLOTS = 16
KEYS = WIN + SLOTS
TILE = 512
EXTRA = 16
BF = jnp.bfloat16
F32 = jnp.float32
HBM = pl.BlockSpec(memory_space=pl.ANY)
VMEM = pl.BlockSpec(memory_space=pltpu.VMEM)
LIMIT = 16 * 2**20


def nn(a, b):
    return lax.dot_general(a, b, (((1,), (0,)), ((), ())), preferred_element_type=F32)


def nt(a, b):
    return lax.dot_general(a, b, (((1,), (1,)), ((), ())), preferred_element_type=F32)


def tn(a, b):
    return lax.dot_general(a, b, (((0,), (0,)), ((), ())), preferred_element_type=F32)


def params(limit=LIMIT):
    return pltpu.CompilerParams(vmem_limit_bytes=limit)


def cost(micros):
    return pl.CostEstimate(flops=int(micros * 0.1e9), bytes_accessed=0, transcendentals=0)


def window(block, length):
    first = min(max(block * QB - 32, 0), length - WIN)
    slot = min(max(block * QB // SEG - MEMS, 0), length // SEG - SLOTS)
    return first, slot


def start_copies(copies):
    for copy in copies:
        copy.start()


def wait_copies(copies):
    for copy in copies:
        copy.wait()


def full(shape, dtype):
    return jax.ShapeDtypeStruct(shape, dtype)


def assemble(plan, parts, segments, sem):
    me = lax.axis_index("fsdp")
    copies = []
    for number, (offset, relative, first, rows, count) in enumerate(plan):
        for each in range(count):
            device = jnp.bitwise_xor(me, offset) if relative else each
            for start, height, target, column in segments:
                low, high = max(first, start), min(first + rows, start + height)
                if low < high:
                    place = pl.multiple_of(device * height, height) + low - start
                    source = parts[number].at[pl.ds(each * rows + low - first, high - low), :]
                    wide = source.shape[1]
                    copies.append(
                        pltpu.make_async_copy(
                            source, target.at[pl.ds(place, high - low), pl.ds(column, wide)], sem
                        )
                    )
    return copies


def pieces_into(grads):
    if len(grads.shape) == 2:

        def put_whole(rows, columns, value, device, within):
            grads[rows, columns] = value

        return put_whole
    me = lax.axis_index("fsdp")
    chips = [jnp.bitwise_xor(me // 2, chip) for chip in range(4)]
    cores = [jnp.bitwise_xor(lax.rem(me, 2), core) for core in range(2)]

    def put(rows, columns, value, device, within):
        grads[cores[device % 2], chips[device // 2], within[0], within[1]] = value

    return put


def put_rows(put, value, width, columns):
    for device in range(value.shape[0] // width):
        rows = slice(device * width, (device + 1) * width)
        put(rows, columns, value[rows], device, (slice(0, width), columns))


def stats(value):
    mean = jnp.mean(value, axis=-1, keepdims=True)
    offset = value - mean
    spread = jnp.mean(offset * offset, axis=-1, keepdims=True)
    scale = lax.rsqrt(spread + 1e-05)
    return offset * scale, scale


def averages(length):
    blocks = length // QB
    rows = blocks * SLOTS
    row = lax.broadcasted_iota(jnp.int32, (rows, length), 0)
    seg = lax.broadcasted_iota(jnp.int32, (rows, length), 1) // SEG
    slot = row % SLOTS
    for block in range(blocks):
        first = window(block, length)[1]
        slot = slot + jnp.where(row // SLOTS == block, first, 0)
    return jnp.where(slot == seg, 1.0 / SEG, 0.0).astype(BF)


def head_pair(value):
    lane = lax.broadcasted_iota(jnp.int32, value.shape, 1)
    zero = jnp.zeros_like(value)
    half = value.shape[1] // 2
    return jnp.concatenate(
        [jnp.where(lane < half, value, zero), jnp.where(lane >= half, value, zero)], axis=0
    )


def diagonal(value):
    half = value.shape[0] // 2
    return jnp.concatenate([value[:half, :QB], value[half:, QB:]], axis=0)


def visible_bias(bias_ref, utter_ref, row, nsegs):
    length = nsegs * SEG
    key = lax.broadcasted_iota(jnp.int32, (KEYS, QB), 0)
    query = lax.broadcasted_iota(jnp.int32, (KEYS, QB), 1)
    segs = QB // SEG
    starts = [jnp.int32(0)]
    for seg in range(1, nsegs):
        same = utter_ref[row, seg] == utter_ref[row, seg - 1]
        starts.append(jnp.where(same, starts[-1], seg))
    for block in range(length // QB):
        first, slot = window(block, length)
        lower = jnp.zeros((KEYS, QB), jnp.int32)
        upper = jnp.zeros((KEYS, QB), jnp.int32)
        for part in range(segs):
            seg = block * segs + part
            more = jnp.int32(0)
            if seg + 1 < nsegs:
                more = jnp.where(utter_ref[row, seg + 1] == utter_ref[row, seg], RIGHT, 0)
            frame_low = jnp.maximum(seg * SEG - LEFT, starts[seg] * SEG) - first
            frame_high = seg * SEG + SEG + more - first
            slot_low = jnp.maximum(seg - MEMS, starts[seg]) - slot + WIN
            slot_high = jnp.int32(seg - slot + WIN)
            here = query // SEG == part
            lower = jnp.where(here, jnp.where(key < WIN, frame_low, slot_low), lower)
            upper = jnp.where(here, jnp.where(key < WIN, frame_high, slot_high), upper)
        seen = (key >= lower) & (key < upper)
        bias_ref[block] = jnp.where(seen, 0.0, -1e9)


def call(body, name, micros, ins, outs, scratch, args, limit=LIMIT):
    kinds = [HBM if by_copy else VMEM for _, by_copy in outs]
    return pl.pallas_call(
        body,
        in_specs=[VMEM] * ins + [HBM] * (len(args) - ins),
        out_specs=kinds,
        out_shape=[shape for shape, _ in outs],
        scratch_shapes=scratch,
        compiler_params=params(limit),
        name=name,
        cost_estimate=cost(micros),
    )(*args)


def attention(q_ref, k_ref, v_ref, p_ref, bias, att_ref, att, length):
    for block in range(length // QB):
        first, _ = window(block, length)
        rows = slice(block * QB, (block + 1) * QB)
        own = slice(length + block * SLOTS, length + (block + 1) * SLOTS)
        for pair in range(HEADS // 2):
            lanes = slice(pair * 128, (pair + 1) * 128)
            keys = jnp.concatenate([k_ref[first : first + WIN, lanes], k_ref[own, lanes]], axis=0)
            vals = jnp.concatenate([v_ref[first : first + WIN, lanes], v_ref[own, lanes]], axis=0)
            seen = bias[block]
            scores = nt(keys, head_pair(q_ref[rows, lanes]))
            scores = scores + jnp.concatenate([seen, seen], axis=1)
            top = jnp.max(scores, axis=0, keepdims=True)
            raised = jnp.exp(scores - top)
            probs = (raised * (1.0 / jnp.sum(raised, axis=0, keepdims=True))).astype(BF)
            p_ref[block, pair] = probs
            found = diagonal(tn(vals, probs))
            att_ref[lanes, rows] = found.astype(BF)
            att[rows, lanes] = found.T.astype(BF)


def early_body(utter, x, dy, units, biases, dyt):
    rows, length, _ = x.shape
    for row in range(rows):
        units[row] = stats(x[row].astype(F32))[0]
        visible_bias(biases.at[row], utter, row, length // SEG)
    dyt[...] = dy[...].T


def early(utter, x, dy):
    rows, length, model = x.shape
    return pl.pallas_call(
        early_body,
        in_specs=[pl.BlockSpec(memory_space=pltpu.SMEM), VMEM, VMEM],
        out_specs=[VMEM] * 3,
        out_shape=[
            full((rows, length, model), F32),
            full((rows, length // QB, KEYS, QB), F32),
            full((model, rows * length), BF),
        ],
        compiler_params=params(),
        name="early",
        cost_estimate=cost(2),
    )(utter, x, dy)


def front_body(row, first_call, plan, width, x, units, biases, vecs_in, w_in_in, w_out_in, *refs):
    nparts = len(plan) if first_call else 0
    parts = refs[:nparts]
    outs = refs[nparts:]
    if first_call:
        vecs, w_in, w_out, *outs = outs
    else:
        vecs, w_in, w_out = vecs_in, w_in_in, w_out_in
    (q_out, k_out, v_out, wide_out, p_out, att_out, resid_out, n2_out, att, *outs) = outs
    length, model = x.shape[1], x.shape[2]
    value = x[row].astype(F32)
    if first_call:
        small, sem = outs
        segments = [(band * width, width, w_in, band * model) for band in range(3)]
        segments += [(3 * width, width, w_out, 0), (4 * width, EXTRA, small, 0)]
        copies = assemble(plan, parts, segments, sem)
        start_copies(copies)
    unit = units[row]
    if first_call:
        wait_copies(copies)
        total = jnp.zeros((8, model), F32)
        ups = [jnp.zeros((1, model), F32) for _ in range(4)]
        for piece in range(model // width):
            found = small[piece * EXTRA : (piece + 1) * EXTRA].astype(F32)
            total = total + pltpu.roll(found, piece * width, 1)[:8]
            for part in range(4):
                place = (piece * 4 + part) * width
                ups[place // model] += pltpu.roll(found, place % model, 1)[8 + part : 9 + part]
        vecs[0:8] = total
        for part in range(4):
            vecs[8 + part : 9 + part] = ups[part]
        vecs[12:16] = jnp.zeros((4, model), F32)
    normed = (unit * vecs[0:1] + vecs[1:2]).astype(BF)
    summary = nn(averages(length), normed).astype(BF)
    wide = jnp.concatenate([normed, summary], axis=0)
    wide_out[...] = wide.T
    q_out[...] = ((nn(normed, w_in[:, :model]) + vecs[2:3]).astype(BF).astype(F32) * 0.125).astype(BF)
    k_out[...] = nn(wide, w_in[:, model : 2 * model]).astype(BF)
    v_out[...] = (nn(wide, w_in[:, 2 * model :]) + vecs[3:4]).astype(BF)
    attention(q_out, k_out, v_out, p_out, biases.at[row], att_out, att, length)
    resid = value + nn(att[...], w_out[...]) + vecs[4:5]
    resid_out[...] = resid
    unit, _ = stats(resid)
    n2_out[...] = (unit * vecs[5:6] + vecs[6:7]).astype(BF)


def front(row, x, units, biases, vecs, w_in, w_out, plan, parts, width):
    _, length, model = x.shape
    blocks = length // QB
    wide = length + blocks * SLOTS
    first_call = vecs is None
    outs = [
        full((length, model), BF),
        full((wide, model), BF),
        full((wide, model), BF),
        full((model, wide), BF),
        full((blocks, HEADS // 2, KEYS, 2 * QB), BF),
        full((model, length), BF),
        full((length, model), F32),
        full((length, model), BF),
    ]
    scratch = [pltpu.VMEM((length, model), BF)]
    if first_call:
        outs = [full((16, model), F32), full((model, 3 * model), BF), full((model, model), BF)] + outs
        pieces = model // width
        scratch += [pltpu.VMEM((pieces * EXTRA, model), BF), pltpu.SemaphoreType.DMA]
        args = [x, units, biases] + list(parts)
        specs = [VMEM] * 3 + [HBM] * len(parts)

        def body(x, units, biases, *refs):
            front_body(row, True, plan, width, x, units, biases, None, None, None, *refs)
    else:
        args = [x, units, biases, vecs, w_in, w_out]
        specs = [VMEM] * 6
        body = functools.partial(front_body, row, False, plan, width)
    return pl.pallas_call(
        body,
        in_specs=specs,
        out_specs=[VMEM] * len(outs),
        out_shape=outs,
        scratch_shapes=scratch,
        compiler_params=params(),
        name=f"front{row}",
        cost_estimate=cost(7),
    )(*args)


def gelu_both(v):
    c = 0.7978845608028654
    square = v * v
    bent = jnp.tanh(c * v * (1.0 + 0.044715 * square))
    half = 0.5 + 0.5 * bent
    slope = half + 0.5 * v * (1.0 - bent * bent) * (c * (1.0 + 3 * 0.044715 * square))
    return v * half, slope


def middle_body(rows, plan, width, *refs):
    n2s = refs[:rows]
    dyt, vecs, *refs = refs[rows:]
    parts = refs[: len(plan)]
    hidden, slopes, up, grads, sem = refs[len(plan) :]
    put = pieces_into(grads)
    model, tokens = dyt.shape
    ff = up.shape[1]
    tall = ff * width // model
    copies = assemble(plan, parts, [(0, width, up, 0)], sem)
    start_copies(copies)
    wait_copies(copies)
    length = n2s[0].shape[0]
    step = length
    for tile in range(ff // TILE):
        cols = slice(tile * TILE, (tile + 1) * TILE)
        for chunk in range(tokens // step):
            rows = slice(chunk * step, (chunk + 1) * step)
            at = chunk * step % length
            u = nn(n2s[chunk * step // length][at : at + step], up[:, cols]) + vecs[8 + tile : 9 + tile]
            value, slope = gelu_both(u)
            hidden[rows, cols] = value.astype(BF)
            slopes[rows, cols] = slope.astype(BF)
        grad = nn(dyt[...], hidden[:, cols]).astype(BF)
        for part in range(TILE // tall):
            inner_cols = slice(part * tall, (part + 1) * tall)
            outer_cols = slice(tile * TILE + part * tall, tile * TILE + (part + 1) * tall)
            device = tile * TILE // tall + part
            rows = slice(0, model)
            put(rows, outer_cols, grad[:, inner_cols], device, (rows, slice(0, tall)))


def middle(n2s, dyt, vecs, parts, plan, width, ff, fast):
    model, tokens = dyt.shape
    tall = ff * width // model
    shape = (2, 4, model, tall) if fast else (model, ff)
    outs = [
        (full((tokens, ff), BF), False),
        (full((tokens, ff), BF), False),
        (full((model, ff), BF), False),
        (full(shape, BF), False),
    ]
    scratch = [pltpu.SemaphoreType.DMA]
    body = functools.partial(middle_body, len(n2s), plan, width)
    return call(body, "middle", 8, len(n2s) + 2, outs, scratch, [*n2s, dyt, vecs, *parts])


def turn_body(plan, dy, slopes, *refs):
    parts = refs[: len(plan)]
    du, ub, down, sem = refs[len(plan) :]
    tokens, model = dy.shape
    ff = down.shape[0]
    tall = plan[0][3]
    length = dy.shape[0] // 2
    copies = assemble(plan, parts, [(0, tall, down, 0)], sem)
    start_copies(copies)
    wait_copies(copies)
    step = length
    for tile in range(ff // TILE):
        cols = slice(tile * TILE, (tile + 1) * TILE)
        sums = jnp.zeros((1, TILE), F32)
        for chunk in range(tokens // step):
            rows = slice(chunk * step, (chunk + 1) * step)
            back = nt(dy[rows], down[cols]).astype(BF).astype(F32) * slopes[rows, cols].astype(F32)
            du[rows, cols] = back.astype(BF)
            sums = sums + jnp.sum(back, axis=0, keepdims=True)
        ub[tile : tile + 1] = sums


def turn(dy, slopes, parts, plan):
    tokens, model = dy.shape
    ff = slopes.shape[1]
    outs = [
        (full((tokens, ff), BF), False),
        (full((ff // TILE, TILE), F32), False),
        (full((ff, model), BF), False),
    ]
    args = [dy, slopes, *parts]
    return call(functools.partial(turn_body, plan), "turn", 5, 2, outs, [pltpu.SemaphoreType.DMA], args)


def rise_body(rows, width, *refs):
    n2s = refs[:rows]
    du, grads, n2t = refs[rows:]
    length, model = n2s[0].shape
    ff = du.shape[1]
    put = pieces_into(grads)
    for row in range(rows):
        n2t[:, row * length : (row + 1) * length] = n2s[row][...].T
    for tile in range(ff // TILE):
        cols = slice(tile * TILE, (tile + 1) * TILE)
        put_rows(put, nn(n2t[...], du[:, cols]).astype(BF), width, cols)


def rise(n2s, du, width, fast):
    tokens, ff = du.shape
    model = n2s[0].shape[1]
    shape = (2, 4, width, ff) if fast else (model, ff)
    scratch = [pltpu.VMEM((model, tokens), BF)]
    body = functools.partial(rise_body, len(n2s), width)
    args = [*n2s, du]
    return call(body, "rise", 4, len(args), [(full(shape, BF), False)], scratch, args)[0]


def norm_back(grad, unit, scale):
    first = jnp.mean(grad, axis=-1, keepdims=True)
    second = jnp.mean(grad * unit, axis=-1, keepdims=True)
    return scale * (grad - first - unit * second)


def back_body(rows, *refs):
    resids = refs[:rows]
    du, dy, vecs, up, w_out, dresid, datt, sums = refs[rows:]
    tokens, model = dy.shape
    length = resids[0].shape[0]
    step = length
    gains = jnp.zeros((1, model), F32)
    shifts = jnp.zeros((1, model), F32)
    biases = jnp.zeros((1, model), F32)
    downs = jnp.zeros((1, model), F32)
    for chunk in range(tokens // step):
        rows = slice(chunk * step, (chunk + 1) * step)
        at = chunk * step % length
        grad = nt(du[rows], up[...])
        unit, scale = stats(resids[chunk * step // length][at : at + step])
        gains = gains + jnp.sum(grad * unit, axis=0, keepdims=True)
        shifts = shifts + jnp.sum(grad, axis=0, keepdims=True)
        top = dy[rows].astype(F32)
        downs = downs + jnp.sum(top, axis=0, keepdims=True)
        total = top + norm_back(grad * vecs[5:6], unit, scale)
        biases = biases + jnp.sum(total, axis=0, keepdims=True)
        dresid[rows] = total
        datt[rows] = nt(total.astype(BF), w_out[...]).astype(BF)
    sums[0:1] = gains
    sums[1:2] = shifts
    sums[2:3] = biases
    sums[3:4] = downs


def back(resids, du, dy, vecs, up, w_out):
    tokens, model = dy.shape
    outs = [
        (full((tokens, model), F32), False),
        (full((tokens, model), BF), False),
        (full((4, model), F32), False),
    ]
    args = [*resids, du, dy, vecs, up, w_out]
    return call(functools.partial(back_body, len(resids)), "back", 8, len(args), outs, [], args)


def rear_body(row, q, k, v, p, datt, mixed, sums, dk, dv):
    length, model = q.shape
    extent = k.shape[0]
    base = row * length
    dk[...] = jnp.zeros_like(dk)
    dv[...] = jnp.zeros_like(dv)
    mixed[length:extent, 0:model] = jnp.zeros((extent - length, model), BF)
    for block in range(length // QB):
        first, _ = window(block, length)
        rows = slice(block * QB, (block + 1) * QB)
        own = slice(length + block * SLOTS, length + (block + 1) * SLOTS)
        span = slice(first, first + WIN)
        for pair in range(HEADS // 2):
            lanes = slice(pair * 128, (pair + 1) * 128)
            keys = jnp.concatenate([k[span, lanes], k[own, lanes]], axis=0)
            vals = jnp.concatenate([v[span, lanes], v[own, lanes]], axis=0)
            queries = head_pair(q[rows, lanes])
            tops = head_pair(datt[base + block * QB : base + (block + 1) * QB, lanes])
            probs = p[block, pair]
            wides = probs.astype(F32)
            back = nt(vals, tops)
            inner = jnp.sum(wides * back, axis=0, keepdims=True)
            dscores = (wides * (back - inner)).astype(BF)
            gv = nn(probs, tops)
            gk = nn(dscores, queries)
            dv[span, lanes] += gv[:WIN]
            dv[own, lanes] = gv[WIN:]
            dk[span, lanes] += gk[:WIN]
            dk[own, lanes] = gk[WIN:]
            gq = diagonal(tn(keys, dscores)).T * 0.125
            mixed[rows, lanes] = gq.astype(BF)
    mixed[:, model : 2 * model] = dk[...].astype(BF)
    mixed[:, 2 * model :] = dv[...].astype(BF)
    sums[0:1] = jnp.sum(mixed[:, 0:model].astype(F32), axis=0, keepdims=True)
    sums[1:2] = jnp.sum(mixed[:, 2 * model :].astype(F32), axis=0, keepdims=True)


def rear(row, q, k, v, p, datt):
    length, model = q.shape
    extent = k.shape[0]
    outs = [(full((extent, 3 * model), BF), False), (full((2, model), F32), False)]
    scratch = [pltpu.VMEM((extent, model), F32), pltpu.VMEM((extent, model), F32)]
    body = functools.partial(rear_body, row)
    return call(body, f"rear{row}", 7, 5, outs, scratch, [q, k, v, p, datt])


def base_body(rows, width, x, dresid, vecs, w_in, gub, back_sums, *refs):
    mixeds = refs[:rows]
    rear_sums = refs[rows : 2 * rows]
    wides = refs[2 * rows : 3 * rows]
    atts = refs[3 * rows : 4 * rows]
    grads, dx, sums = refs[4 * rows :]
    length, model = x.shape[1], x.shape[2]
    put = pieces_into(grads)
    for tile in range(3):
        cols = slice(tile * model, (tile + 1) * model)
        total = nn(wides[0][...], mixeds[0][:, cols])
        for row in range(1, rows):
            total = total + nn(wides[row][...], mixeds[row][:, cols])
        put_rows(put, total.astype(BF), width, cols)
    total = nn(atts[0][...], dresid[0:length].astype(BF))
    for row in range(1, rows):
        total = total + nn(atts[row][...], dresid[row * length : (row + 1) * length].astype(BF))
    put_rows(put, total.astype(BF), width, slice(3 * model, 4 * model))
    average = averages(length)
    gains = jnp.zeros((1, model), F32)
    shifts = jnp.zeros((1, model), F32)
    for row in range(rows):
        unit, scale = stats(x[row].astype(F32))
        grad = nt(mixeds[row][...], w_in[...])
        grad = grad[:length] + tn(average, grad[length:].astype(BF))
        gains = gains + jnp.sum(grad * unit, axis=0, keepdims=True)
        shifts = shifts + jnp.sum(grad, axis=0, keepdims=True)
        dx[row] = dresid[row * length : (row + 1) * length] + norm_back(grad * vecs[0:1], unit, scale)
    sums[0:1] = gains
    sums[1:2] = shifts
    sums[2:4] = wide_sum(*[part[...] for part in rear_sums])
    sums[4:8] = back_sums[...]
    sums[8:12] = gub[...]
    sums[12:16] = jnp.zeros((4, model), F32)
    if len(grads.shape) == 4:
        for device in range(model // width):
            block = [sums[0:8, device * width : (device + 1) * width]]
            for part in range(4):
                place = (device * 4 + part) * width
                row, low = 8 + place // model, place % model
                block.append(sums[row : row + 1, low : low + width])
            block.append(jnp.zeros((4, width), F32))
            block = jnp.concatenate(block, axis=0)
            block = jnp.concatenate([block, jnp.zeros((16, 128 - width), F32)], axis=1)
            put(None, None, block.astype(BF), device, (slice(0, 16), slice(4 * model, 4 * model + 128)))
            put(
                None,
                None,
                jnp.zeros((width - 16, 128), BF),
                device,
                (slice(16, width), slice(4 * model, 4 * model + 128)),
            )


def base(x, dresid, vecs, w_in, gub, back_sums, mixeds, rear_sums, wides, atts, width, fast):
    rows, length, model = x.shape
    shape = (2, 4, width, 4 * model + 128) if fast else (model, 4 * model)
    outs = [
        (full(shape, BF), False),
        (full((rows, length, model), F32), False),
        (full((16, model), F32), False),
    ]
    args = [x, dresid, vecs, w_in, gub, back_sums, *mixeds, *rear_sums, *wides, *atts]
    return call(functools.partial(base_body, rows, width), "base", 6, len(args), outs, [], args)


def finish_body(rows, vecs, hidden, down, *refs):
    resids = refs[:rows]
    out = refs[rows]
    length = resids[0].shape[0]
    step = length
    for chunk in range(hidden.shape[0] // step):
        rows = slice(chunk * step, (chunk + 1) * step)
        at = chunk * step % length
        resid = resids[chunk * step // length][at : at + step]
        out[rows] = (resid + nn(hidden[rows], down[...]) + vecs[7:8]).astype(BF)


def finish(vecs, hidden, down, resids):
    outs = [(full((hidden.shape[0], down.shape[1]), BF), False)]
    args = [vecs, hidden, down, *resids]
    return call(functools.partial(finish_body, len(resids)), "finish", 4, len(args), outs, [], args)[0]


def along(value, offset):
    return lax.ppermute(value, "fsdp", [(i, i ^ offset) for i in range(8)])


def across(value, offset, size):
    return lax.ppermute(value, "dp", [(i, i ^ offset) for i in range(size)])


def pack_body(*refs):
    sources, out = refs[:11], refs[11]
    w_in, w_out, *rows, sem = refs[12:]
    width, model = w_out.shape
    targets = [w_in, w_out, *rows]
    copies = [pltpu.make_async_copy(a, b, sem) for a, b in zip(sources, targets)]
    start_copies(copies)
    out[4 * width :] = jnp.zeros((EXTRA, model), BF)
    wait_copies(copies)
    for band in range(3):
        out[band * width : (band + 1) * width] = w_in[:, band * model : (band + 1) * model]
    out[3 * width : 4 * width] = w_out[...]
    lines = [row[...].astype(F32).reshape(1, width) for row in rows[:8]]
    bias = rows[8][...].astype(F32).reshape(1, 4 * width)
    lines += [bias[:, at * width : (at + 1) * width] for at in range(4)]
    lines += [jnp.zeros((4, width), F32)]
    out[4 * width :, 0:width] = jnp.concatenate(lines, axis=0).astype(BF)


def pack(project_in, project_out, vectors, up_bias):
    width, model = project_out.shape
    outs = [(full((4 * width + EXTRA, model), BF), False)]
    args = [project_in, project_out, *vectors, up_bias]
    scratch = [pltpu.VMEM(arg.shape, BF) for arg in args] + [pltpu.SemaphoreType.DMA]
    return call(pack_body, "pack", 2, 0, outs, scratch, args, 60 * 2**20)[0]


def settle_body(width, tall, small, *refs):
    me = lax.axis_index("fsdp")
    value = small[...]
    model = value.shape[1]
    turned = pltpu.roll(value, lax.rem(model - me * width, model), 1)
    for row, out in enumerate(refs[:8]):
        out[...] = turned[row : row + 1, 0:width].reshape(width)
    place = me * tall
    wide = jnp.zeros((1, model), F32)
    for row in range(4):
        wide = jnp.where(place // model == row, value[8 + row : 9 + row], wide)
    wide = jnp.concatenate([wide] * 8, axis=0)
    turned = pltpu.roll(wide, lax.rem(model - lax.rem(place, model), model), 1)
    refs[8][...] = turned[0:1, 0:tall].reshape(tall)


def settle(small, width, tall):
    outs = [(full((width,), F32), False)] * 8 + [(full((tall,), F32), False)]
    return call(functools.partial(settle_body, width, tall), "settle", 2, 1, outs, [], [small])


def wide_sum(*values):
    total = values[0].astype(F32)
    for value in values[1:]:
        total = total + value.astype(F32)
    return total


def plus(*values):
    def body(*refs):
        refs[-1][...] = wide_sum(*[ref[...] for ref in refs[:-1]]).astype(refs[-1].dtype)

    outs = [(full(values[0].shape, values[0].dtype), False)]
    return call(body, "plus", 1, len(values), outs, [], values)[0]


def plus_here(both, there):
    def body(both, there, out):
        out[...] = wide_sum(both[0], there[...]).astype(BF)

    return call(body, "plus", 1, 2, [(full(there.shape, BF), False)], [], [both, there])[0]


def own_sum(held, *others):
    return wide_sum(held[0], *[other[...] for other in others]).astype(BF)


def cross_halves(held):
    def body(held, to_x, to_y):
        half = held.shape[1] // 2
        to_x[0] = held[1, :half]
        to_x[1] = held[3, :half]
        to_y[0] = held[2, half:]
        to_y[1] = held[3, half:]

    _, rows, columns = held.shape
    outs = [(full((2, rows // 2, columns), BF), False)] * 2
    return call(body, "cross_halves", 1, 1, outs, [], [held])


def second(held, from_x, from_y):
    def body(held, from_x, from_y, to_x, to_y):
        half = held.shape[1] // 2
        to_x[...] = wide_sum(held[1, half:], from_y[1]).astype(BF)
        to_y[...] = wide_sum(held[2, :half], from_x[1]).astype(BF)

    outs = [(full(from_x.shape[1:], BF), False)] * 2
    return call(body, "second", 1, 3, outs, [], [held, from_x, from_y])


def hop_halves(*args):
    def body(held, from_x, from_y, last_x, last_y, keep, send):
        half = keep.shape[0]
        top = wide_sum(held[0, :half], from_x[0], last_y[...]).astype(BF)
        bottom = wide_sum(held[0, half:], from_y[0], last_x[...]).astype(BF)
        odd = odd_plane()

        @pl.when(odd)
        def _():
            keep[...] = bottom
            send[...] = top

        @pl.when(jnp.logical_not(odd))
        def _():
            keep[...] = top
            send[...] = bottom

    _, rows, columns = args[0].shape
    outs = [(full((rows // 2, columns), BF), False)] * 2
    return call(body, "hop_halves", 1, 5, outs, [], args)


def odd_plane():
    return lax.rem(lax.axis_index("dp"), 2) == 1


def by_halves(*args):
    def body(*refs):
        keep, send = refs[-2:]
        total = own_sum(*refs[:-2])
        half = keep.shape[0]
        odd = odd_plane()

        @pl.when(odd)
        def _():
            keep[...] = total[half:]
            send[...] = total[:half]

        @pl.when(jnp.logical_not(odd))
        def _():
            keep[...] = total[:half]
            send[...] = total[half:]

    rows, columns = args[1].shape
    outs = [(full((rows // 2, columns), BF), False)] * 2
    return call(body, "by_halves", 1, len(args), outs, [], args)


def by_quarters(*args):
    def body(*refs):
        outs = refs[-5:-1]
        whole = refs[-1]
        whole[...] = own_sum(*refs[:-5])
        rows = outs[0].shape[0]
        me = lax.axis_index("dp")
        for offset, out in enumerate(outs):
            place = pl.multiple_of(jnp.bitwise_xor(me, offset) * rows, rows)
            out[...] = whole[pl.ds(place, rows), :]

    rows, columns = args[1].shape
    outs = [(full((rows // 4, columns), BF), False)] * 4
    scratch = [pltpu.VMEM((rows, columns), BF)]
    return call(body, "by_quarters", 1, len(args), outs, scratch, args)


def last_down(keep, other):
    def body(keep, other, out):
        half = keep.shape[0]
        odd = odd_plane()

        @pl.when(odd)
        def _():
            out[:, :half] = other[...].astype(F32).T
            out[:, half:] = keep[...].astype(F32).T

        @pl.when(jnp.logical_not(odd))
        def _():
            out[:, :half] = keep[...].astype(F32).T
            out[:, half:] = other[...].astype(F32).T

    half, tall = keep.shape
    return call(body, "last_down", 1, 2, [(full((tall, 2 * half), F32), False)], [], [keep, other])[0]


def last_up(keep, other):
    def body(keep, other, out):
        half = keep.shape[0]
        odd = odd_plane()

        @pl.when(odd)
        def _():
            out[:half] = other[...].astype(F32)
            out[half:] = keep[...].astype(F32)

        @pl.when(jnp.logical_not(odd))
        def _():
            out[:half] = keep[...].astype(F32)
            out[half:] = other[...].astype(F32)

    half, ff = keep.shape
    return call(body, "last_up", 1, 2, [(full((2 * half, ff), F32), False)], [], [keep, other])[0]


def last_in(quarters, model, width, tall):
    def body(*refs):
        parts, g_in, g_out, small = refs[:4], refs[4], refs[5], refs[15]
        vectors = refs[6:15]
        rows = parts[0].shape[0]
        me = lax.axis_index("dp")
        for offset, part in enumerate(parts):
            place = pl.multiple_of(jnp.bitwise_xor(me, offset) * rows, rows)
            g_in[pl.ds(place, rows), :] = part[:, : 3 * model].astype(F32)
            g_out[pl.ds(place, rows), :] = part[:, 3 * model : 4 * model].astype(F32)
            small[pl.ds(place, rows), :] = part[:, 4 * model :].astype(F32)
        for row in range(8):
            vectors[row][...] = small[row : row + 1, 0:width].reshape(width)
        wide = jnp.concatenate([small[8 + part : 9 + part, 0:width] for part in range(4)], axis=1)
        vectors[8][...] = wide.reshape(tall)

    outs = [(full((width, 3 * model), F32), False), (full((width, model), F32), False)]
    outs += [(full((width,), F32), False)] * 8 + [(full((tall,), F32), False)]
    scratch = [pltpu.VMEM((width, 128), F32)]
    return call(body, "last_in", 1, 4, outs, scratch, quarters)


def after(value, *others):
    return lax.optimization_barrier((value,) + others)[0]


def whole_plan(rows, size):
    return [(0, False, 0, rows, size)]


def near_plan(rows):
    return [(offset, True, 0, rows, 1) for offset in (0, 1, 2, 4, 6, 3, 5, 7)]


def shards(
    group,
    frames,
    upstream,
    utterance,
    first_gain,
    first_shift,
    project_in,
    query_bias,
    value_bias,
    project_out,
    out_bias,
    second_gain,
    second_shift,
    up_weight,
    up_bias,
    down_weight,
    down_bias,
):
    micro, nrows, length, model = frames.shape
    rows = micro * nrows
    width = project_out.shape[0]
    size = model // width
    ff = up_weight.shape[1]
    tall = ff // size
    x = frames.reshape(rows, length, model)
    dy = upstream.reshape(rows * length, model)
    utter = utterance.reshape(rows, length // SEG)
    vectors = (first_gain, first_shift, query_bias, value_bias, out_bias, second_gain, second_shift, down_bias)
    fast = size == 8 and group == 4 and rows == 2
    packed = pack(project_in, project_out, vectors, up_bias)
    if fast:
        plan_a, plan_u, plan_d = near_plan(packed.shape[0]), near_plan(width), near_plan(tall)
        a2, a4, a6, a1 = [along(packed, offset) for offset in (2, 4, 6, 1)]
        units, biases, dyt = early(after(utter, a1), x, dy)
        a2, a4, a6, dyt = lax.optimization_barrier((a2, a4, a6, dyt))
        up_piece = after(up_weight, a2, a4, a6)
        u2, u4, u1 = along(up_piece, 2), along(up_piece, 4), along(up_piece, 1)
        parts_a = [packed, a1, a2, a4, a6, along(a2, 1), along(a4, 1)] + [along(a6, 1)]
        u6 = along(up_piece, 6)
        first = x
    else:
        plan_a, plan_u, plan_d = whole_plan(packed.shape[0], size), whole_plan(width, size), whole_plan(tall, size)
        parts_a = [lax.all_gather(packed, "fsdp", axis=0, tiled=True)]
        parts_u = [lax.all_gather(up_weight, "fsdp", axis=0, tiled=True)]
        parts_d = [lax.all_gather(down_weight, "fsdp", axis=0, tiled=True)]
        first = x
        units, biases, dyt = early(utter, x, dy)
    saved = []
    vecs, w_in, w_out, *first = front(0, first, units, biases, None, None, None, plan_a, parts_a, width)
    saved.append(first)
    held = vecs
    if fast:
        held = vecs
    for row in range(1, rows):
        saved.append(front(row, x, units, biases, held, w_in, w_out, plan_a, None, width))
    qs, ks, vs, wides, ps, atts, resids, n2s = zip(*saved)
    if fast:
        down_piece = after(down_weight, n2s[0])
        d2, d4 = along(down_piece, 2), along(down_piece, 4)
        *u_got, done = lax.optimization_barrier((u2, u4, u6, n2s[1]))
        parts_u = [up_piece, u1, *u_got] + [along(part, 1) for part in u_got[:2]] + [along(u_got[2], 1)]
        d2, d4, down_piece, done = lax.optimization_barrier((d2, d4, down_piece, done))
        held = after(vecs, d2, d4)
        d3, d5, d6, d1 = along(d2, 1), along(d4, 1), along(down_piece, 6), along(down_piece, 1)
    hidden, slopes, up, gdown = middle(n2s, dyt, held, parts_u, plan_u, width, ff, fast)
    if fast:
        d6 = after(d6, slopes)
        parts_d = [down_piece, d1, d2, d4, d6, d3, d5, along(d6, 1)]
    if fast:
        du, gub, down = turn(dy, slopes, parts_d, plan_d)
        d_core = along(after(gdown, gub)[1], 1)
        gup = rise(n2s, du, width, fast)
        d_sum = plus_here(gdown, after(d_core, gup))
        to_x, to_y = cross_halves(d_sum)
        d_x, d_y = along(to_x, 2), along(to_y, 4)
        u_core = along(gup[1], 1)
        dresid, datt, sums2 = back(resids, after(du, to_x), dy, vecs, up, w_out)
        u_core, done = lax.optimization_barrier((u_core, sums2))
        u_sum = plus_here(gup, u_core)
        to_x, to_y = cross_halves(u_sum)
        u_x, u_y = along(to_x, 2), along(to_y, 4)
        mixed0, sums0 = rear(0, after(qs[0], to_x), ks[0], vs[0], ps[0], datt)
        d_x, d_y, done = lax.optimization_barrier((d_x, d_y, sums0))
        to_x, to_y = second(d_sum, d_x, d_y)
        d_x2, d_y2 = along(to_x, 2), along(to_y, 4)
        mixed1, sums1 = rear(1, after(qs[1], to_x), ks[1], vs[1], ps[1], datt)
        u_x, u_y, d_x2, d_y2, done = lax.optimization_barrier((u_x, u_y, d_x2, d_y2, sums1))
        to_x, to_y = second(u_sum, u_x, u_y)
        u_x2, u_y2 = along(to_x, 2), along(to_y, 4)
        d_keep, d_send = hop_halves(d_sum, d_x, d_y, d_x2, d_y2)
        d_z = across(d_send, 1, group)
        mixeds = (mixed0, mixed1)
        out = finish(after(vecs, sums1), hidden, down, resids)
        gin, dx, small = base(
            x,
            after(dresid, to_x, d_send, out),
            vecs,
            w_in,
            gub,
            sums2,
            mixeds,
            (sums0, sums1),
            wides,
            atts,
            width,
            fast,
        )
        u_x2, u_y2, d_z, done = lax.optimization_barrier((u_x2, u_y2, d_z, small))
        u_keep, u_send = hop_halves(u_sum, u_x, u_y, u_x2, u_y2)
        u_z = across(u_send, 1, group)
        d_keep = plus(d_keep, d_z)
        d_z2 = across(d_keep, 2, group)
        i_core = along(after(gin, u_send, d_keep)[1], 1)
        i_sum = plus_here(gin, i_core)
        i_got = [along(i_sum[1], 2), along(i_sum[2], 4), along(i_sum[3], 6)]
        u_z, d_z2, done = lax.optimization_barrier((u_z, d_z2, i_sum))
        u_keep = plus(u_keep, u_z)
        u_z2 = across(u_keep, 2, group)
        d_keep = plus(d_keep, d_z2)
        d_other = across(d_keep, 1, group)
        i_own, *i_send = by_quarters(i_sum, *i_got)
        i_got = [across(part, offset, group) for offset, part in zip((1, 2, 3), i_send)]
        u_keep = plus(u_keep, u_z2)
        u_other = across(u_keep, 1, group)
        i_own = plus(i_own, *i_got)
        i_got = [across(i_own, offset, group) for offset in (1, 2, 3)]
        gdown = last_down(after(d_keep, i_own), d_other)
        g_up = last_up(after(u_keep, i_own), u_other)
        g_in, g_out, *vectors = last_in([i_own, *i_got], model, width, tall)
    else:
        du, gub, down = turn(dy, slopes, parts_d, plan_d)
        dresid, datt, sums2 = back(resids, du, dy, vecs, up, w_out)
        gup = rise(n2s, du, width, fast)
        pairs = [rear(row, qs[row], ks[row], vs[row], ps[row], datt) for row in range(rows)]
        mixeds, rear_sums = zip(*pairs)
        gin, dx, small = base(
            x, dresid, vecs, w_in, gub, sums2, mixeds, rear_sums, wides, atts, width, fast
        )
        out = finish(vecs, hidden, down, resids)

        def total(value, dim):
            own = lax.psum_scatter(value, "fsdp", scatter_dimension=dim, tiled=True)
            return lax.psum(own, "dp").astype(F32)

        gdown = total(gdown, 1).T
        g_up = total(gup, 0)
        gin = total(gin, 0)
        g_in, g_out = gin[:, : 3 * model], gin[:, 3 * model :]
        vectors = settle(lax.psum(small, ("dp", "fsdp")), width, tall)
    return (
        out.reshape(frames.shape),
        dx.reshape(frames.shape),
        vectors[0],
        vectors[1],
        g_in,
        vectors[2],
        vectors[3],
        g_out,
        vectors[6],
        vectors[4],
        vectors[5],
        g_up,
        vectors[8],
        gdown,
        vectors[7],
    )


def solution(mesh):
    rows = P(None, ("dp", "fsdp"), None, None)
    vector = P("fsdp")
    matrix = P("fsdp", None)
    weights = (vector, vector, matrix, vector, vector, matrix, vector, vector, vector, matrix, vector, matrix, vector)
    return jax.shard_map(
        functools.partial(shards, mesh.shape["dp"]),
        mesh=mesh,
        in_specs=(rows, rows, P(None, ("dp", "fsdp"), None)) + weights,
        out_specs=(rows, rows) + weights,
        check_vma=False,
    )
```

profile of v0, /device:TPU:0, one launch (start us, length us, event | category | flops | bytes accessed | tf_op | source)
XLA Modules:
  0.0 127.6 jit_solution(2228482761337548751)
XLA Ops:
  0.7 1.8 %pack.1.refs_0_ = bf16[272,512]{1,0:T(8,128)(2,1)} custom-call(bf16[64,1536]{1,0:T(8,128)(2,1)} %refs_0_.1, bf16[64,512]{1,0:T(8,128)(2,1)} %refs_1_.1, bf16[64]{0:T(256)(128)(2,1)} %refs_2_.1, bf16[64]{0:T(256)(128)(2,1)} %refs_3_.1, bf16[64]{0:T(256)(128)(2,1)} %refs_4_.1, bf16[64]{0:T(256)(128)(2,1)} %refs_5_.1, bf16[64]{0:T(256)(128)(2,1)} %refs_6_.1, ...), custom_call_target="tpu_custom_call" | custom-call | flops 200000000 | tf_op jit(solution)/shard_map/pack/pallas_call | solution.py:176
  3.0 3.5 %collective-permute-start.3 = (bf16[272,512]{1,0:T(8,128)(2,1)}, bf16[272,512]{1,0:T(8,128)(2,1)S(1)}, u32[]{:S(2)}, u32[]{:S(2)}) collective-permute-start(bf16[272,512]{1,0:T(8,128)(2,1)} %pack.1.refs_0_), channel_id=1, source_target_pairs={{0,6},{1,7},{2,4},{3,5},{4,2},{5,3},{6,0},{7,1},{8,14},{9,15},{10,... | collective-permute-start | bytes 835592 | tf_op jit(solution)/shard_map/ppermute | solution.py:611
  11.5 2.7 %collective-permute-done.3.refs_4_ = bf16[272,512]{1,0:T(8,128)(2,1)S(1)} collective-permute-done((bf16[272,512]{1,0:T(8,128)(2,1)}, bf16[272,512]{1,0:T(8,128)(2,1)S(1)}, u32[]{:S(2)}, u32[]{:S(2)}) %collective-permute-start.3) | collective-permute-done | bytes 278560 | tf_op jit(solution)/shard_map/ppermute | solution.py:611
  14.2 5.7 %collective-permute-done.2.refs_3_ = bf16[272,512]{1,0:T(8,128)(2,1)S(1)} collective-permute-done((bf16[272,512]{1,0:T(8,128)(2,1)}, bf16[272,512]{1,0:T(8,128)(2,1)S(1)}, u32[]{:S(2)}, u32[]{:S(2)}) %collective-permute-start.2) | collective-permute-done | bytes 278560 | tf_op jit(solution)/shard_map/ppermute | solution.py:611
  24.3 6.5 %front0.1 = (f32[16,512]{1,0:T(8,128)S(1)}, bf16[512,1536]{1,0:T(8,128)(2,1)S(1)}, bf16[512,512]{1,0:T(8,128)(2,1)S(1)}, bf16[384,512]{1,0:T(8,128)(2,1)S(1)}, b...) custom-call(bf16[2,384,512]{2,1,0:T(8,128)(2,1)S(1)} %bitcast.22, ...), custom_call_target="tpu_custom_call" | custom-call | flops 700000000 | tf_op jit(solution)/shard_map/front0/pallas_call | solution.py:309
  32.8 5.0 %front1.1 = (bf16[384,512]{1,0:T(8,128)(2,1)S(1)}, bf16[432,512]{1,0:T(8,128)(2,1)S(1)}, bf16[432,512]{1,0:T(8,128)(2,1)S(1)}, bf16[512,432]{1,0:T(8,128)(2,1)S(...) custom-call(bf16[2,384,512]{2,1,0:T(8,128)(2,1)S(1)} %bitcast.23, ...), custom_call_target="tpu_custom_call" | custom-call | flops 700000000 | tf_op jit(solution)/shard_map/front1/pallas_call | solution.py:309
  38.5 3.0 %collective-permute-done.8.refs_3_ = bf16[256,512]{1,0:T(8,128)(2,1)S(1)} collective-permute-done((bf16[256,512]{1,0:T(8,128)(2,1)S(1)}, bf16[256,512]{1,0:T(8,128)(2,1)S(1)}, u32[]{:S(2)}, u32[]{:S(2)}) %collective-permute-start.8) | collective-permute-done | bytes 262176 | tf_op jit(solution)/shard_map/ppermute | solution.py:611
  43.8 6.8 %middle.1 = (bf16[768,2048]{1,0:T(8,128)(2,1)S(1)}, bf16[768,2048]{1,0:T(8,128)(2,1)S(1)}, bf16[512,2048]{1,0:T(8,128)(2,1)S(1)}, bf16[2,4,512,256]{3,2,1,0:T(8,128)(2,1)S(1)}) custom-call(bf16[384,512]{1,0:T(8,128)(2,1)S(1)} %get-tuple-element.128.refs_0_, bf16[384,512]{1,0:T(8,128)(2,1)S(1)} %get-tuple-element.129.refs_1_, ...), custom_call_target="tpu_custom_call" | custom-call | flops 800000000 | tf_op jit(solution)/shard_map/middle/pallas_call | solution.py:176
  52.8 2.1 %turn.1 = (bf16[768,2048]{1,0:T(8,128)(2,1)S(1)}, f32[4,512]{1,0:T(4,128)S(1)}, bf16[2048,512]{1,0:T(8,128)(2,1)S(1)}) custom-call(bf16[768,512]{1,0:T(8,128)(2,1)S(1)} %bitcast.26, bf16[768,2048]{1,0:T(8,128)(2,1)S(1)} %get-tuple-element.140.slopes, bf16[256,512]{1,0:T(8,128)(2,1)S(1)} %copy-done.6, bf16[256,512]{1,0:T(8,128)(2,1)S(1)} %collective-permute-done.16.refs_1_, ...), custom_call_target="tpu_custom_call" | custom-call | flops 500000000 | tf_op jit(solution)/shard_map/turn/pallas_call | solution.py:176
  55.2 1.8 %rise.1.both = bf16[2,4,64,2048]{3,2,1,0:T(8,128)(2,1)S(1)} custom-call(bf16[384,512]{1,0:T(8,128)(2,1)S(1)} %get-tuple-element.128.refs_0_, bf16[384,512]{1,0:T(8,128)(2,1)S(1)} %get-tuple-element.129.refs_1_, bf16[768,2048]{1,0:T(8,128)(2,1)S(1)} %get-tuple-element.152.refs_2_), custom_call_target="tpu_custom_call" | custom-call | flops 400000000 | tf_op jit(solution)/shard_map/rise/pallas_call | solution.py:176
  60.1 2.9 %back.1 = (f32[768,512]{1,0:T(8,128)S(1)}, bf16[768,512]{1,0:T(8,128)(2,1)S(1)}, f32[4,512]{1,0:T(4,128)S(1)}) custom-call(f32[384,512]{1,0:T(8,128)S(1)} %get-tuple-element.150.refs_0_, f32[384,512]{1,0:T(8,128)S(1)} %get-tuple-element.151.refs_1_, bf16[768,2048]{1,0:T(8,128)(2,1)S(1)} %get-tuple-element.152.refs_2_, bf16[768,512]{1,0:T(8,128)(2,1)S(1)} %bitcast.27, ...), custom_call_target="tpu_custom_call" | custom-call | flops 800000000 | tf_op jit(solution)/shard_map/back/pallas_call | solution.py:176
  65.4 3.2 %rear0.1 = (bf16[432,1536]{1,0:T(8,128)(2,1)S(1)}, f32[2,512]{1,0:T(2,128)S(1)}) custom-call(bf16[384,512]{1,0:T(8,128)(2,1)S(1)} %get-tuple-element.157.q, bf16[432,512]{1,0:T(8,128)(2,1)S(1)} %get-tuple-element.158.k, bf16[432,512]{1,0:T(8,128)(2,1)S(1)} %get-tuple-element.159.v, bf16[3,4,192,256]{3,2,1,0:T(8,128)(2,1)S(1)} %get-tuple-element.160.p, ...), custom_call_target="tpu_custom_call" | custom-call | flops 700000000 | tf_op jit(solution)/shard_map/rear0/pallas_call | solution.py:176
  70.8 3.3 %rear1.1 = (bf16[432,1536]{1,0:T(8,128)(2,1)S(1)}, f32[2,512]{1,0:T(2,128)S(1)}) custom-call(bf16[384,512]{1,0:T(8,128)(2,1)S(1)} %get-tuple-element.166.q, bf16[432,512]{1,0:T(8,128)(2,1)S(1)} %get-tuple-element.167.k, bf16[432,512]{1,0:T(8,128)(2,1)S(1)} %get-tuple-element.168.v, bf16[3,4,192,256]{3,2,1,0:T(8,128)(2,1)S(1)} %get-tuple-element.169.p, ...), custom_call_target="tpu_custom_call" | custom-call | flops 700000000 | tf_op jit(solution)/shard_map/rear1/pallas_call | solution.py:176
  76.3 1.6 %collective-permute-start.31 = (bf16[256,256]{1,0:T(8,128)(2,1)S(1)}, bf16[256,256]{1,0:T(8,128)(2,1)S(1)}, u32[]{:S(2)}, u32[]{:S(2)}) collective-permute-start(bf16[256,256]{1,0:T(8,128)(2,1)S(1)} %get-tuple-element.182), channel_id=1, source_target_pairs={{0,8},{8,0},{16,24},{24,16},{1,9},{9,1},{17,25},{25,17},{2,10},{10... | collective-permute-start | bytes 393224 | tf_op jit(solution)/shard_map/ppermute | solution.py:615
  80.2 2.7 %finish.1 = bf16[768,512]{1,0:T(8,128)(2,1)} custom-call(f32[16,512]{1,0:T(8,128)S(1)} %get-tuple-element.171.vecs_in.refs_3_.refs_4_.vecs, bf16[768,2048]{1,0:T(8,128)(2,1)S(1)} %get-tuple-element.172.hidden, bf16[2048,512]{1,0:T(8,128)(2,1)S(1)} %get-tuple-element.173.down, f32[384,512]{1,0:T(8,128)S(1)} %get-tuple-element.150.refs_0_, ...), custom_call_target="tpu_custom_call" | custom-call | flops 400000000 | tf_op jit(solution)/shard_map/finish/pallas_call | solution.py:176
  82.9 5.8 %base.1 = (bf16[2,4,64,2176]{3,2,1,0:T(8,128)(2,1)S(1)}, f32[2,384,512]{2,1,0:T(8,128)}, f32[16,512]{1,0:T(8,128)}) custom-call(bf16[2,384,512]{2,1,0:T(8,128)(2,1)S(1)} %bitcast.24, f32[768,512]{1,0:T(8,128)S(1)} %get-tuple-element.183.dresid, f32[16,512]{1,0:T(8,128)S(1)} %get-tuple-element.171.vecs_in.refs_3_.refs_4_.vecs, ...), custom_call_target="tpu_custom_call" | custom-call | flops 600000000 | tf_op jit(solution)/shard_map/base/pallas_call | solution.py:176
  89.6 2.6 %collective-permute-start.43 = (bf16[256,256]{1,0:T(8,128)(2,1)S(1)}, bf16[256,256]{1,0:T(8,128)(2,1)S(1)}, u32[]{:S(2)}, u32[]{:S(2)}) collective-permute-start(bf16[256,256]{1,0:T(8,128)(2,1)S(1)} %plus.10.refs_0_), channel_id=1, source_target_pairs={{0,16},{8,24},{16,0},{24,8},{1,17},{9,25},{17,1},{25,9},{2,18},{10... | collective-permute-start | bytes 393224 | tf_op jit(solution)/shard_map/ppermute | solution.py:615
  96.1 1.7 %collective-permute-done.42.refs_1_ = bf16[32,2048]{1,0:T(8,128)(2,1)S(1)} collective-permute-done((bf16[32,2048]{1,0:T(8,128)(2,1)S(1)}, bf16[32,2048]{1,0:T(8,128)(2,1)S(1)}, u32[]{:S(2)}, u32[]{:S(2)}) %collective-permute-start.42) | collective-permute-done | bytes 131104 | tf_op jit(solution)/shard_map/ppermute | solution.py:615
  99.4 7.4 %collective-permute-done.44.refs_1_ = bf16[32,2048]{1,0:T(8,128)(2,1)S(1)} collective-permute-done((bf16[32,2048]{1,0:T(8,128)(2,1)S(1)}, bf16[32,2048]{1,0:T(8,128)(2,1)S(1)}, u32[]{:S(2)}, u32[]{:S(2)}) %collective-permute-start.44) | collective-permute-done | bytes 131104 | tf_op jit(solution)/shard_map/ppermute | solution.py:615
  108.2 1.6 %collective-permute-start.36 = (bf16[16,2176]{1,0:T(8,128)(2,1)S(1)}, bf16[16,2176]{1,0:T(8,128)(2,1)S(1)}, u32[]{:S(2)}, u32[]{:S(2)}) collective-permute-start(bf16[16,2176]{1,0:T(8,128)(2,1)S(1)} %get-tuple-element.200), channel_id=1, source_target_pairs={{0,8},{8,0},{16,24},{24,16},{1,9},{9,1},{17,25},{25,17},{2,10},{10... | collective-permute-start | bytes 208904 | tf_op jit(solution)/shard_map/ppermute | solution.py:615
  113.8 4.4 %collective-permute-done.37.refs_2_ = bf16[16,2176]{1,0:T(8,128)(2,1)S(1)} collective-permute-done((bf16[16,2176]{1,0:T(8,128)(2,1)S(1)}, bf16[16,2176]{1,0:T(8,128)(2,1)S(1)}, u32[]{:S(2)}, u32[]{:S(2)}) %collective-permute-start.37) | collective-permute-done | bytes 69664 | tf_op jit(solution)/shard_map/ppermute | solution.py:615
  118.3 2.3 %collective-permute-start.41 = (bf16[16,2176]{1,0:T(8,128)(2,1)S(1)}, bf16[16,2176]{1,0:T(8,128)(2,1)S(1)}, u32[]{:S(2)}, u32[]{:S(2)}) collective-permute-start(bf16[16,2176]{1,0:T(8,128)(2,1)S(1)} %plus.12.refs_0_), channel_id=1, source_target_pairs={{0,24},{8,16},{16,8},{24,0},{1,25},{9,17},{17,9},{25,1},{2,26},{10... | collective-permute-start | bytes 208904 | tf_op jit(solution)/shard_map/ppermute | solution.py:615
  121.1 1.6 %collective-permute-start.39 = (bf16[16,2176]{1,0:T(8,128)(2,1)S(1)}, bf16[16,2176]{1,0:T(8,128)(2,1)S(1)}, u32[]{:S(2)}, u32[]{:S(2)}) collective-permute-start(bf16[16,2176]{1,0:T(8,128)(2,1)S(1)} %plus.12.refs_0_), channel_id=1, source_target_pairs={{0,8},{8,0},{16,24},{24,16},{1,9},{9,1},{17,25},{25,17},{2,10},{10... | collective-permute-start | bytes 208904 | tf_op jit(solution)/shard_map/ppermute | solution.py:615
  125.2 1.6 %collective-permute-done.40.refs_2_ = bf16[16,2176]{1,0:T(8,128)(2,1)S(1)} collective-permute-done((bf16[16,2176]{1,0:T(8,128)(2,1)S(1)}, bf16[16,2176]{1,0:T(8,128)(2,1)S(1)}, u32[]{:S(2)}, u32[]{:S(2)}) %collective-permute-start.40) | collective-permute-done | bytes 69664 | tf_op jit(solution)/shard_map/ppermute | solution.py:615
  (120 shorter events, 45.0 us)
Async XLA Ops:
  3.0 11.3 %collective-permute-start.3 = (bf16[272,512]{1,0:T(8,128)(2,1)}, bf16[272,512]{1,0:T(8,128)(2,1)S(1)}, u32[]{:S(2)}, u32[]{:S(2)}) collective-permute-start(bf16[272,512]{1,0:T(8,128)(2,1)} %pack.1.refs_0_), channel_id=1, source_target_pairs={{0,6},{1,7},{2,4},{3,5},{4,2},{5,3},{6,0},{7,1},{8,14},{9,15},{10,... | collective-permute-start | bytes 835592 | tf_op jit(solution)/shard_map/ppermute | solution.py:611
  6.5 13.4 %collective-permute-start.2 = (bf16[272,512]{1,0:T(8,128)(2,1)}, bf16[272,512]{1,0:T(8,128)(2,1)S(1)}, u32[]{:S(2)}, u32[]{:S(2)}) collective-permute-start(bf16[272,512]{1,0:T(8,128)(2,1)} %pack.1.refs_0_), channel_id=1, source_target_pairs={{0,4},{1,5},{2,6},{3,7},{4,0},{5,1},{6,2},{7,3},{8,12},{9,13},{10,... | collective-permute-start | bytes 835592 | tf_op jit(solution)/shard_map/ppermute | solution.py:611
  7.0 13.2 %collective-permute-start.1 = (bf16[272,512]{1,0:T(8,128)(2,1)}, bf16[272,512]{1,0:T(8,128)(2,1)S(1)}, u32[]{:S(2)}, u32[]{:S(2)}) collective-permute-start(bf16[272,512]{1,0:T(8,128)(2,1)} %pack.1.refs_0_), channel_id=1, source_target_pairs={{0,2},{1,3},{2,0},{3,1},{4,6},{5,7},{6,4},{7,5},{8,10},{9,11},{10,... | collective-permute-start | bytes 835592 | tf_op jit(solution)/shard_map/ppermute | solution.py:611
  20.7 17.1 %collective-permute-start.12 = (bf16[64,2048]{1,0:T(8,128)(2,1)S(1)}, bf16[64,2048]{1,0:T(8,128)(2,1)S(1)}, u32[]{:S(2)}, u32[]{:S(2)}) collective-permute-start(bf16[64,2048]{1,0:T(8,128)(2,1)S(1)} %copy-done.5), channel_id=1, source_target_pairs={{0,6},{1,7},{2,4},{3,5},{4,2},{5,3},{6,0},{7,1},{8,14},{9,15},{10,... | collective-permute-start | bytes 786440 | tf_op jit(solution)/shard_map/ppermute | solution.py:611
  22.2 15.7 %collective-permute-start.11 = (bf16[64,2048]{1,0:T(8,128)(2,1)S(1)}, bf16[64,2048]{1,0:T(8,128)(2,1)S(1)}, u32[]{:S(2)}, u32[]{:S(2)}) collective-permute-start(bf16[64,2048]{1,0:T(8,128)(2,1)S(1)} %copy-done.5), channel_id=1, source_target_pairs={{0,4},{1,5},{2,6},{3,7},{4,0},{5,1},{6,2},{7,3},{8,12},{9,13},{10,... | collective-permute-start | bytes 786440 | tf_op jit(solution)/shard_map/ppermute | solution.py:611
  23.7 14.2 %collective-permute-start.10 = (bf16[64,2048]{1,0:T(8,128)(2,1)S(1)}, bf16[64,2048]{1,0:T(8,128)(2,1)S(1)}, u32[]{:S(2)}, u32[]{:S(2)}) collective-permute-start(bf16[64,2048]{1,0:T(8,128)(2,1)S(1)} %copy-done.5), channel_id=1, source_target_pairs={{0,2},{1,3},{2,0},{3,1},{4,6},{5,7},{6,4},{7,5},{8,10},{9,11},{10,... | collective-permute-start | bytes 786440 | tf_op jit(solution)/shard_map/ppermute | solution.py:611
  30.8 10.8 %collective-permute-start.8 = (bf16[256,512]{1,0:T(8,128)(2,1)S(1)}, bf16[256,512]{1,0:T(8,128)(2,1)S(1)}, u32[]{:S(2)}, u32[]{:S(2)}) collective-permute-start(bf16[256,512]{1,0:T(8,128)(2,1)S(1)} %copy-done.6), channel_id=1, source_target_pairs={{0,4},{1,5},{2,6},{3,7},{4,0},{5,1},{6,2},{7,3},{8,12},{9,13},{10,... | collective-permute-start | bytes 786440 | tf_op jit(solution)/shard_map/ppermute | solution.py:611
  32.3 9.4 %collective-permute-start.7 = (bf16[256,512]{1,0:T(8,128)(2,1)S(1)}, bf16[256,512]{1,0:T(8,128)(2,1)S(1)}, u32[]{:S(2)}, u32[]{:S(2)}) collective-permute-start(bf16[256,512]{1,0:T(8,128)(2,1)S(1)} %copy-done.6), channel_id=1, source_target_pairs={{0,2},{1,3},{2,0},{3,1},{4,6},{5,7},{6,4},{7,5},{8,10},{9,11},{10,... | collective-permute-start | bytes 786440 | tf_op jit(solution)/shard_map/ppermute | solution.py:611
  41.6 9.6 %collective-permute-start.17 = (bf16[256,512]{1,0:T(8,128)(2,1)S(1)}, bf16[256,512]{1,0:T(8,128)(2,1)S(1)}, u32[]{:S(2)}, u32[]{:S(2)}) collective-permute-start(bf16[256,512]{1,0:T(8,128)(2,1)S(1)} %copy-done.6), channel_id=1, source_target_pairs={{0,6},{1,7},{2,4},{3,5},{4,2},{5,3},{6,0},{7,1},{8,14},{9,15},{10,... | collective-permute-start | bytes 786440 | tf_op jit(solution)/shard_map/ppermute | solution.py:611
  58.0 10.6 %collective-permute-start.23 = (bf16[2,256,256]{2,1,0:T(8,128)(2,1)S(1)}, bf16[2,256,256]{2,1,0:T(8,128)(2,1)S(1)}, u32[]{:S(2)}, u32[]{:S(2)}) collective-permute-start(bf16[2,256,256]{2,1,0:T(8,128)(2,1)S(1)} %get-tuple-element.148), channel_id=1, source_target_pairs={{0,4},{1,5},{2,6},{3,7},{4,0},{5,1},{6,2},{7,3},{8,12},{9,13},{10,... | collective-permute-start | bytes 786440 | tf_op jit(solution)/shard_map/ppermute | solution.py:611
  59.5 9.2 %collective-permute-start.22 = (bf16[2,256,256]{2,1,0:T(8,128)(2,1)S(1)}, bf16[2,256,256]{2,1,0:T(8,128)(2,1)S(1)}, u32[]{:S(2)}, u32[]{:S(2)}) collective-permute-start(bf16[2,256,256]{2,1,0:T(8,128)(2,1)S(1)} %get-tuple-element.147), channel_id=1, source_target_pairs={{0,2},{1,3},{2,0},{3,1},{4,6},{5,7},{6,4},{7,5},{8,10},{9,11},{10,... | collective-permute-start | bytes 786440 | tf_op jit(solution)/shard_map/ppermute | solution.py:611
  63.3 10.8 %collective-permute-start.26 = (bf16[2,32,2048]{2,1,0:T(8,128)(2,1)S(1)}, bf16[2,32,2048]{2,1,0:T(8,128)(2,1)S(1)}, u32[]{:S(2)}, u32[]{:S(2)}) collective-permute-start(bf16[2,32,2048]{2,1,0:T(8,128)(2,1)S(1)} %get-tuple-element.175), channel_id=1, source_target_pairs={{0,4},{1,5},{2,6},{3,7},{4,0},{5,1},{6,2},{7,3},{8,12},{9,13},{10,... | collective-permute-start | bytes 786440 | tf_op jit(solution)/shard_map/ppermute | solution.py:611
  64.8 9.2 %collective-permute-start.25 = (bf16[2,32,2048]{2,1,0:T(8,128)(2,1)S(1)}, bf16[2,32,2048]{2,1,0:T(8,128)(2,1)S(1)}, u32[]{:S(2)}, u32[]{:S(2)}) collective-permute-start(bf16[2,32,2048]{2,1,0:T(8,128)(2,1)S(1)} %get-tuple-element.156), channel_id=1, source_target_pairs={{0,2},{1,3},{2,0},{3,1},{4,6},{5,7},{6,4},{7,5},{8,10},{9,11},{10,... | collective-permute-start | bytes 786440 | tf_op jit(solution)/shard_map/ppermute | solution.py:611
  76.3 12.4 %collective-permute-start.31 = (bf16[256,256]{1,0:T(8,128)(2,1)S(1)}, bf16[256,256]{1,0:T(8,128)(2,1)S(1)}, u32[]{:S(2)}, u32[]{:S(2)}) collective-permute-start(bf16[256,256]{1,0:T(8,128)(2,1)S(1)} %get-tuple-element.182), channel_id=1, source_target_pairs={{0,8},{8,0},{16,24},{24,16},{1,9},{9,1},{17,25},{25,17},{2,10},{10... | collective-permute-start | bytes 393224 | tf_op jit(solution)/shard_map/ppermute | solution.py:615
  78.0 10.7 %collective-permute-start.30 = (bf16[32,2048]{1,0:T(8,128)(2,1)S(1)}, bf16[32,2048]{1,0:T(8,128)(2,1)S(1)}, u32[]{:S(2)}, u32[]{:S(2)}) collective-permute-start(bf16[32,2048]{1,0:T(8,128)(2,1)S(1)} %get-tuple-element.192), channel_id=1, source_target_pairs={{0,4},{1,5},{2,6},{3,7},{4,0},{5,1},{6,2},{7,3},{8,12},{9,13},{10,... | collective-permute-start | bytes 393224 | tf_op jit(solution)/shard_map/ppermute | solution.py:611
  78.7 10.0 %collective-permute-start.29 = (bf16[32,2048]{1,0:T(8,128)(2,1)S(1)}, bf16[32,2048]{1,0:T(8,128)(2,1)S(1)}, u32[]{:S(2)}, u32[]{:S(2)}) collective-permute-start(bf16[32,2048]{1,0:T(8,128)(2,1)S(1)} %get-tuple-element.179), channel_id=1, source_target_pairs={{0,2},{1,3},{2,0},{3,1},{4,6},{5,7},{6,4},{7,5},{8,10},{9,11},{10,... | collective-permute-start | bytes 393224 | tf_op jit(solution)/shard_map/ppermute | solution.py:611
  89.1 8.7 %collective-permute-start.42 = (bf16[32,2048]{1,0:T(8,128)(2,1)S(1)}, bf16[32,2048]{1,0:T(8,128)(2,1)S(1)}, u32[]{:S(2)}, u32[]{:S(2)}) collective-permute-start(bf16[32,2048]{1,0:T(8,128)(2,1)S(1)} %get-tuple-element.195), channel_id=1, source_target_pairs={{0,8},{8,0},{16,24},{24,16},{1,9},{9,1},{17,25},{25,17},{2,10},{10... | collective-permute-start | bytes 393224 | tf_op jit(solution)/shard_map/ppermute | solution.py:615
  92.5 14.3 %collective-permute-start.35 = (bf16[64,2176]{1,0:T(8,128)(2,1)S(1)}, bf16[64,2176]{1,0:T(8,128)(2,1)S(1)}, u32[]{:S(2)}, u32[]{:S(2)}) collective-permute-start(bf16[64,2176]{1,0:T(8,128)(2,1)S(1)} %get-tuple-element.234), channel_id=1, source_target_pairs={{0,6},{1,7},{2,4},{3,5},{4,2},{5,3},{6,0},{7,1},{8,14},{9,15},{10,... | collective-permute-start | bytes 835592 | tf_op jit(solution)/shard_map/ppermute | solution.py:611
  94.0 13.9 %collective-permute-start.34 = (bf16[64,2176]{1,0:T(8,128)(2,1)S(1)}, bf16[64,2176]{1,0:T(8,128)(2,1)S(1)}, u32[]{:S(2)}, u32[]{:S(2)}) collective-permute-start(bf16[64,2176]{1,0:T(8,128)(2,1)S(1)} %get-tuple-element.235), channel_id=1, source_target_pairs={{0,4},{1,5},{2,6},{3,7},{4,0},{5,1},{6,2},{7,3},{8,12},{9,13},{10,... | collective-permute-start | bytes 835592 | tf_op jit(solution)/shard_map/ppermute | solution.py:611
  94.6 13.3 %collective-permute-start.33 = (bf16[64,2176]{1,0:T(8,128)(2,1)S(1)}, bf16[64,2176]{1,0:T(8,128)(2,1)S(1)}, u32[]{:S(2)}, u32[]{:S(2)}) collective-permute-start(bf16[64,2176]{1,0:T(8,128)(2,1)S(1)} %get-tuple-element.236), channel_id=1, source_target_pairs={{0,2},{1,3},{2,0},{3,1},{4,6},{5,7},{6,4},{7,5},{8,10},{9,11},{10,... | collective-permute-start | bytes 835592 | tf_op jit(solution)/shard_map/ppermute | solution.py:611
  97.8 8.9 %collective-permute-start.44 = (bf16[32,2048]{1,0:T(8,128)(2,1)S(1)}, bf16[32,2048]{1,0:T(8,128)(2,1)S(1)}, u32[]{:S(2)}, u32[]{:S(2)}) collective-permute-start(bf16[32,2048]{1,0:T(8,128)(2,1)S(1)} %plus.13.refs_0_), channel_id=1, source_target_pairs={{0,16},{8,24},{16,0},{24,8},{1,17},{9,25},{17,1},{25,9},{2,18},{10... | collective-permute-start | bytes 393224 | tf_op jit(solution)/shard_map/ppermute | solution.py:615
  106.7 16.0 %collective-permute-start.45 = (bf16[32,2048]{1,0:T(8,128)(2,1)S(1)}, bf16[32,2048]{1,0:T(8,128)(2,1)S(1)}, u32[]{:S(2)}, u32[]{:S(2)}) collective-permute-start(bf16[32,2048]{1,0:T(8,128)(2,1)S(1)} %plus.14.keep), channel_id=1, source_target_pairs={{0,8},{8,0},{16,24},{24,16},{1,9},{9,1},{17,25},{25,17},{2,10},{10... | collective-permute-start | bytes 393224 | tf_op jit(solution)/shard_map/ppermute | solution.py:615
  109.8 8.5 %collective-permute-start.37 = (bf16[16,2176]{1,0:T(8,128)(2,1)S(1)}, bf16[16,2176]{1,0:T(8,128)(2,1)S(1)}, u32[]{:S(2)}, u32[]{:S(2)}) collective-permute-start(bf16[16,2176]{1,0:T(8,128)(2,1)S(1)} %get-tuple-element.201), channel_id=1, source_target_pairs={{0,16},{8,24},{16,0},{24,8},{1,17},{9,25},{17,1},{25,9},{2,18},{10... | collective-permute-start | bytes 208904 | tf_op jit(solution)/shard_map/ppermute | solution.py:615
  112.7 10.9 %collective-permute-start.46 = (bf16[256,256]{1,0:T(8,128)(2,1)S(1)}, bf16[256,256]{1,0:T(8,128)(2,1)S(1)}, u32[]{:S(2)}, u32[]{:S(2)}) collective-permute-start(bf16[256,256]{1,0:T(8,128)(2,1)S(1)} %plus.15.keep), channel_id=1, source_target_pairs={{0,8},{8,0},{16,24},{24,16},{1,9},{9,1},{17,25},{25,17},{2,10},{10... | collective-permute-start | bytes 393224 | tf_op jit(solution)/shard_map/ppermute | solution.py:615
  (31 other events, 194.9 us)
where the time goes:
time: 128 us
  Pallas kernels  47.8 us (37%)
  starting transfers between devices  42.4 us (33%)
  waiting for transfers between devices  33.2 us (26%)
  local copies, waits for them, and re-layouts  3.26 us (3%)
    pallas_call x27, Pallas kernels, call(): pl.pallas_call(body, in_specs=[VMEM] * ins + [HBM] * (len(args) - ins), o...  34.9 us
    ppermute x35, starting transfers between devices, along(): return lax.ppermute(value, 'fsdp', [(i, i ^ offset) for i in range(8)])  26.4 us
    ppermute x35, waiting for transfers between devices, along(): return lax.ppermute(value, 'fsdp', [(i, i ^ offset) for i in range(8)])  17.1 us
    ppermute x12, waiting for transfers between devices, across(): return lax.ppermute(value, 'dp', [(i, i ^ offset) for i in range(size)])  16.2 us
    ppermute x12, starting transfers between devices, across(): return lax.ppermute(value, 'dp', [(i, i ^ offset) for i in range(size)])  16 us
    pallas_call x2, Pallas kernels, front(): pl.pallas_call(body, in_specs=specs, out_specs=[VMEM] * len(outs), out_sh...  11.4 us
    unnamed x16, local copies, waits for them, and re-layouts  2.97 us
  transfers between devices with their start and end apart: 47, of which 16 were waited for; matrix products, arithmetic and copies ran while one was open for 0% of the time, Pallas kernels for 33%

commit v1 on v0

--- a/solution.py
+++ b/solution.py
@@ -51,23 +51,12 @@
     return first, slot
 
 
-def start_copies(copies):
-    for copy in copies:
-        copy.start()
-
-
-def wait_copies(copies):
-    for copy in copies:
-        copy.wait()
-
-
 def full(shape, dtype):
     return jax.ShapeDtypeStruct(shape, dtype)
 
 
-def assemble(plan, parts, segments, sem):
+def assemble(plan, parts, segments):
     me = lax.axis_index("fsdp")
-    copies = []
     for number, (offset, relative, first, rows, count) in enumerate(plan):
         for each in range(count):
             device = jnp.bitwise_xor(me, offset) if relative else each
@@ -75,14 +64,9 @@
                 low, high = max(first, start), min(first + rows, start + height)
                 if low < high:
                     place = pl.multiple_of(device * height, height) + low - start
-                    source = parts[number].at[pl.ds(each * rows + low - first, high - low), :]
-                    wide = source.shape[1]
-                    copies.append(
-                        pltpu.make_async_copy(
-                            source, target.at[pl.ds(place, high - low), pl.ds(column, wide)], sem
-                        )
-                    )
-    return copies
+                    at = each * rows + low - first
+                    value = parts[number][at : at + high - low, :]
+                    target[pl.ds(place, high - low), column : column + value.shape[1]] = value
 
 
 def pieces_into(grads):
@@ -243,14 +227,10 @@
     length, model = x.shape[1], x.shape[2]
     value = x[row].astype(F32)
     if first_call:
-        small, sem = outs
+        (small,) = outs
         segments = [(band * width, width, w_in, band * model) for band in range(3)]
         segments += [(3 * width, width, w_out, 0), (4 * width, EXTRA, small, 0)]
-        copies = assemble(plan, parts, segments, sem)
-        start_copies(copies)
-    unit = units[row]
-    if first_call:
-        wait_copies(copies)
+        assemble(plan, parts, segments)
         total = jnp.zeros((8, model), F32)
         ups = [jnp.zeros((1, model), F32) for _ in range(4)]
         for piece in range(model // width):
@@ -263,7 +243,7 @@
         for part in range(4):
             vecs[8 + part : 9 + part] = ups[part]
         vecs[12:16] = jnp.zeros((4, model), F32)
-    normed = (unit * vecs[0:1] + vecs[1:2]).astype(BF)
+    normed = (units[row] * vecs[0:1] + vecs[1:2]).astype(BF)
     summary = nn(averages(length), normed).astype(BF)
     wide = jnp.concatenate([normed, summary], axis=0)
     wide_out[...] = wide.T
@@ -296,9 +276,9 @@
     if first_call:
         outs = [full((16, model), F32), full((model, 3 * model), BF), full((model, model), BF)] + outs
         pieces = model // width
-        scratch += [pltpu.VMEM((pieces * EXTRA, model), BF), pltpu.SemaphoreType.DMA]
+        scratch += [pltpu.VMEM((pieces * EXTRA, model), BF)]
         args = [x, units, biases] + list(parts)
-        specs = [VMEM] * 3 + [HBM] * len(parts)
+        specs = [VMEM] * len(args)
 
         def body(x, units, biases, *refs):
             front_body(row, True, plan, width, x, units, biases, None, None, None, *refs)
@@ -331,14 +311,12 @@
     n2s = refs[:rows]
     dyt, vecs, *refs = refs[rows:]
     parts = refs[: len(plan)]
-    hidden, slopes, up, grads, sem = refs[len(plan) :]
+    hidden, slopes, up, grads = refs[len(plan) :]
     put = pieces_into(grads)
     model, tokens = dyt.shape
     ff = up.shape[1]
     tall = ff * width // model
-    copies = assemble(plan, parts, [(0, width, up, 0)], sem)
-    start_copies(copies)
-    wait_copies(copies)
+    assemble(plan, parts, [(0, width, up, 0)])
     length = n2s[0].shape[0]
     step = length
     for tile in range(ff // TILE):
@@ -369,21 +347,19 @@
         (full((model, ff), BF), False),
         (full(shape, BF), False),
     ]
-    scratch = [pltpu.SemaphoreType.DMA]
     body = functools.partial(middle_body, len(n2s), plan, width)
-    return call(body, "middle", 8, len(n2s) + 2, outs, scratch, [*n2s, dyt, vecs, *parts])
+    args = [*n2s, dyt, vecs, *parts]
+    return call(body, "middle", 8, len(args), outs, [], args)
 
 
 def turn_body(plan, dy, slopes, *refs):
     parts = refs[: len(plan)]
-    du, ub, down, sem = refs[len(plan) :]
+    du, ub, down = refs[len(plan) :]
     tokens, model = dy.shape
     ff = down.shape[0]
     tall = plan[0][3]
     length = dy.shape[0] // 2
-    copies = assemble(plan, parts, [(0, tall, down, 0)], sem)
-    start_copies(copies)
-    wait_copies(copies)
+    assemble(plan, parts, [(0, tall, down, 0)])
     step = length
     for tile in range(ff // TILE):
         cols = slice(tile * TILE, (tile + 1) * TILE)
@@ -405,7 +381,7 @@
         (full((ff, model), BF), False),
     ]
     args = [dy, slopes, *parts]
-    return call(functools.partial(turn_body, plan), "turn", 5, 2, outs, [pltpu.SemaphoreType.DMA], args)
+    return call(functools.partial(turn_body, plan), "turn", 5, len(args), outs, [], args)
 
 
 def rise_body(rows, width, *refs):
@@ -621,9 +597,11 @@
     width, model = w_out.shape
     targets = [w_in, w_out, *rows]
     copies = [pltpu.make_async_copy(a, b, sem) for a, b in zip(sources, targets)]
-    start_copies(copies)
+    for copy in copies:
+        copy.start()
     out[4 * width :] = jnp.zeros((EXTRA, model), BF)
-    wait_copies(copies)
+    for copy in copies:
+        copy.wait()
     for band in range(3):
         out[band * width : (band + 1) * width] = w_in[:, band * model : (band + 1) * model]
     out[3 * width : 4 * width] = w_out[...]
@@ -889,7 +867,7 @@
         u2, u4, u1 = along(up_piece, 2), along(up_piece, 4), along(up_piece, 1)
         parts_a = [packed, a1, a2, a4, a6, along(a2, 1), along(a4, 1)] + [along(a6, 1)]
         u6 = along(up_piece, 6)
-        first = x
+        first = after(x, u1)
     else:
         plan_a, plan_u, plan_d = whole_plan(packed.shape[0], size), whole_plan(width, size), whole_plan(tall, size)
         parts_a = [lax.all_gather(packed, "fsdp", axis=0, tiled=True)]
@@ -942,10 +920,9 @@
         d_keep, d_send = hop_halves(d_sum, d_x, d_y, d_x2, d_y2)
         d_z = across(d_send, 1, group)
         mixeds = (mixed0, mixed1)
-        out = finish(after(vecs, sums1), hidden, down, resids)
         gin, dx, small = base(
             x,
-            after(dresid, to_x, d_send, out),
+            after(dresid, to_x, d_send),
             vecs,
             w_in,
             gub,
@@ -965,17 +942,19 @@
         i_core = along(after(gin, u_send, d_keep)[1], 1)
         i_sum = plus_here(gin, i_core)
         i_got = [along(i_sum[1], 2), along(i_sum[2], 4), along(i_sum[3], 6)]
+        out = finish(after(vecs, i_sum), hidden, down, resids)
+        *i_got, done = lax.optimization_barrier((*i_got, out))
         u_z, d_z2, done = lax.optimization_barrier((u_z, d_z2, i_sum))
         u_keep = plus(u_keep, u_z)
         u_z2 = across(u_keep, 2, group)
         d_keep = plus(d_keep, d_z2)
         d_other = across(d_keep, 1, group)
         i_own, *i_send = by_quarters(i_sum, *i_got)
-        i_got = [across(part, offset, group) for offset, part in zip((1, 2, 3), i_send)]
+        i_got = [across(i_send[offset - 1], offset, group) for offset in (3, 2, 1)]
         u_keep = plus(u_keep, u_z2)
         u_other = across(u_keep, 1, group)
         i_own = plus(i_own, *i_got)
-        i_got = [across(i_own, offset, group) for offset in (1, 2, 3)]
+        i_got = [across(i_own, offset, group) for offset in (3, 2, 1)][::-1]
         gdown = last_down(after(d_keep, i_own), d_other)
         g_up = last_up(after(u_keep, i_own), u_other)
         g_in, g_out, *vectors = last_in([i_own, *i_got], model, width, tall)

time: 128 us -> 125 us (0.977)
  waiting for transfers between devices: 33.2 us -> 31 us
  Pallas kernels: 47.8 us -> 46.5 us
    ppermute x12, waiting for transfers between devices: 16.2 us -> 13.8 us  [across(): return lax.ppermute(value, 'dp', [(i, i ^ offset) for i in range(size)])]
    pallas_call x2, Pallas kernels: 11.4 us -> 10.1 us  [front(): pl.pallas_call(body, in_specs=specs, out_specs=[VMEM] * len(outs), out_sh...]
  transfers between devices with their start and end apart: 47 -> 47, of which waited for: 16 -> 17; matrix products, arithmetic and copies ran while one was open for 0% -> 0% of each run, Pallas kernels for 33% -> 33%
where the time goes in v1:
time: 125 us
  Pallas kernels  46.5 us (37%)
  starting transfers between devices  42.8 us (34%)
  waiting for transfers between devices  31 us (25%)
  local copies, waits for them, and re-layouts  3.25 us (3%)
    pallas_call x27, Pallas kernels, call(): pl.pallas_call(body, in_specs=[VMEM] * ins + [HBM] * (len(args) - ins), o...  34.9 us
    ppermute x35, starting transfers between devices, along(): return lax.ppermute(value, 'fsdp', [(i, i ^ offset) for i in range(8)])  26.9 us
    ppermute x35, waiting for transfers between devices, along(): return lax.ppermute(value, 'fsdp', [(i, i ^ offset) for i in range(8)])  17.2 us
    ppermute x12, starting transfers between devices, across(): return lax.ppermute(value, 'dp', [(i, i ^ offset) for i in range(size)])  16 us
    ppermute x12, waiting for transfers between devices, across(): return lax.ppermute(value, 'dp', [(i, i ^ offset) for i in range(size)])  13.8 us
    pallas_call x2, Pallas kernels, front(): pl.pallas_call(body, in_specs=specs, out_specs=[VMEM] * len(outs), out_sh...  10.1 us
    unnamed x16, local copies, waits for them, and re-layouts  2.97 us
  transfers between devices with their start and end apart: 47, of which 17 were waited for; matrix products, arithmetic and copies ran while one was open for 0% of the time, Pallas kernels for 33%

profile of v1, /device:TPU:0, one launch (start us, length us, event | category | flops | bytes accessed | tf_op | source)
XLA Modules:
  0.0 124.5 jit_solution(17328252064334374691)
XLA Ops:
  0.7 1.8 %pack.1.refs_0_ = bf16[272,512]{1,0:T(8,128)(2,1)} custom-call(bf16[64,1536]{1,0:T(8,128)(2,1)} %refs_0_.1, bf16[64,512]{1,0:T(8,128)(2,1)} %refs_1_.1, bf16[64]{0:T(256)(128)(2,1)} %refs_2_.1, bf16[64]{0:T(256)(128)(2,1)} %refs_3_.1, bf16[64]{0:T(256)(128)(2,1)} %refs_4_.1, bf16[64]{0:T(256)(128)(2,1)} %refs_5_.1, bf16[64]{0:T(256)(128)(2,1)} %refs_6_.1, ...), custom_call_target="tpu_custom_call" | custom-call | flops 200000000 | tf_op jit(solution)/shard_map/pack/pallas_call | solution.py:160
  3.0 3.5 %collective-permute-start.2 = (bf16[272,512]{1,0:T(8,128)(2,1)}, bf16[272,512]{1,0:T(8,128)(2,1)S(1)}, u32[]{:S(2)}, u32[]{:S(2)}) collective-permute-start(bf16[272,512]{1,0:T(8,128)(2,1)} %pack.1.refs_0_), channel_id=1, source_target_pairs={{0,6},{1,7},{2,4},{3,5},{4,2},{5,3},{6,0},{7,1},{8,14},{9,15},{10,... | collective-permute-start | bytes 835592 | tf_op jit(solution)/shard_map/ppermute | solution.py:587
  11.5 2.7 %collective-permute-done.2.refs_4_ = bf16[272,512]{1,0:T(8,128)(2,1)S(1)} collective-permute-done((bf16[272,512]{1,0:T(8,128)(2,1)}, bf16[272,512]{1,0:T(8,128)(2,1)S(1)}, u32[]{:S(2)}, u32[]{:S(2)}) %collective-permute-start.2) | collective-permute-done | bytes 278560 | tf_op jit(solution)/shard_map/ppermute | solution.py:587
  14.2 5.7 %collective-permute-done.1.refs_3_ = bf16[272,512]{1,0:T(8,128)(2,1)S(1)} collective-permute-done((bf16[272,512]{1,0:T(8,128)(2,1)}, bf16[272,512]{1,0:T(8,128)(2,1)S(1)}, u32[]{:S(2)}, u32[]{:S(2)}) %collective-permute-start.1) | collective-permute-done | bytes 278560 | tf_op jit(solution)/shard_map/ppermute | solution.py:587
  25.0 5.2 %front0.1 = (f32[16,512]{1,0:T(8,128)S(1)}, bf16[512,1536]{1,0:T(8,128)(2,1)S(1)}, bf16[512,512]{1,0:T(8,128)(2,1)S(1)}, bf16[384,512]{1,0:T(8,128)(2,1)S(1)}, b...) custom-call(bf16[2,384,512]{2,1,0:T(8,128)(2,1)S(1)} %bitcast.22, ...), custom_call_target="tpu_custom_call" | custom-call | flops 700000000 | tf_op jit(solution)/shard_map/front0/pallas_call | solution.py:289
  32.3 4.9 %front1.1 = (bf16[384,512]{1,0:T(8,128)(2,1)S(1)}, bf16[432,512]{1,0:T(8,128)(2,1)S(1)}, bf16[432,512]{1,0:T(8,128)(2,1)S(1)}, bf16[512,432]{1,0:T(8,128)(2,1)S(...) custom-call(bf16[2,384,512]{2,1,0:T(8,128)(2,1)S(1)} %bitcast.23, ...), custom_call_target="tpu_custom_call" | custom-call | flops 700000000 | tf_op jit(solution)/shard_map/front1/pallas_call | solution.py:289
  37.9 3.7 %collective-permute-done.9.refs_3_ = bf16[256,512]{1,0:T(8,128)(2,1)S(1)} collective-permute-done((bf16[256,512]{1,0:T(8,128)(2,1)S(1)}, bf16[256,512]{1,0:T(8,128)(2,1)S(1)}, u32[]{:S(2)}, u32[]{:S(2)}) %collective-permute-start.9) | collective-permute-done | bytes 262176 | tf_op jit(solution)/shard_map/ppermute | solution.py:587
  43.7 6.8 %middle.1 = (bf16[768,2048]{1,0:T(8,128)(2,1)S(1)}, bf16[768,2048]{1,0:T(8,128)(2,1)S(1)}, bf16[512,2048]{1,0:T(8,128)(2,1)S(1)}, bf16[2,4,512,256]{3,2,1,0:T(8,128)(2,1)S(1)}) custom-call(bf16[384,512]{1,0:T(8,128)(2,1)S(1)} %get-tuple-element.135.refs_0_, bf16[384,512]{1,0:T(8,128)(2,1)S(1)} %get-tuple-element.136.refs_1_, ...), custom_call_target="tpu_custom_call" | custom-call | flops 800000000 | tf_op jit(solution)/shard_map/middle/pallas_call | solution.py:160
  52.3 2.1 %turn.1 = (bf16[768,2048]{1,0:T(8,128)(2,1)S(1)}, f32[4,512]{1,0:T(4,128)S(1)}, bf16[2048,512]{1,0:T(8,128)(2,1)S(1)}) custom-call(bf16[768,512]{1,0:T(8,128)(2,1)S(1)} %bitcast.26, bf16[768,2048]{1,0:T(8,128)(2,1)S(1)} %get-tuple-element.145.slopes, bf16[256,512]{1,0:T(8,128)(2,1)S(1)} %copy-done.6, bf16[256,512]{1,0:T(8,128)(2,1)S(1)} %collective-permute-done.16.refs_1_, ...), custom_call_target="tpu_custom_call" | custom-call | flops 500000000 | tf_op jit(solution)/shard_map/turn/pallas_call | solution.py:160
  54.8 1.8 %rise.1.both = bf16[2,4,64,2048]{3,2,1,0:T(8,128)(2,1)S(1)} custom-call(bf16[384,512]{1,0:T(8,128)(2,1)S(1)} %get-tuple-element.135.refs_0_, bf16[384,512]{1,0:T(8,128)(2,1)S(1)} %get-tuple-element.136.refs_1_, bf16[768,2048]{1,0:T(8,128)(2,1)S(1)} %get-tuple-element.154.refs_2_), custom_call_target="tpu_custom_call" | custom-call | flops 400000000 | tf_op jit(solution)/shard_map/rise/pallas_call | solution.py:160
  59.6 2.9 %back.1 = (f32[768,512]{1,0:T(8,128)S(1)}, bf16[768,512]{1,0:T(8,128)(2,1)S(1)}, f32[4,512]{1,0:T(4,128)S(1)}) custom-call(f32[384,512]{1,0:T(8,128)S(1)} %get-tuple-element.131.refs_0_, f32[384,512]{1,0:T(8,128)S(1)} %get-tuple-element.134.refs_1_, bf16[768,2048]{1,0:T(8,128)(2,1)S(1)} %get-tuple-element.154.refs_2_, bf16[768,512]{1,0:T(8,128)(2,1)S(1)} %bitcast.27, ...), custom_call_target="tpu_custom_call" | custom-call | flops 800000000 | tf_op jit(solution)/shard_map/back/pallas_call | solution.py:160
  64.9 3.5 %rear0.1 = (bf16[432,1536]{1,0:T(8,128)(2,1)S(1)}, f32[2,512]{1,0:T(2,128)S(1)}) custom-call(bf16[384,512]{1,0:T(8,128)(2,1)S(1)} %get-tuple-element.163.q, bf16[432,512]{1,0:T(8,128)(2,1)S(1)} %get-tuple-element.164.k, bf16[432,512]{1,0:T(8,128)(2,1)S(1)} %get-tuple-element.165.v, bf16[3,4,192,256]{3,2,1,0:T(8,128)(2,1)S(1)} %get-tuple-element.166.p, ...), custom_call_target="tpu_custom_call" | custom-call | flops 700000000 | tf_op jit(solution)/shard_map/rear0/pallas_call | solution.py:160
  70.5 3.3 %rear1.1 = (bf16[432,1536]{1,0:T(8,128)(2,1)S(1)}, f32[2,512]{1,0:T(2,128)S(1)}) custom-call(bf16[384,512]{1,0:T(8,128)(2,1)S(1)} %get-tuple-element.174.q, bf16[432,512]{1,0:T(8,128)(2,1)S(1)} %get-tuple-element.175.k, bf16[432,512]{1,0:T(8,128)(2,1)S(1)} %get-tuple-element.176.v, bf16[3,4,192,256]{3,2,1,0:T(8,128)(2,1)S(1)} %get-tuple-element.177.p, ...), custom_call_target="tpu_custom_call" | custom-call | flops 700000000 | tf_op jit(solution)/shard_map/rear1/pallas_call | solution.py:160
  75.7 1.6 %collective-permute-start.31 = (bf16[256,256]{1,0:T(8,128)(2,1)S(1)}, bf16[256,256]{1,0:T(8,128)(2,1)S(1)}, u32[]{:S(2)}, u32[]{:S(2)}) collective-permute-start(bf16[256,256]{1,0:T(8,128)(2,1)S(1)} %get-tuple-element.184), channel_id=1, source_target_pairs={{0,8},{8,0},{16,24},{24,16},{1,9},{9,1},{17,25},{25,17},{2,10},{10... | collective-permute-start | bytes 393224 | tf_op jit(solution)/shard_map/ppermute | solution.py:591
  79.5 5.9 %base.1 = (bf16[2,4,64,2176]{3,2,1,0:T(8,128)(2,1)S(1)}, f32[2,384,512]{2,1,0:T(8,128)}, f32[16,512]{1,0:T(8,128)}) custom-call(bf16[2,384,512]{2,1,0:T(8,128)(2,1)S(1)} %bitcast.24, f32[768,512]{1,0:T(8,128)S(1)} %get-tuple-element.185.dresid, f32[16,512]{1,0:T(8,128)S(1)} %get-tuple-element.200.vecs_in.refs_3_.refs_4_.vecs, ...), custom_call_target="tpu_custom_call" | custom-call | flops 600000000 | tf_op jit(solution)/shard_map/base/pallas_call | solution.py:160
  86.3 2.6 %collective-permute-start.43 = (bf16[256,256]{1,0:T(8,128)(2,1)S(1)}, bf16[256,256]{1,0:T(8,128)(2,1)S(1)}, u32[]{:S(2)}, u32[]{:S(2)}) collective-permute-start(bf16[256,256]{1,0:T(8,128)(2,1)S(1)} %plus.10.refs_0_), channel_id=1, source_target_pairs={{0,16},{8,24},{16,0},{24,8},{1,17},{9,25},{17,1},{25,9},{2,18},{10... | collective-permute-start | bytes 393224 | tf_op jit(solution)/shard_map/ppermute | solution.py:591
  92.8 1.7 %collective-permute-done.42.refs_1_ = bf16[32,2048]{1,0:T(8,128)(2,1)S(1)} collective-permute-done((bf16[32,2048]{1,0:T(8,128)(2,1)S(1)}, bf16[32,2048]{1,0:T(8,128)(2,1)S(1)}, u32[]{:S(2)}, u32[]{:S(2)}) %collective-permute-start.42) | collective-permute-done | bytes 131104 | tf_op jit(solution)/shard_map/ppermute | solution.py:591
  96.0 2.7 %finish.1 = bf16[768,512]{1,0:T(8,128)(2,1)} custom-call(f32[16,512]{1,0:T(8,128)S(1)} %get-tuple-element.200.vecs_in.refs_3_.refs_4_.vecs, bf16[768,2048]{1,0:T(8,128)(2,1)S(1)} %get-tuple-element.201.hidden, bf16[2048,512]{1,0:T(8,128)(2,1)S(1)} %get-tuple-element.202.down, f32[384,512]{1,0:T(8,128)S(1)} %get-tuple-element.131.refs_0_, ...), custom_call_target="tpu_custom_call" | custom-call | flops 400000000 | tf_op jit(solution)/shard_map/finish/pallas_call | solution.py:160
  98.7 4.7 %collective-permute-done.44.refs_1_ = bf16[32,2048]{1,0:T(8,128)(2,1)S(1)} collective-permute-done((bf16[32,2048]{1,0:T(8,128)(2,1)S(1)}, bf16[32,2048]{1,0:T(8,128)(2,1)S(1)}, u32[]{:S(2)}, u32[]{:S(2)}) %collective-permute-start.44) | collective-permute-done | bytes 131104 | tf_op jit(solution)/shard_map/ppermute | solution.py:591
  104.8 2.4 %collective-permute-start.36 = (bf16[16,2176]{1,0:T(8,128)(2,1)S(1)}, bf16[16,2176]{1,0:T(8,128)(2,1)S(1)}, u32[]{:S(2)}, u32[]{:S(2)}) collective-permute-start(bf16[16,2176]{1,0:T(8,128)(2,1)S(1)} %get-tuple-element.208), channel_id=1, source_target_pairs={{0,24},{8,16},{16,8},{24,0},{1,25},{9,17},{17,9},{25,1},{2,26},{10... | collective-permute-start | bytes 208904 | tf_op jit(solution)/shard_map/ppermute | solution.py:591
  111.5 3.1 %collective-permute-done.37.refs_2_ = bf16[16,2176]{1,0:T(8,128)(2,1)S(1)} collective-permute-done((bf16[16,2176]{1,0:T(8,128)(2,1)S(1)}, bf16[16,2176]{1,0:T(8,128)(2,1)S(1)}, u32[]{:S(2)}, u32[]{:S(2)}) %collective-permute-start.37) | collective-permute-done | bytes 69664 | tf_op jit(solution)/shard_map/ppermute | solution.py:591
  114.7 2.5 %collective-permute-start.41 = (bf16[16,2176]{1,0:T(8,128)(2,1)S(1)}, bf16[16,2176]{1,0:T(8,128)(2,1)S(1)}, u32[]{:S(2)}, u32[]{:S(2)}) collective-permute-start(bf16[16,2176]{1,0:T(8,128)(2,1)S(1)} %plus.12.refs_0_), channel_id=1, source_target_pairs={{0,24},{8,16},{16,8},{24,0},{1,25},{9,17},{17,9},{25,1},{2,26},{10... | collective-permute-start | bytes 208904 | tf_op jit(solution)/shard_map/ppermute | solution.py:591
  117.1 2.0 %collective-permute-start.39 = (bf16[16,2176]{1,0:T(8,128)(2,1)S(1)}, bf16[16,2176]{1,0:T(8,128)(2,1)S(1)}, u32[]{:S(2)}, u32[]{:S(2)}) collective-permute-start(bf16[16,2176]{1,0:T(8,128)(2,1)S(1)} %plus.12.refs_0_), channel_id=1, source_target_pairs={{0,8},{8,0},{16,24},{24,16},{1,9},{9,1},{17,25},{25,17},{2,10},{10... | collective-permute-start | bytes 208904 | tf_op jit(solution)/shard_map/ppermute | solution.py:591
  121.1 2.6 %collective-permute-done.40.refs_2_ = bf16[16,2176]{1,0:T(8,128)(2,1)S(1)} collective-permute-done((bf16[16,2176]{1,0:T(8,128)(2,1)S(1)}, bf16[16,2176]{1,0:T(8,128)(2,1)S(1)}, u32[]{:S(2)}, u32[]{:S(2)}) %collective-permute-start.40) | collective-permute-done | bytes 69664 | tf_op jit(solution)/shard_map/ppermute | solution.py:591
  (120 shorter events, 44.0 us)
Async XLA Ops:
  3.0 11.3 %collective-permute-start.2 = (bf16[272,512]{1,0:T(8,128)(2,1)}, bf16[272,512]{1,0:T(8,128)(2,1)S(1)}, u32[]{:S(2)}, u32[]{:S(2)}) collective-permute-start(bf16[272,512]{1,0:T(8,128)(2,1)} %pack.1.refs_0_), channel_id=1, source_target_pairs={{0,6},{1,7},{2,4},{3,5},{4,2},{5,3},{6,0},{7,1},{8,14},{9,15},{10,... | collective-permute-start | bytes 835592 | tf_op jit(solution)/shard_map/ppermute | solution.py:587
  6.5 13.4 %collective-permute-start.1 = (bf16[272,512]{1,0:T(8,128)(2,1)}, bf16[272,512]{1,0:T(8,128)(2,1)S(1)}, u32[]{:S(2)}, u32[]{:S(2)}) collective-permute-start(bf16[272,512]{1,0:T(8,128)(2,1)} %pack.1.refs_0_), channel_id=1, source_target_pairs={{0,4},{1,5},{2,6},{3,7},{4,0},{5,1},{6,2},{7,3},{8,12},{9,13},{10,... | collective-permute-start | bytes 835592 | tf_op jit(solution)/shard_map/ppermute | solution.py:587
  7.0 13.2 %collective-permute-start = (bf16[272,512]{1,0:T(8,128)(2,1)}, bf16[272,512]{1,0:T(8,128)(2,1)S(1)}, u32[]{:S(2)}, u32[]{:S(2)}) collective-permute-start(bf16[272,512]{1,0:T(8,128)(2,1)} %pack.1.refs_0_), channel_id=1, source_target_pairs={{0,2},{1,3},{2,0},{3,1},{4,6},{5,7},{6,4},{7,5},{8,10},{9,11},{10,... | collective-permute-start | bytes 835592 | tf_op jit(solution)/shard_map/ppermute | solution.py:587
  21.2 16.0 %collective-permute-start.12 = (bf16[64,2048]{1,0:T(8,128)(2,1)S(1)}, bf16[64,2048]{1,0:T(8,128)(2,1)S(1)}, u32[]{:S(2)}, u32[]{:S(2)}) collective-permute-start(bf16[64,2048]{1,0:T(8,128)(2,1)S(1)} %copy-done.5), channel_id=1, source_target_pairs={{0,6},{1,7},{2,4},{3,5},{4,2},{5,3},{6,0},{7,1},{8,14},{9,15},{10,... | collective-permute-start | bytes 786440 | tf_op jit(solution)/shard_map/ppermute | solution.py:587
  22.9 14.3 %collective-permute-start.11 = (bf16[64,2048]{1,0:T(8,128)(2,1)S(1)}, bf16[64,2048]{1,0:T(8,128)(2,1)S(1)}, u32[]{:S(2)}, u32[]{:S(2)}) collective-permute-start(bf16[64,2048]{1,0:T(8,128)(2,1)S(1)} %copy-done.5), channel_id=1, source_target_pairs={{0,4},{1,5},{2,6},{3,7},{4,0},{5,1},{6,2},{7,3},{8,12},{9,13},{10,... | collective-permute-start | bytes 786440 | tf_op jit(solution)/shard_map/ppermute | solution.py:587
  24.4 12.9 %collective-permute-start.10 = (bf16[64,2048]{1,0:T(8,128)(2,1)S(1)}, bf16[64,2048]{1,0:T(8,128)(2,1)S(1)}, u32[]{:S(2)}, u32[]{:S(2)}) collective-permute-start(bf16[64,2048]{1,0:T(8,128)(2,1)S(1)} %copy-done.5), channel_id=1, source_target_pairs={{0,2},{1,3},{2,0},{3,1},{4,6},{5,7},{6,4},{7,5},{8,10},{9,11},{10,... | collective-permute-start | bytes 786440 | tf_op jit(solution)/shard_map/ppermute | solution.py:587
  30.2 11.4 %collective-permute-start.9 = (bf16[256,512]{1,0:T(8,128)(2,1)S(1)}, bf16[256,512]{1,0:T(8,128)(2,1)S(1)}, u32[]{:S(2)}, u32[]{:S(2)}) collective-permute-start(bf16[256,512]{1,0:T(8,128)(2,1)S(1)} %copy-done.6), channel_id=1, source_target_pairs={{0,4},{1,5},{2,6},{3,7},{4,0},{5,1},{6,2},{7,3},{8,12},{9,13},{10,... | collective-permute-start | bytes 786440 | tf_op jit(solution)/shard_map/ppermute | solution.py:587
  31.7 9.9 %collective-permute-start.8 = (bf16[256,512]{1,0:T(8,128)(2,1)S(1)}, bf16[256,512]{1,0:T(8,128)(2,1)S(1)}, u32[]{:S(2)}, u32[]{:S(2)}) collective-permute-start(bf16[256,512]{1,0:T(8,128)(2,1)S(1)} %copy-done.6), channel_id=1, source_target_pairs={{0,2},{1,3},{2,0},{3,1},{4,6},{5,7},{6,4},{7,5},{8,10},{9,11},{10,... | collective-permute-start | bytes 786440 | tf_op jit(solution)/shard_map/ppermute | solution.py:587
  41.6 9.1 %collective-permute-start.17 = (bf16[256,512]{1,0:T(8,128)(2,1)S(1)}, bf16[256,512]{1,0:T(8,128)(2,1)S(1)}, u32[]{:S(2)}, u32[]{:S(2)}) collective-permute-start(bf16[256,512]{1,0:T(8,128)(2,1)S(1)} %copy-done.6), channel_id=1, source_target_pairs={{0,6},{1,7},{2,4},{3,5},{4,2},{5,3},{6,0},{7,1},{8,14},{9,15},{10,... | collective-permute-start | bytes 786440 | tf_op jit(solution)/shard_map/ppermute | solution.py:587
  43.1 7.9 %collective-permute-start.18 = (bf16[256,512]{1,0:T(8,128)(2,1)S(1)}, bf16[256,512]{1,0:T(8,128)(2,1)S(1)}, u32[]{:S(2)}, u32[]{:S(2)}) collective-permute-start(bf16[256,512]{1,0:T(8,128)(2,1)S(1)} %collective-permute-done.8.refs_2_), channel_id=1, source_target_pairs={{0,1},{1,0},{2,3},{3,2},{4,5},{5,4},{6,7},{7,6},{8,9},{9,8},{10,11... | collective-permute-start | bytes 786440 | tf_op jit(solution)/shard_map/ppermute | solution.py:587
  57.5 10.9 %collective-permute-start.26 = (bf16[2,256,256]{2,1,0:T(8,128)(2,1)S(1)}, bf16[2,256,256]{2,1,0:T(8,128)(2,1)S(1)}, u32[]{:S(2)}, u32[]{:S(2)}) collective-permute-start(bf16[2,256,256]{2,1,0:T(8,128)(2,1)S(1)} %get-tuple-element.161), channel_id=1, source_target_pairs={{0,4},{1,5},{2,6},{3,7},{4,0},{5,1},{6,2},{7,3},{8,12},{9,13},{10,... | collective-permute-start | bytes 786440 | tf_op jit(solution)/shard_map/ppermute | solution.py:587
  59.0 9.4 %collective-permute-start.25 = (bf16[2,256,256]{2,1,0:T(8,128)(2,1)S(1)}, bf16[2,256,256]{2,1,0:T(8,128)(2,1)S(1)}, u32[]{:S(2)}, u32[]{:S(2)}) collective-permute-start(bf16[2,256,256]{2,1,0:T(8,128)(2,1)S(1)} %get-tuple-element.153), channel_id=1, source_target_pairs={{0,2},{1,3},{2,0},{3,1},{4,6},{5,7},{6,4},{7,5},{8,10},{9,11},{10,... | collective-permute-start | bytes 786440 | tf_op jit(solution)/shard_map/ppermute | solution.py:587
  62.8 11.0 %collective-permute-start.24 = (bf16[2,32,2048]{2,1,0:T(8,128)(2,1)S(1)}, bf16[2,32,2048]{2,1,0:T(8,128)(2,1)S(1)}, u32[]{:S(2)}, u32[]{:S(2)}) collective-permute-start(bf16[2,32,2048]{2,1,0:T(8,128)(2,1)S(1)} %get-tuple-element.160), channel_id=1, source_target_pairs={{0,4},{1,5},{2,6},{3,7},{4,0},{5,1},{6,2},{7,3},{8,12},{9,13},{10,... | collective-permute-start | bytes 786440 | tf_op jit(solution)/shard_map/ppermute | solution.py:587
  64.4 9.4 %collective-permute-start.23 = (bf16[2,32,2048]{2,1,0:T(8,128)(2,1)S(1)}, bf16[2,32,2048]{2,1,0:T(8,128)(2,1)S(1)}, u32[]{:S(2)}, u32[]{:S(2)}) collective-permute-start(bf16[2,32,2048]{2,1,0:T(8,128)(2,1)S(1)} %get-tuple-element.159), channel_id=1, source_target_pairs={{0,2},{1,3},{2,0},{3,1},{4,6},{5,7},{6,4},{7,5},{8,10},{9,11},{10,... | collective-permute-start | bytes 786440 | tf_op jit(solution)/shard_map/ppermute | solution.py:587
  75.7 9.7 %collective-permute-start.31 = (bf16[256,256]{1,0:T(8,128)(2,1)S(1)}, bf16[256,256]{1,0:T(8,128)(2,1)S(1)}, u32[]{:S(2)}, u32[]{:S(2)}) collective-permute-start(bf16[256,256]{1,0:T(8,128)(2,1)S(1)} %get-tuple-element.184), channel_id=1, source_target_pairs={{0,8},{8,0},{16,24},{24,16},{1,9},{9,1},{17,25},{25,17},{2,10},{10... | collective-permute-start | bytes 393224 | tf_op jit(solution)/shard_map/ppermute | solution.py:591
  77.5 8.0 %collective-permute-start.30 = (bf16[32,2048]{1,0:T(8,128)(2,1)S(1)}, bf16[32,2048]{1,0:T(8,128)(2,1)S(1)}, u32[]{:S(2)}, u32[]{:S(2)}) collective-permute-start(bf16[32,2048]{1,0:T(8,128)(2,1)S(1)} %get-tuple-element.193), channel_id=1, source_target_pairs={{0,4},{1,5},{2,6},{3,7},{4,0},{5,1},{6,2},{7,3},{8,12},{9,13},{10,... | collective-permute-start | bytes 393224 | tf_op jit(solution)/shard_map/ppermute | solution.py:587
  85.8 8.7 %collective-permute-start.42 = (bf16[32,2048]{1,0:T(8,128)(2,1)S(1)}, bf16[32,2048]{1,0:T(8,128)(2,1)S(1)}, u32[]{:S(2)}, u32[]{:S(2)}) collective-permute-start(bf16[32,2048]{1,0:T(8,128)(2,1)S(1)} %get-tuple-element.196), channel_id=1, source_target_pairs={{0,8},{8,0},{16,24},{24,16},{1,9},{9,1},{17,25},{25,17},{2,10},{10... | collective-permute-start | bytes 393224 | tf_op jit(solution)/shard_map/ppermute | solution.py:591
  86.3 8.2 %collective-permute-start.43 = (bf16[256,256]{1,0:T(8,128)(2,1)S(1)}, bf16[256,256]{1,0:T(8,128)(2,1)S(1)}, u32[]{:S(2)}, u32[]{:S(2)}) collective-permute-start(bf16[256,256]{1,0:T(8,128)(2,1)S(1)} %plus.10.refs_0_), channel_id=1, source_target_pairs={{0,16},{8,24},{16,0},{24,8},{1,17},{9,25},{17,1},{25,9},{2,18},{10... | collective-permute-start | bytes 393224 | tf_op jit(solution)/shard_map/ppermute | solution.py:591
  89.2 14.3 %collective-permute-start.35 = (bf16[64,2176]{1,0:T(8,128)(2,1)S(1)}, bf16[64,2176]{1,0:T(8,128)(2,1)S(1)}, u32[]{:S(2)}, u32[]{:S(2)}) collective-permute-start(bf16[64,2176]{1,0:T(8,128)(2,1)S(1)} %get-tuple-element.242), channel_id=1, source_target_pairs={{0,6},{1,7},{2,4},{3,5},{4,2},{5,3},{6,0},{7,1},{8,14},{9,15},{10,... | collective-permute-start | bytes 835592 | tf_op jit(solution)/shard_map/ppermute | solution.py:587
  90.8 13.8 %collective-permute-start.34 = (bf16[64,2176]{1,0:T(8,128)(2,1)S(1)}, bf16[64,2176]{1,0:T(8,128)(2,1)S(1)}, u32[]{:S(2)}, u32[]{:S(2)}) collective-permute-start(bf16[64,2176]{1,0:T(8,128)(2,1)S(1)} %get-tuple-element.243), channel_id=1, source_target_pairs={{0,4},{1,5},{2,6},{3,7},{4,0},{5,1},{6,2},{7,3},{8,12},{9,13},{10,... | collective-permute-start | bytes 835592 | tf_op jit(solution)/shard_map/ppermute | solution.py:587
  91.5 13.1 %collective-permute-start.33 = (bf16[64,2176]{1,0:T(8,128)(2,1)S(1)}, bf16[64,2176]{1,0:T(8,128)(2,1)S(1)}, u32[]{:S(2)}, u32[]{:S(2)}) collective-permute-start(bf16[64,2176]{1,0:T(8,128)(2,1)S(1)} %get-tuple-element.244), channel_id=1, source_target_pairs={{0,2},{1,3},{2,0},{3,1},{4,6},{5,7},{6,4},{7,5},{8,10},{9,11},{10,... | collective-permute-start | bytes 835592 | tf_op jit(solution)/shard_map/ppermute | solution.py:587
  94.5 8.9 %collective-permute-start.44 = (bf16[32,2048]{1,0:T(8,128)(2,1)S(1)}, bf16[32,2048]{1,0:T(8,128)(2,1)S(1)}, u32[]{:S(2)}, u32[]{:S(2)}) collective-permute-start(bf16[32,2048]{1,0:T(8,128)(2,1)S(1)} %plus.13.refs_0_), channel_id=1, source_target_pairs={{0,16},{8,24},{16,0},{24,8},{1,17},{9,25},{17,1},{25,9},{2,18},{10... | collective-permute-start | bytes 393224 | tf_op jit(solution)/shard_map/ppermute | solution.py:591
  103.4 15.7 %collective-permute-start.45 = (bf16[32,2048]{1,0:T(8,128)(2,1)S(1)}, bf16[32,2048]{1,0:T(8,128)(2,1)S(1)}, u32[]{:S(2)}, u32[]{:S(2)}) collective-permute-start(bf16[32,2048]{1,0:T(8,128)(2,1)S(1)} %plus.14.keep), channel_id=1, source_target_pairs={{0,8},{8,0},{16,24},{24,16},{1,9},{9,1},{17,25},{25,17},{2,10},{10... | collective-permute-start | bytes 393224 | tf_op jit(solution)/shard_map/ppermute | solution.py:591
  109.3 10.6 %collective-permute-start.46 = (bf16[256,256]{1,0:T(8,128)(2,1)S(1)}, bf16[256,256]{1,0:T(8,128)(2,1)S(1)}, u32[]{:S(2)}, u32[]{:S(2)}) collective-permute-start(bf16[256,256]{1,0:T(8,128)(2,1)S(1)} %plus.15.keep), channel_id=1, source_target_pairs={{0,8},{8,0},{16,24},{24,16},{1,9},{9,1},{17,25},{25,17},{2,10},{10... | collective-permute-start | bytes 393224 | tf_op jit(solution)/shard_map/ppermute | solution.py:591
  (31 other events, 198.6 us)

commit v2 on v1

--- a/solution.py
+++ b/solution.py
@@ -190,29 +190,37 @@
             att[rows, lanes] = found.T.astype(BF)
 
 
-def early_body(utter, x, dy, units, biases, dyt):
+def early_body(utter, x, units, scales, biases):
     rows, length, _ = x.shape
     for row in range(rows):
-        units[row] = stats(x[row].astype(F32))[0]
+        unit, scale = stats(x[row].astype(F32))
+        units[row] = unit
+        scales[row] = jnp.broadcast_to(scale, scales.shape[1:])
         visible_bias(biases.at[row], utter, row, length // SEG)
-    dyt[...] = dy[...].T
-
-
-def early(utter, x, dy):
+
+
+def turned(dy):
+    def body(dy, out):
+        out[...] = dy[...].T
+
+    return call(body, "turned", 1, 1, [(full(dy.shape[::-1], BF), False)], [], [dy])[0]
+
+
+def early(utter, x):
     rows, length, model = x.shape
     return pl.pallas_call(
         early_body,
-        in_specs=[pl.BlockSpec(memory_space=pltpu.SMEM), VMEM, VMEM],
+        in_specs=[pl.BlockSpec(memory_space=pltpu.SMEM), VMEM],
         out_specs=[VMEM] * 3,
         out_shape=[
             full((rows, length, model), F32),
+            full((rows, length, 128), F32),
             full((rows, length // QB, KEYS, QB), F32),
-            full((model, rows * length), BF),
         ],
         compiler_params=params(),
         name="early",
         cost_estimate=cost(2),
-    )(utter, x, dy)
+    )(utter, x)
 
 
 def front_body(row, first_call, plan, width, x, units, biases, vecs_in, w_in_in, w_out_in, *refs):
@@ -223,7 +231,8 @@
         vecs, w_in, w_out, *outs = outs
     else:
         vecs, w_in, w_out = vecs_in, w_in_in, w_out_in
-    (q_out, k_out, v_out, wide_out, p_out, att_out, resid_out, n2_out, att, *outs) = outs
+    (q_out, k_out, v_out, wide_out, p_out, att_out, resid_out) = outs[:7]
+    (n2_out, n2t_out, unit_out, scale_out, att, *outs) = outs[7:]
     length, model = x.shape[1], x.shape[2]
     value = x[row].astype(F32)
     if first_call:
@@ -253,8 +262,12 @@
     attention(q_out, k_out, v_out, p_out, biases.at[row], att_out, att, length)
     resid = value + nn(att[...], w_out[...]) + vecs[4:5]
     resid_out[...] = resid
-    unit, _ = stats(resid)
-    n2_out[...] = (unit * vecs[5:6] + vecs[6:7]).astype(BF)
+    unit, scale = stats(resid)
+    unit_out[...] = unit
+    scale_out[...] = jnp.broadcast_to(scale, scale_out.shape)
+    normed = (unit * vecs[5:6] + vecs[6:7]).astype(BF)
+    n2_out[...] = normed
+    n2t_out[...] = normed.T
 
 
 def front(row, x, units, biases, vecs, w_in, w_out, plan, parts, width):
@@ -271,6 +284,9 @@
         full((model, length), BF),
         full((length, model), F32),
         full((length, model), BF),
+        full((model, length), BF),
+        full((length, model), F32),
+        full((length, 128), F32),
     ]
     scratch = [pltpu.VMEM((length, model), BF)]
     if first_call:
@@ -300,11 +316,11 @@
 
 def gelu_both(v):
     c = 0.7978845608028654
+    a = 0.044715
     square = v * v
-    bent = jnp.tanh(c * v * (1.0 + 0.044715 * square))
-    half = 0.5 + 0.5 * bent
-    slope = half + 0.5 * v * (1.0 - bent * bent) * (c * (1.0 + 3 * 0.044715 * square))
-    return v * half, slope
+    half = 0.5 + 0.5 * jnp.tanh(v * (c + (c * a) * square))
+    value = v * half
+    return value, half + value * (1.0 - half) * (2 * c + (6 * c * a) * square)
 
 
 def middle_body(rows, plan, width, *refs):
@@ -328,6 +344,8 @@
             value, slope = gelu_both(u)
             hidden[rows, cols] = value.astype(BF)
             slopes[rows, cols] = slope.astype(BF)
+    for tile in range(ff // TILE):
+        cols = slice(tile * TILE, (tile + 1) * TILE)
         grad = nn(dyt[...], hidden[:, cols]).astype(BF)
         for part in range(TILE // tall):
             inner_cols = slice(part * tall, (part + 1) * tall)
@@ -385,25 +403,24 @@
 
 
 def rise_body(rows, width, *refs):
-    n2s = refs[:rows]
-    du, grads, n2t = refs[rows:]
-    length, model = n2s[0].shape
-    ff = du.shape[1]
+    n2ts = refs[:rows]
+    du, grads, turned = refs[rows:]
+    length = n2ts[0].shape[1]
     put = pieces_into(grads)
     for row in range(rows):
-        n2t[:, row * length : (row + 1) * length] = n2s[row][...].T
-    for tile in range(ff // TILE):
+        turned[:, row * length : (row + 1) * length] = n2ts[row][...]
+    for tile in range(du.shape[1] // TILE):
         cols = slice(tile * TILE, (tile + 1) * TILE)
-        put_rows(put, nn(n2t[...], du[:, cols]).astype(BF), width, cols)
-
-
-def rise(n2s, du, width, fast):
+        put_rows(put, nn(turned[...], du[:, cols]).astype(BF), width, cols)
+
+
+def rise(n2ts, du, width, fast):
     tokens, ff = du.shape
-    model = n2s[0].shape[1]
+    model = n2ts[0].shape[0]
     shape = (2, 4, width, ff) if fast else (model, ff)
+    body = functools.partial(rise_body, len(n2ts), width)
+    args = [*n2ts, du]
     scratch = [pltpu.VMEM((model, tokens), BF)]
-    body = functools.partial(rise_body, len(n2s), width)
-    args = [*n2s, du]
     return call(body, "rise", 4, len(args), [(full(shape, BF), False)], scratch, args)[0]
 
 
@@ -414,10 +431,11 @@
 
 
 def back_body(rows, *refs):
-    resids = refs[:rows]
-    du, dy, vecs, up, w_out, dresid, datt, sums = refs[rows:]
+    units = refs[:rows]
+    scales = refs[rows : 2 * rows]
+    du, dy, vecs, up, w_out, dresid, datt, sums = refs[2 * rows :]
     tokens, model = dy.shape
-    length = resids[0].shape[0]
+    length = units[0].shape[0]
     step = length
     gains = jnp.zeros((1, model), F32)
     shifts = jnp.zeros((1, model), F32)
@@ -427,7 +445,8 @@
         rows = slice(chunk * step, (chunk + 1) * step)
         at = chunk * step % length
         grad = nt(du[rows], up[...])
-        unit, scale = stats(resids[chunk * step // length][at : at + step])
+        unit = units[chunk * step // length][at : at + step]
+        scale = scales[chunk * step // length][at : at + step, 0:1]
         gains = gains + jnp.sum(grad * unit, axis=0, keepdims=True)
         shifts = shifts + jnp.sum(grad, axis=0, keepdims=True)
         top = dy[rows].astype(F32)
@@ -442,15 +461,15 @@
     sums[3:4] = downs
 
 
-def back(resids, du, dy, vecs, up, w_out):
+def back(units, scales, du, dy, vecs, up, w_out):
     tokens, model = dy.shape
     outs = [
         (full((tokens, model), F32), False),
         (full((tokens, model), BF), False),
         (full((4, model), F32), False),
     ]
-    args = [*resids, du, dy, vecs, up, w_out]
-    return call(functools.partial(back_body, len(resids)), "back", 8, len(args), outs, [], args)
+    args = [*units, *scales, du, dy, vecs, up, w_out]
+    return call(functools.partial(back_body, len(units)), "back", 8, len(args), outs, [], args)
 
 
 def rear_body(row, q, k, v, p, datt, mixed, sums, dk, dv):
@@ -499,13 +518,13 @@
     return call(body, f"rear{row}", 7, 5, outs, scratch, [q, k, v, p, datt])
 
 
-def base_body(rows, width, x, dresid, vecs, w_in, gub, back_sums, *refs):
+def base_body(rows, width, units, dresid, w_in, gub, back_sums, *refs):
     mixeds = refs[:rows]
     rear_sums = refs[rows : 2 * rows]
     wides = refs[2 * rows : 3 * rows]
     atts = refs[3 * rows : 4 * rows]
-    grads, dx, sums = refs[4 * rows :]
-    length, model = x.shape[1], x.shape[2]
+    grads, dnormed, sums = refs[4 * rows :]
+    length, model = units.shape[1], units.shape[2]
     put = pieces_into(grads)
     for tile in range(3):
         cols = slice(tile * model, (tile + 1) * model)
@@ -521,12 +540,11 @@
     gains = jnp.zeros((1, model), F32)
     shifts = jnp.zeros((1, model), F32)
     for row in range(rows):
-        unit, scale = stats(x[row].astype(F32))
         grad = nt(mixeds[row][...], w_in[...])
         grad = grad[:length] + tn(average, grad[length:].astype(BF))
-        gains = gains + jnp.sum(grad * unit, axis=0, keepdims=True)
+        gains = gains + jnp.sum(grad * units[row], axis=0, keepdims=True)
         shifts = shifts + jnp.sum(grad, axis=0, keepdims=True)
-        dx[row] = dresid[row * length : (row + 1) * length] + norm_back(grad * vecs[0:1], unit, scale)
+        dnormed[row] = grad
     sums[0:1] = gains
     sums[1:2] = shifts
     sums[2:4] = wide_sum(*[part[...] for part in rear_sums])
@@ -553,16 +571,28 @@
             )
 
 
-def base(x, dresid, vecs, w_in, gub, back_sums, mixeds, rear_sums, wides, atts, width, fast):
-    rows, length, model = x.shape
+def base(units, dresid, w_in, gub, back_sums, mixeds, rear_sums, wides, atts, width, fast):
+    rows, length, model = units.shape
     shape = (2, 4, width, 4 * model + 128) if fast else (model, 4 * model)
     outs = [
         (full(shape, BF), False),
         (full((rows, length, model), F32), False),
         (full((16, model), F32), False),
     ]
-    args = [x, dresid, vecs, w_in, gub, back_sums, *mixeds, *rear_sums, *wides, *atts]
+    args = [units, dresid, w_in, gub, back_sums, *mixeds, *rear_sums, *wides, *atts]
     return call(functools.partial(base_body, rows, width), "base", 6, len(args), outs, [], args)
+
+
+def shed_body(units, scales, dresid, vecs, dnormed, dx):
+    rows, length, _ = units.shape
+    for row in range(rows):
+        own = dresid[row * length : (row + 1) * length]
+        dx[row] = own + norm_back(dnormed[row] * vecs[0:1], units[row], scales[row, :, 0:1])
+
+
+def shed(units, scales, dresid, vecs, dnormed):
+    args = [units, scales, dresid, vecs, dnormed]
+    return call(shed_body, "shed", 2, 5, [(full(units.shape, F32), False)], [], args)[0]
 
 
 def finish_body(rows, vecs, hidden, down, *refs):
@@ -861,9 +891,11 @@
     if fast:
         plan_a, plan_u, plan_d = near_plan(packed.shape[0]), near_plan(width), near_plan(tall)
         a2, a4, a6, a1 = [along(packed, offset) for offset in (2, 4, 6, 1)]
-        units, biases, dyt = early(after(utter, a1), x, dy)
-        a2, a4, a6, dyt = lax.optimization_barrier((a2, a4, a6, dyt))
-        up_piece = after(up_weight, a2, a4, a6)
+        units, scales, biases = early(after(utter, a1), x)
+        a6, units = lax.optimization_barrier((a6, units))
+        up_piece = after(up_weight, a6)
+        dyt = turned(after(dy, a6))
+        a2, a4, dyt = lax.optimization_barrier((a2, a4, dyt))
         u2, u4, u1 = along(up_piece, 2), along(up_piece, 4), along(up_piece, 1)
         parts_a = [packed, a1, a2, a4, a6, along(a2, 1), along(a4, 1)] + [along(a6, 1)]
         u6 = along(up_piece, 6)
@@ -874,24 +906,29 @@
         parts_u = [lax.all_gather(up_weight, "fsdp", axis=0, tiled=True)]
         parts_d = [lax.all_gather(down_weight, "fsdp", axis=0, tiled=True)]
         first = x
-        units, biases, dyt = early(utter, x, dy)
+        units, scales, biases = early(utter, x)
+        dyt = turned(dy)
     saved = []
     vecs, w_in, w_out, *first = front(0, first, units, biases, None, None, None, plan_a, parts_a, width)
     saved.append(first)
     held = vecs
     if fast:
-        held = vecs
+        held = after(vecs, u2, u4)
+        done = first[-1]
+        u3, u5 = along(after(u2, done), 1), along(after(u4, done), 1)
     for row in range(1, rows):
         saved.append(front(row, x, units, biases, held, w_in, w_out, plan_a, None, width))
-    qs, ks, vs, wides, ps, atts, resids, n2s = zip(*saved)
+    qs, ks, vs, wides, ps, atts, resids, n2s, n2ts, unit2s, scale2s = zip(*saved)
     if fast:
         down_piece = after(down_weight, n2s[0])
         d2, d4 = along(down_piece, 2), along(down_piece, 4)
-        *u_got, done = lax.optimization_barrier((u2, u4, u6, n2s[1]))
-        parts_u = [up_piece, u1, *u_got] + [along(part, 1) for part in u_got[:2]] + [along(u_got[2], 1)]
-        d2, d4, down_piece, done = lax.optimization_barrier((d2, d4, down_piece, done))
+        u6, u3, u5, done = lax.optimization_barrier((u6, u3, u5, n2s[1]))
+        parts_u = [up_piece, u1, u2, u4, u6, u3, u5, along(u6, 1)]
+        down_piece, done = lax.optimization_barrier((down_piece, done))
+        d6 = along(down_piece, 6)
+        d2, d4, done = lax.optimization_barrier((d2, d4, done))
         held = after(vecs, d2, d4)
-        d3, d5, d6, d1 = along(d2, 1), along(d4, 1), along(down_piece, 6), along(down_piece, 1)
+        d3, d5, d1 = along(d2, 1), along(d4, 1), along(after(down_piece, d2), 1)
     hidden, slopes, up, gdown = middle(n2s, dyt, held, parts_u, plan_u, width, ff, fast)
     if fast:
         d6 = after(d6, slopes)
@@ -899,12 +936,12 @@
     if fast:
         du, gub, down = turn(dy, slopes, parts_d, plan_d)
         d_core = along(after(gdown, gub)[1], 1)
-        gup = rise(n2s, du, width, fast)
+        gup = rise(n2ts, du, width, fast)
         d_sum = plus_here(gdown, after(d_core, gup))
         to_x, to_y = cross_halves(d_sum)
         d_x, d_y = along(to_x, 2), along(to_y, 4)
         u_core = along(gup[1], 1)
-        dresid, datt, sums2 = back(resids, after(du, to_x), dy, vecs, up, w_out)
+        dresid, datt, sums2 = back(unit2s, scale2s, after(du, to_x), dy, vecs, up, w_out)
         u_core, done = lax.optimization_barrier((u_core, sums2))
         u_sum = plus_here(gup, u_core)
         to_x, to_y = cross_halves(u_sum)
@@ -920,10 +957,9 @@
         d_keep, d_send = hop_halves(d_sum, d_x, d_y, d_x2, d_y2)
         d_z = across(d_send, 1, group)
         mixeds = (mixed0, mixed1)
-        gin, dx, small = base(
-            x,
+        gin, dnormed, small = base(
+            units,
             after(dresid, to_x, d_send),
-            vecs,
             w_in,
             gub,
             sums2,
@@ -943,7 +979,8 @@
         i_sum = plus_here(gin, i_core)
         i_got = [along(i_sum[1], 2), along(i_sum[2], 4), along(i_sum[3], 6)]
         out = finish(after(vecs, i_sum), hidden, down, resids)
-        *i_got, done = lax.optimization_barrier((*i_got, out))
+        dx = shed(units, scales, dresid, after(vecs, out), dnormed)
+        *i_got, done = lax.optimization_barrier((*i_got, dx))
         u_z, d_z2, done = lax.optimization_barrier((u_z, d_z2, i_sum))
         u_keep = plus(u_keep, u_z)
         u_z2 = across(u_keep, 2, group)
@@ -960,13 +997,14 @@
         g_in, g_out, *vectors = last_in([i_own, *i_got], model, width, tall)
     else:
         du, gub, down = turn(dy, slopes, parts_d, plan_d)
-        dresid, datt, sums2 = back(resids, du, dy, vecs, up, w_out)
-        gup = rise(n2s, du, width, fast)
+        dresid, datt, sums2 = back(unit2s, scale2s, du, dy, vecs, up, w_out)
+        gup = rise(n2ts, du, width, fast)
         pairs = [rear(row, qs[row], ks[row], vs[row], ps[row], datt) for row in range(rows)]
         mixeds, rear_sums = zip(*pairs)
-        gin, dx, small = base(
-            x, dresid, vecs, w_in, gub, sums2, mixeds, rear_sums, wides, atts, width, fast
+        gin, dnormed, small = base(
+            units, dresid, w_in, gub, sums2, mixeds, rear_sums, wides, atts, width, fast
         )
+        dx = shed(units, scales, dresid, vecs, dnormed)
         out = finish(vecs, hidden, down, resids)
 
         def total(value, dim):

time: 125 us -> 121 us (0.968)
  waiting for transfers between devices: 31 us -> 26.8 us
    ppermute x35, waiting for transfers between devices: 17.2 us -> 14.9 us  [along(): return lax.ppermute(value, 'fsdp', [(i, i ^ offset) for i in range(8)])]
    ppermute x12, waiting for transfers between devices: 13.8 us -> 11.9 us  [across(): return lax.ppermute(value, 'dp', [(i, i ^ offset) for i in range(size)])]
    pallas_call x27 -> x29, Pallas kernels: 34.9 us -> 35.3 us  [call(): pl.pallas_call(body, in_specs=[VMEM] * ins + [HBM] * (len(args) - ins), o...]
  transfers between devices with their start and end apart: 47 -> 47, of which waited for: 17 -> 17; matrix products, arithmetic and copies ran while one was open for 0% -> 0% of each run, Pallas kernels for 33% -> 34%
where the time goes in v2:
time: 121 us
  Pallas kernels  46.8 us (39%)
  starting transfers between devices  43.4 us (36%)
  waiting for transfers between devices  26.8 us (22%)
  local copies, waits for them, and re-layouts  3.25 us (3%)
    pallas_call x29, Pallas kernels, call(): pl.pallas_call(body, in_specs=[VMEM] * ins + [HBM] * (len(args) - ins), o...  35.3 us
    ppermute x35, starting transfers between devices, along(): return lax.ppermute(value, 'fsdp', [(i, i ^ offset) for i in range(8)])  26.5 us
    ppermute x12, starting transfers between devices, across(): return lax.ppermute(value, 'dp', [(i, i ^ offset) for i in range(size)])  16.9 us
    ppermute x35, waiting for transfers between devices, along(): return lax.ppermute(value, 'fsdp', [(i, i ^ offset) for i in range(8)])  14.9 us
    ppermute x12, waiting for transfers between devices, across(): return lax.ppermute(value, 'dp', [(i, i ^ offset) for i in range(size)])  11.9 us
    pallas_call x2, Pallas kernels, front(): pl.pallas_call(body, in_specs=specs, out_specs=[VMEM] * len(outs), out_sh...  10.2 us
    unnamed x16, local copies, waits for them, and re-layouts  2.97 us
  transfers between devices with their start and end apart: 47, of which 17 were waited for; matrix products, arithmetic and copies ran while one was open for 0% of the time, Pallas kernels for 34%

profile of v2, /device:TPU:0, one launch (start us, length us, event | category | flops | bytes accessed | tf_op | source)
XLA Modules:
  0.0 121.2 jit_solution(7509058807936424342)
XLA Ops:
  0.7 1.8 %pack.1.refs_0_ = bf16[272,512]{1,0:T(8,128)(2,1)} custom-call(bf16[64,1536]{1,0:T(8,128)(2,1)} %refs_0_.1, bf16[64,512]{1,0:T(8,128)(2,1)} %refs_1_.1, bf16[64]{0:T(256)(128)(2,1)} %refs_2_.1, bf16[64]{0:T(256)(128)(2,1)} %refs_3_.1, bf16[64]{0:T(256)(128)(2,1)} %refs_4_.1, bf16[64]{0:T(256)(128)(2,1)} %refs_5_.1, bf16[64]{0:T(256)(128)(2,1)} %refs_6_.1, ...), custom_call_target="tpu_custom_call" | custom-call | flops 200000000 | tf_op jit(solution)/shard_map/pack/pallas_call | solution.py:160
  3.0 3.5 %collective-permute-start = (bf16[272,512]{1,0:T(8,128)(2,1)}, bf16[272,512]{1,0:T(8,128)(2,1)S(1)}, u32[]{:S(2)}, u32[]{:S(2)}) collective-permute-start(bf16[272,512]{1,0:T(8,128)(2,1)} %pack.1.refs_0_), channel_id=1, source_target_pairs={{0,6},{1,7},{2,4},{3,5},{4,2},{5,3},{6,0},{7,1},{8,14},{9,15},{10,... | collective-permute-start | bytes 835592 | tf_op jit(solution)/shard_map/ppermute | solution.py:617
  10.2 4.0 %collective-permute-done.refs_4_ = bf16[272,512]{1,0:T(8,128)(2,1)S(1)} collective-permute-done((bf16[272,512]{1,0:T(8,128)(2,1)}, bf16[272,512]{1,0:T(8,128)(2,1)S(1)}, u32[]{:S(2)}, u32[]{:S(2)}) %collective-permute-start) | collective-permute-done | bytes 278560 | tf_op jit(solution)/shard_map/ppermute | solution.py:617
  16.1 3.8 %collective-permute-done.4.refs_3_ = bf16[272,512]{1,0:T(8,128)(2,1)S(1)} collective-permute-done((bf16[272,512]{1,0:T(8,128)(2,1)}, bf16[272,512]{1,0:T(8,128)(2,1)S(1)}, u32[]{:S(2)}, u32[]{:S(2)}) %collective-permute-start.4) | collective-permute-done | bytes 278560 | tf_op jit(solution)/shard_map/ppermute | solution.py:617
  24.3 5.2 %front0.1 = (f32[16,512]{1,0:T(8,128)S(1)}, bf16[512,1536]{1,0:T(8,128)(2,1)S(1)}, bf16[512,512]{1,0:T(8,128)(2,1)S(1)}, bf16[384,512]{1,0:T(8,128)(2,1)S(1)}, b...) custom-call(bf16[2,384,512]{2,1,0:T(8,128)(2,1)S(1)} %bitcast.22, ...), custom_call_target="tpu_custom_call" | custom-call | flops 700000000 | tf_op jit(solution)/shard_map/front0/pallas_call | solution.py:305
  29.5 1.9 %collective-permute-done.8.refs_6_ = bf16[64,2048]{1,0:T(8,128)(2,1)S(1)} collective-permute-done((bf16[64,2048]{1,0:T(8,128)(2,1)S(1)}, bf16[64,2048]{1,0:T(8,128)(2,1)S(1)}, u32[]{:S(2)}, u32[]{:S(2)}) %collective-permute-start.8) | collective-permute-done | bytes 262176 | tf_op jit(solution)/shard_map/ppermute | solution.py:617
  34.0 5.0 %front1.1 = (bf16[384,512]{1,0:T(8,128)(2,1)S(1)}, bf16[432,512]{1,0:T(8,128)(2,1)S(1)}, bf16[432,512]{1,0:T(8,128)(2,1)S(1)}, bf16[512,432]{1,0:T(8,128)(2,1)S(...) custom-call(bf16[2,384,512]{2,1,0:T(8,128)(2,1)S(1)} %bitcast.23, ...), custom_call_target="tpu_custom_call" | custom-call | flops 700000000 | tf_op jit(solution)/shard_map/front1/pallas_call | solution.py:305
  41.9 6.2 %middle.1 = (bf16[768,2048]{1,0:T(8,128)(2,1)S(1)}, bf16[768,2048]{1,0:T(8,128)(2,1)S(1)}, bf16[512,2048]{1,0:T(8,128)(2,1)S(1)}, bf16[2,4,512,256]{3,2,1,0:T(8,128)(2,1)S(1)}) custom-call(bf16[384,512]{1,0:T(8,128)(2,1)S(1)} %get-tuple-element.151.refs_0_, bf16[384,512]{1,0:T(8,128)(2,1)S(1)} %get-tuple-element.152.refs_1_, ...), custom_call_target="tpu_custom_call" | custom-call | flops 800000000 | tf_op jit(solution)/shard_map/middle/pallas_call | solution.py:160
  50.3 2.1 %turn.1 = (bf16[768,2048]{1,0:T(8,128)(2,1)S(1)}, f32[4,512]{1,0:T(4,128)S(1)}, bf16[2048,512]{1,0:T(8,128)(2,1)S(1)}) custom-call(bf16[768,512]{1,0:T(8,128)(2,1)S(1)} %bitcast.25, bf16[768,2048]{1,0:T(8,128)(2,1)S(1)} %get-tuple-element.163.slopes, bf16[256,512]{1,0:T(8,128)(2,1)S(1)} %copy-done.6, bf16[256,512]{1,0:T(8,128)(2,1)S(1)} %collective-permute-done.16.refs_1_, ...), custom_call_target="tpu_custom_call" | custom-call | flops 500000000 | tf_op jit(solution)/shard_map/turn/pallas_call | solution.py:160
  52.7 1.8 %rise.1.both = bf16[2,4,64,2048]{3,2,1,0:T(8,128)(2,1)S(1)} custom-call(bf16[512,384]{1,0:T(8,128)(2,1)S(1)} %get-tuple-element.170.refs_0_, bf16[512,384]{1,0:T(8,128)(2,1)S(1)} %get-tuple-element.171.refs_1_, bf16[768,2048]{1,0:T(8,128)(2,1)S(1)} %get-tuple-element.174.refs_2_.refs_4_), custom_call_target="tpu_custom_call" | custom-call | flops 400000000 | tf_op jit(solution)/shard_map/rise/pallas_call | solution.py:160
  57.5 2.9 %back.1 = (f32[768,512]{1,0:T(8,128)S(1)}, bf16[768,512]{1,0:T(8,128)(2,1)S(1)}, f32[4,512]{1,0:T(4,128)S(1)}) custom-call(f32[384,512]{1,0:T(8,128)S(1)} %get-tuple-element.144.refs_0_, f32[384,512]{1,0:T(8,128)S(1)} %get-tuple-element.148.refs_1_, f32[384,128]{1,0:T(8,128)S(1)} %get-tuple-element.149.refs_2_, f32[384,128]{1,0:T(8,128)S(1)} %get-tuple-element.150.refs_3_, ...), custom_call_target="tpu_custom_call" | custom-call | flops 800000000 | tf_op jit(solution)/shard_map/back/pallas_call | solution.py:160
  62.9 3.5 %rear0.1 = (bf16[432,1536]{1,0:T(8,128)(2,1)S(1)}, f32[2,512]{1,0:T(2,128)S(1)}) custom-call(bf16[384,512]{1,0:T(8,128)(2,1)S(1)} %get-tuple-element.183.q, bf16[432,512]{1,0:T(8,128)(2,1)S(1)} %get-tuple-element.184.k, bf16[432,512]{1,0:T(8,128)(2,1)S(1)} %get-tuple-element.185.v, bf16[3,4,192,256]{3,2,1,0:T(8,128)(2,1)S(1)} %get-tuple-element.186.p, ...), custom_call_target="tpu_custom_call" | custom-call | flops 700000000 | tf_op jit(solution)/shard_map/rear0/pallas_call | solution.py:160
  68.5 3.2 %rear1.1 = (bf16[432,1536]{1,0:T(8,128)(2,1)S(1)}, f32[2,512]{1,0:T(2,128)S(1)}) custom-call(bf16[384,512]{1,0:T(8,128)(2,1)S(1)} %get-tuple-element.194.q, bf16[432,512]{1,0:T(8,128)(2,1)S(1)} %get-tuple-element.195.k, bf16[432,512]{1,0:T(8,128)(2,1)S(1)} %get-tuple-element.196.v, bf16[3,4,192,256]{3,2,1,0:T(8,128)(2,1)S(1)} %get-tuple-element.197.p, ...), custom_call_target="tpu_custom_call" | custom-call | flops 700000000 | tf_op jit(solution)/shard_map/rear1/pallas_call | solution.py:160
  77.3 4.8 %base.1 = (bf16[2,4,64,2176]{3,2,1,0:T(8,128)(2,1)S(1)}, f32[2,384,512]{2,1,0:T(8,128)S(1)}, f32[16,512]{1,0:T(8,128)}) custom-call(f32[2,384,512]{2,1,0:T(8,128)S(1)} %get-tuple-element.138.units, f32[768,512]{1,0:T(8,128)S(1)} %get-tuple-element.205.dresid, bf16[512,1536]{1,0:T(8,128)(2,1)S(1)} %get-tuple-element.146.w_in_in.w_in, ...), custom_call_target="tpu_custom_call" | custom-call | flops 600000000 | tf_op jit(solution)/shard_map/base/pallas_call | solution.py:160
  82.9 2.6 %collective-permute-start.43 = (bf16[256,256]{1,0:T(8,128)(2,1)S(1)}, bf16[256,256]{1,0:T(8,128)(2,1)S(1)}, u32[]{:S(2)}, u32[]{:S(2)}) collective-permute-start(bf16[256,256]{1,0:T(8,128)(2,1)S(1)} %plus.10.refs_0_), channel_id=1, source_target_pairs={{0,16},{8,24},{16,0},{24,8},{1,17},{9,25},{17,1},{25,9},{2,18},{10... | collective-permute-start | bytes 393224 | tf_op jit(solution)/shard_map/ppermute | solution.py:621
  89.4 1.7 %collective-permute-done.42.refs_1_ = bf16[32,2048]{1,0:T(8,128)(2,1)S(1)} collective-permute-done((bf16[32,2048]{1,0:T(8,128)(2,1)S(1)}, bf16[32,2048]{1,0:T(8,128)(2,1)S(1)}, u32[]{:S(2)}, u32[]{:S(2)}) %collective-permute-start.42) | collective-permute-done | bytes 131104 | tf_op jit(solution)/shard_map/ppermute | solution.py:621
  92.7 2.7 %finish.1 = bf16[768,512]{1,0:T(8,128)(2,1)} custom-call(f32[16,512]{1,0:T(8,128)S(1)} %get-tuple-element.226.vecs_in.refs_3_.refs_6_.vecs, bf16[768,2048]{1,0:T(8,128)(2,1)S(1)} %get-tuple-element.221.hidden, bf16[2048,512]{1,0:T(8,128)(2,1)S(1)} %get-tuple-element.222.down, f32[384,512]{1,0:T(8,128)S(1)} %get-tuple-element.223.refs_0_, ...), custom_call_target="tpu_custom_call" | custom-call | flops 400000000 | tf_op jit(solution)/shard_map/finish/pallas_call | solution.py:160
  95.4 1.9 %shed.1 = f32[2,384,512]{2,1,0:T(8,128)} custom-call(f32[2,384,512]{2,1,0:T(8,128)S(1)} %get-tuple-element.138.units, f32[2,384,128]{2,1,0:T(8,128)S(1)} %get-tuple-element.225.scales, f32[768,512]{1,0:T(8,128)S(1)} %get-tuple-element.205.dresid, f32[16,512]{1,0:T(8,128)S(1)} %get-tuple-element.226.vecs_in.refs_3_.refs_6_.vecs, ...), custom_call_target="tpu_custom_call" | custom-call | flops 200000000 | tf_op jit(solution)/shard_map/shed/pallas_call | solution.py:160
  97.2 2.8 %collective-permute-done.44.refs_1_ = bf16[32,2048]{1,0:T(8,128)(2,1)S(1)} collective-permute-done((bf16[32,2048]{1,0:T(8,128)(2,1)S(1)}, bf16[32,2048]{1,0:T(8,128)(2,1)S(1)}, u32[]{:S(2)}, u32[]{:S(2)}) %collective-permute-start.44) | collective-permute-done | bytes 131104 | tf_op jit(solution)/shard_map/ppermute | solution.py:621
  101.5 2.4 %collective-permute-start.36 = (bf16[16,2176]{1,0:T(8,128)(2,1)S(1)}, bf16[16,2176]{1,0:T(8,128)(2,1)S(1)}, u32[]{:S(2)}, u32[]{:S(2)}) collective-permute-start(bf16[16,2176]{1,0:T(8,128)(2,1)S(1)} %get-tuple-element.232), channel_id=1, source_target_pairs={{0,24},{8,16},{16,8},{24,0},{1,25},{9,17},{17,9},{25,1},{2,26},{10... | collective-permute-start | bytes 208904 | tf_op jit(solution)/shard_map/ppermute | solution.py:621
  108.1 3.2 %collective-permute-done.37.refs_2_ = bf16[16,2176]{1,0:T(8,128)(2,1)S(1)} collective-permute-done((bf16[16,2176]{1,0:T(8,128)(2,1)S(1)}, bf16[16,2176]{1,0:T(8,128)(2,1)S(1)}, u32[]{:S(2)}, u32[]{:S(2)}) %collective-permute-start.37) | collective-permute-done | bytes 69664 | tf_op jit(solution)/shard_map/ppermute | solution.py:621
  111.3 2.5 %collective-permute-start.41 = (bf16[16,2176]{1,0:T(8,128)(2,1)S(1)}, bf16[16,2176]{1,0:T(8,128)(2,1)S(1)}, u32[]{:S(2)}, u32[]{:S(2)}) collective-permute-start(bf16[16,2176]{1,0:T(8,128)(2,1)S(1)} %plus.12.refs_0_), channel_id=1, source_target_pairs={{0,24},{8,16},{16,8},{24,0},{1,25},{9,17},{17,9},{25,1},{2,26},{10... | collective-permute-start | bytes 208904 | tf_op jit(solution)/shard_map/ppermute | solution.py:621
  113.8 2.0 %collective-permute-start.39 = (bf16[16,2176]{1,0:T(8,128)(2,1)S(1)}, bf16[16,2176]{1,0:T(8,128)(2,1)S(1)}, u32[]{:S(2)}, u32[]{:S(2)}) collective-permute-start(bf16[16,2176]{1,0:T(8,128)(2,1)S(1)} %plus.12.refs_0_), channel_id=1, source_target_pairs={{0,8},{8,0},{16,24},{24,16},{1,9},{9,1},{17,25},{25,17},{2,10},{10... | collective-permute-start | bytes 208904 | tf_op jit(solution)/shard_map/ppermute | solution.py:621
  117.8 2.6 %collective-permute-done.40.refs_2_ = bf16[16,2176]{1,0:T(8,128)(2,1)S(1)} collective-permute-done((bf16[16,2176]{1,0:T(8,128)(2,1)S(1)}, bf16[16,2176]{1,0:T(8,128)(2,1)S(1)}, u32[]{:S(2)}, u32[]{:S(2)}) %collective-permute-start.40) | collective-permute-done | bytes 69664 | tf_op jit(solution)/shard_map/ppermute | solution.py:621
  (122 shorter events, 46.3 us)
Async XLA Ops:
  3.0 11.3 %collective-permute-start = (bf16[272,512]{1,0:T(8,128)(2,1)}, bf16[272,512]{1,0:T(8,128)(2,1)S(1)}, u32[]{:S(2)}, u32[]{:S(2)}) collective-permute-start(bf16[272,512]{1,0:T(8,128)(2,1)} %pack.1.refs_0_), channel_id=1, source_target_pairs={{0,6},{1,7},{2,4},{3,5},{4,2},{5,3},{6,0},{7,1},{8,14},{9,15},{10,... | collective-permute-start | bytes 835592 | tf_op jit(solution)/shard_map/ppermute | solution.py:617
  6.5 13.4 %collective-permute-start.4 = (bf16[272,512]{1,0:T(8,128)(2,1)}, bf16[272,512]{1,0:T(8,128)(2,1)S(1)}, u32[]{:S(2)}, u32[]{:S(2)}) collective-permute-start(bf16[272,512]{1,0:T(8,128)(2,1)} %pack.1.refs_0_), channel_id=1, source_target_pairs={{0,4},{1,5},{2,6},{3,7},{4,0},{5,1},{6,2},{7,3},{8,12},{9,13},{10,... | collective-permute-start | bytes 835592 | tf_op jit(solution)/shard_map/ppermute | solution.py:617
  7.0 13.2 %collective-permute-start.3 = (bf16[272,512]{1,0:T(8,128)(2,1)}, bf16[272,512]{1,0:T(8,128)(2,1)S(1)}, u32[]{:S(2)}, u32[]{:S(2)}) collective-permute-start(bf16[272,512]{1,0:T(8,128)(2,1)} %pack.1.refs_0_), channel_id=1, source_target_pairs={{0,2},{1,3},{2,0},{3,1},{4,6},{5,7},{6,4},{7,5},{8,10},{9,11},{10,... | collective-permute-start | bytes 835592 | tf_op jit(solution)/shard_map/ppermute | solution.py:617
  14.2 7.9 %collective-permute-start.2 = (bf16[64,2048]{1,0:T(8,128)(2,1)}, bf16[64,2048]{1,0:T(8,128)(2,1)S(1)}, u32[]{:S(2)}, u32[]{:S(2)}) collective-permute-start(bf16[64,2048]{1,0:T(8,128)(2,1)} %refs_4_.2), channel_id=1, source_target_pairs={{0,1},{1,0},{2,3},{3,2},{4,5},{5,4},{6,7},{7,6},{8,9},{9,8},{10,11... | collective-permute-start | bytes 786440 | tf_op jit(solution)/shard_map/ppermute | solution.py:617
  14.2 8.5 %collective-permute-start.7 = (bf16[272,512]{1,0:T(8,128)(2,1)S(1)}, bf16[272,512]{1,0:T(8,128)(2,1)S(1)}, u32[]{:S(2)}, u32[]{:S(2)}) collective-permute-start(bf16[272,512]{1,0:T(8,128)(2,1)S(1)} %collective-permute-done.refs_4_), channel_id=1, source_target_pairs={{0,1},{1,0},{2,3},{3,2},{4,5},{5,4},{6,7},{7,6},{8,9},{9,8},{10,11... | collective-permute-start | bytes 835592 | tf_op jit(solution)/shard_map/ppermute | solution.py:617
  20.7 8.7 %collective-permute-start.9 = (bf16[64,2048]{1,0:T(8,128)(2,1)S(1)}, bf16[64,2048]{1,0:T(8,128)(2,1)S(1)}, u32[]{:S(2)}, u32[]{:S(2)}) collective-permute-start(bf16[64,2048]{1,0:T(8,128)(2,1)S(1)} %copy-done.5), channel_id=1, source_target_pairs={{0,4},{1,5},{2,6},{3,7},{4,0},{5,1},{6,2},{7,3},{8,12},{9,13},{10,... | collective-permute-start | bytes 786440 | tf_op jit(solution)/shard_map/ppermute | solution.py:617
  22.2 9.2 %collective-permute-start.8 = (bf16[64,2048]{1,0:T(8,128)(2,1)S(1)}, bf16[64,2048]{1,0:T(8,128)(2,1)S(1)}, u32[]{:S(2)}, u32[]{:S(2)}) collective-permute-start(bf16[64,2048]{1,0:T(8,128)(2,1)S(1)} %copy-done.5), channel_id=1, source_target_pairs={{0,2},{1,3},{2,0},{3,1},{4,6},{5,7},{6,4},{7,5},{8,10},{9,11},{10,... | collective-permute-start | bytes 786440 | tf_op jit(solution)/shard_map/ppermute | solution.py:617
  22.8 16.3 %collective-permute-start.12 = (bf16[64,2048]{1,0:T(8,128)(2,1)S(1)}, bf16[64,2048]{1,0:T(8,128)(2,1)S(1)}, u32[]{:S(2)}, u32[]{:S(2)}) collective-permute-start(bf16[64,2048]{1,0:T(8,128)(2,1)S(1)} %copy-done.5), channel_id=1, source_target_pairs={{0,6},{1,7},{2,4},{3,5},{4,2},{5,3},{6,0},{7,1},{8,14},{9,15},{10,... | collective-permute-start | bytes 786440 | tf_op jit(solution)/shard_map/ppermute | solution.py:617
  31.9 9.5 %collective-permute-start.11 = (bf16[256,512]{1,0:T(8,128)(2,1)S(1)}, bf16[256,512]{1,0:T(8,128)(2,1)S(1)}, u32[]{:S(2)}, u32[]{:S(2)}) collective-permute-start(bf16[256,512]{1,0:T(8,128)(2,1)S(1)} %copy-done.6), channel_id=1, source_target_pairs={{0,4},{1,5},{2,6},{3,7},{4,0},{5,1},{6,2},{7,3},{8,12},{9,13},{10,... | collective-permute-start | bytes 786440 | tf_op jit(solution)/shard_map/ppermute | solution.py:617
  32.5 8.9 %collective-permute-start.10 = (bf16[256,512]{1,0:T(8,128)(2,1)S(1)}, bf16[256,512]{1,0:T(8,128)(2,1)S(1)}, u32[]{:S(2)}, u32[]{:S(2)}) collective-permute-start(bf16[256,512]{1,0:T(8,128)(2,1)S(1)} %copy-done.6), channel_id=1, source_target_pairs={{0,2},{1,3},{2,0},{3,1},{4,6},{5,7},{6,4},{7,5},{8,10},{9,11},{10,... | collective-permute-start | bytes 786440 | tf_op jit(solution)/shard_map/ppermute | solution.py:617
  39.2 9.6 %collective-permute-start.17 = (bf16[256,512]{1,0:T(8,128)(2,1)S(1)}, bf16[256,512]{1,0:T(8,128)(2,1)S(1)}, u32[]{:S(2)}, u32[]{:S(2)}) collective-permute-start(bf16[256,512]{1,0:T(8,128)(2,1)S(1)} %copy-done.6), channel_id=1, source_target_pairs={{0,6},{1,7},{2,4},{3,5},{4,2},{5,3},{6,0},{7,1},{8,14},{9,15},{10,... | collective-permute-start | bytes 786440 | tf_op jit(solution)/shard_map/ppermute | solution.py:617
  55.5 10.8 %collective-permute-start.26 = (bf16[2,256,256]{2,1,0:T(8,128)(2,1)S(1)}, bf16[2,256,256]{2,1,0:T(8,128)(2,1)S(1)}, u32[]{:S(2)}, u32[]{:S(2)}) collective-permute-start(bf16[2,256,256]{2,1,0:T(8,128)(2,1)S(1)} %get-tuple-element.181), channel_id=1, source_target_pairs={{0,4},{1,5},{2,6},{3,7},{4,0},{5,1},{6,2},{7,3},{8,12},{9,13},{10,... | collective-permute-start | bytes 786440 | tf_op jit(solution)/shard_map/ppermute | solution.py:617
  56.6 9.8 %collective-permute-start.25 = (bf16[2,256,256]{2,1,0:T(8,128)(2,1)S(1)}, bf16[2,256,256]{2,1,0:T(8,128)(2,1)S(1)}, u32[]{:S(2)}, u32[]{:S(2)}) collective-permute-start(bf16[2,256,256]{2,1,0:T(8,128)(2,1)S(1)} %get-tuple-element.173), channel_id=1, source_target_pairs={{0,2},{1,3},{2,0},{3,1},{4,6},{5,7},{6,4},{7,5},{8,10},{9,11},{10,... | collective-permute-start | bytes 786440 | tf_op jit(solution)/shard_map/ppermute | solution.py:617
  60.7 11.0 %collective-permute-start.24 = (bf16[2,32,2048]{2,1,0:T(8,128)(2,1)S(1)}, bf16[2,32,2048]{2,1,0:T(8,128)(2,1)S(1)}, u32[]{:S(2)}, u32[]{:S(2)}) collective-permute-start(bf16[2,32,2048]{2,1,0:T(8,128)(2,1)S(1)} %get-tuple-element.180), channel_id=1, source_target_pairs={{0,4},{1,5},{2,6},{3,7},{4,0},{5,1},{6,2},{7,3},{8,12},{9,13},{10,... | collective-permute-start | bytes 786440 | tf_op jit(solution)/shard_map/ppermute | solution.py:617
  61.9 9.9 %collective-permute-start.23 = (bf16[2,32,2048]{2,1,0:T(8,128)(2,1)S(1)}, bf16[2,32,2048]{2,1,0:T(8,128)(2,1)S(1)}, u32[]{:S(2)}, u32[]{:S(2)}) collective-permute-start(bf16[2,32,2048]{2,1,0:T(8,128)(2,1)S(1)} %get-tuple-element.179), channel_id=1, source_target_pairs={{0,2},{1,3},{2,0},{3,1},{4,6},{5,7},{6,4},{7,5},{8,10},{9,11},{10,... | collective-permute-start | bytes 786440 | tf_op jit(solution)/shard_map/ppermute | solution.py:617
  73.4 8.6 %collective-permute-start.31 = (bf16[256,256]{1,0:T(8,128)(2,1)S(1)}, bf16[256,256]{1,0:T(8,128)(2,1)S(1)}, u32[]{:S(2)}, u32[]{:S(2)}) collective-permute-start(bf16[256,256]{1,0:T(8,128)(2,1)S(1)} %get-tuple-element.204), channel_id=1, source_target_pairs={{0,8},{8,0},{16,24},{24,16},{1,9},{9,1},{17,25},{25,17},{2,10},{10... | collective-permute-start | bytes 393224 | tf_op jit(solution)/shard_map/ppermute | solution.py:621
  82.4 8.7 %collective-permute-start.42 = (bf16[32,2048]{1,0:T(8,128)(2,1)S(1)}, bf16[32,2048]{1,0:T(8,128)(2,1)S(1)}, u32[]{:S(2)}, u32[]{:S(2)}) collective-permute-start(bf16[32,2048]{1,0:T(8,128)(2,1)S(1)} %get-tuple-element.216), channel_id=1, source_target_pairs={{0,8},{8,0},{16,24},{24,16},{1,9},{9,1},{17,25},{25,17},{2,10},{10... | collective-permute-start | bytes 393224 | tf_op jit(solution)/shard_map/ppermute | solution.py:621
  82.9 8.2 %collective-permute-start.43 = (bf16[256,256]{1,0:T(8,128)(2,1)S(1)}, bf16[256,256]{1,0:T(8,128)(2,1)S(1)}, u32[]{:S(2)}, u32[]{:S(2)}) collective-permute-start(bf16[256,256]{1,0:T(8,128)(2,1)S(1)} %plus.10.refs_0_), channel_id=1, source_target_pairs={{0,16},{8,24},{16,0},{24,8},{1,17},{9,25},{17,1},{25,9},{2,18},{10... | collective-permute-start | bytes 393224 | tf_op jit(solution)/shard_map/ppermute | solution.py:621
  85.9 15.2 %collective-permute-start.35 = (bf16[64,2176]{1,0:T(8,128)(2,1)S(1)}, bf16[64,2176]{1,0:T(8,128)(2,1)S(1)}, u32[]{:S(2)}, u32[]{:S(2)}) collective-permute-start(bf16[64,2176]{1,0:T(8,128)(2,1)S(1)} %get-tuple-element.266), channel_id=1, source_target_pairs={{0,6},{1,7},{2,4},{3,5},{4,2},{5,3},{6,0},{7,1},{8,14},{9,15},{10,... | collective-permute-start | bytes 835592 | tf_op jit(solution)/shard_map/ppermute | solution.py:617
  87.4 13.9 %collective-permute-start.34 = (bf16[64,2176]{1,0:T(8,128)(2,1)S(1)}, bf16[64,2176]{1,0:T(8,128)(2,1)S(1)}, u32[]{:S(2)}, u32[]{:S(2)}) collective-permute-start(bf16[64,2176]{1,0:T(8,128)(2,1)S(1)} %get-tuple-element.267), channel_id=1, source_target_pairs={{0,4},{1,5},{2,6},{3,7},{4,0},{5,1},{6,2},{7,3},{8,12},{9,13},{10,... | collective-permute-start | bytes 835592 | tf_op jit(solution)/shard_map/ppermute | solution.py:617
  88.2 13.0 %collective-permute-start.33 = (bf16[64,2176]{1,0:T(8,128)(2,1)S(1)}, bf16[64,2176]{1,0:T(8,128)(2,1)S(1)}, u32[]{:S(2)}, u32[]{:S(2)}) collective-permute-start(bf16[64,2176]{1,0:T(8,128)(2,1)S(1)} %get-tuple-element.268), channel_id=1, source_target_pairs={{0,2},{1,3},{2,0},{3,1},{4,6},{5,7},{6,4},{7,5},{8,10},{9,11},{10,... | collective-permute-start | bytes 835592 | tf_op jit(solution)/shard_map/ppermute | solution.py:617
  91.2 8.8 %collective-permute-start.44 = (bf16[32,2048]{1,0:T(8,128)(2,1)S(1)}, bf16[32,2048]{1,0:T(8,128)(2,1)S(1)}, u32[]{:S(2)}, u32[]{:S(2)}) collective-permute-start(bf16[32,2048]{1,0:T(8,128)(2,1)S(1)} %plus.13.refs_0_), channel_id=1, source_target_pairs={{0,16},{8,24},{16,0},{24,8},{1,17},{9,25},{17,1},{25,9},{2,18},{10... | collective-permute-start | bytes 393224 | tf_op jit(solution)/shard_map/ppermute | solution.py:621
  100.1 15.7 %collective-permute-start.45 = (bf16[32,2048]{1,0:T(8,128)(2,1)S(1)}, bf16[32,2048]{1,0:T(8,128)(2,1)S(1)}, u32[]{:S(2)}, u32[]{:S(2)}) collective-permute-start(bf16[32,2048]{1,0:T(8,128)(2,1)S(1)} %plus.14.keep), channel_id=1, source_target_pairs={{0,8},{8,0},{16,24},{24,16},{1,9},{9,1},{17,25},{25,17},{2,10},{10... | collective-permute-start | bytes 393224 | tf_op jit(solution)/shard_map/ppermute | solution.py:621
  106.0 10.6 %collective-permute-start.46 = (bf16[256,256]{1,0:T(8,128)(2,1)S(1)}, bf16[256,256]{1,0:T(8,128)(2,1)S(1)}, u32[]{:S(2)}, u32[]{:S(2)}) collective-permute-start(bf16[256,256]{1,0:T(8,128)(2,1)S(1)} %plus.15.keep), channel_id=1, source_target_pairs={{0,8},{8,0},{16,24},{24,16},{1,9},{9,1},{17,25},{25,17},{2,10},{10... | collective-permute-start | bytes 393224 | tf_op jit(solution)/shard_map/ppermute | solution.py:621
  (31 other events, 196.3 us)

commit v3 on v2

--- a/solution.py
+++ b/solution.py
@@ -476,8 +476,7 @@
     length, model = q.shape
     extent = k.shape[0]
     base = row * length
-    dk[...] = jnp.zeros_like(dk)
-    dv[...] = jnp.zeros_like(dv)
+    done = 0
     mixed[length:extent, 0:model] = jnp.zeros((extent - length, model), BF)
     for block in range(length // QB):
         first, _ = window(block, length)
@@ -497,12 +496,14 @@
             dscores = (wides * (back - inner)).astype(BF)
             gv = nn(probs, tops)
             gk = nn(dscores, queries)
-            dv[span, lanes] += gv[:WIN]
-            dv[own, lanes] = gv[WIN:]
-            dk[span, lanes] += gk[:WIN]
-            dk[own, lanes] = gk[WIN:]
+            for total, part in ((dv, gv), (dk, gk)):
+                if done > first:
+                    total[first:done, lanes] += part[: done - first]
+                total[max(first, done) : first + WIN, lanes] = part[max(done - first, 0) : WIN]
+                total[own, lanes] = part[WIN:]
             gq = diagonal(tn(keys, dscores)).T * 0.125
             mixed[rows, lanes] = gq.astype(BF)
+        done = first + WIN
     mixed[:, model : 2 * model] = dk[...].astype(BF)
     mixed[:, 2 * model :] = dv[...].astype(BF)
     sums[0:1] = jnp.sum(mixed[:, 0:model].astype(F32), axis=0, keepdims=True)

time: 121 us -> 121 us (level)
  no operation moved by 1% of the time
where the time goes in v3:
time: 121 us
  Pallas kernels  46.8 us (39%)
  starting transfers between devices  43.4 us (36%)
  waiting for transfers between devices  26.8 us (22%)
  local copies, waits for them, and re-layouts  3.25 us (3%)
    pallas_call x29, Pallas kernels, call(): pl.pallas_call(body, in_specs=[VMEM] * ins + [HBM] * (len(args) - ins), o...  35.3 us
    ppermute x35, starting transfers between devices, along(): return lax.ppermute(value, 'fsdp', [(i, i ^ offset) for i in range(8)])  26.5 us
    ppermute x12, starting transfers between devices, across(): return lax.ppermute(value, 'dp', [(i, i ^ offset) for i in range(size)])  16.9 us
    ppermute x35, waiting for transfers between devices, along(): return lax.ppermute(value, 'fsdp', [(i, i ^ offset) for i in range(8)])  14.9 us
    ppermute x12, waiting for transfers between devices, across(): return lax.ppermute(value, 'dp', [(i, i ^ offset) for i in range(size)])  11.9 us
    pallas_call x2, Pallas kernels, front(): pl.pallas_call(body, in_specs=specs, out_specs=[VMEM] * len(outs), out_sh...  10.2 us
    unnamed x16, local copies, waits for them, and re-layouts  2.97 us
  transfers between devices with their start and end apart: 47, of which 17 were waited for; matrix products, arithmetic and copies ran while one was open for 0% of the time, Pallas kernels for 34%

profile of v3, /device:TPU:0, one launch (start us, length us, event | category | flops | bytes accessed | tf_op | source)
XLA Modules:
  0.0 121.2 jit_solution(7509058807936424342)
XLA Ops:
  0.7 1.8 %pack.1.refs_0_ = bf16[272,512]{1,0:T(8,128)(2,1)} custom-call(bf16[64,1536]{1,0:T(8,128)(2,1)} %refs_0_.1, bf16[64,512]{1,0:T(8,128)(2,1)} %refs_1_.1, bf16[64]{0:T(256)(128)(2,1)} %refs_2_.1, bf16[64]{0:T(256)(128)(2,1)} %refs_3_.1, bf16[64]{0:T(256)(128)(2,1)} %refs_4_.1, bf16[64]{0:T(256)(128)(2,1)} %refs_5_.1, bf16[64]{0:T(256)(128)(2,1)} %refs_6_.1, ...), custom_call_target="tpu_custom_call" | custom-call | flops 200000000 | tf_op jit(solution)/shard_map/pack/pallas_call | solution.py:160
  3.0 3.5 %collective-permute-start = (bf16[272,512]{1,0:T(8,128)(2,1)}, bf16[272,512]{1,0:T(8,128)(2,1)S(1)}, u32[]{:S(2)}, u32[]{:S(2)}) collective-permute-start(bf16[272,512]{1,0:T(8,128)(2,1)} %pack.1.refs_0_), channel_id=1, source_target_pairs={{0,6},{1,7},{2,4},{3,5},{4,2},{5,3},{6,0},{7,1},{8,14},{9,15},{10,... | collective-permute-start | bytes 835592 | tf_op jit(solution)/shard_map/ppermute | solution.py:618
  10.2 4.0 %collective-permute-done.refs_4_ = bf16[272,512]{1,0:T(8,128)(2,1)S(1)} collective-permute-done((bf16[272,512]{1,0:T(8,128)(2,1)}, bf16[272,512]{1,0:T(8,128)(2,1)S(1)}, u32[]{:S(2)}, u32[]{:S(2)}) %collective-permute-start) | collective-permute-done | bytes 278560 | tf_op jit(solution)/shard_map/ppermute | solution.py:618
  16.1 3.8 %collective-permute-done.4.refs_3_ = bf16[272,512]{1,0:T(8,128)(2,1)S(1)} collective-permute-done((bf16[272,512]{1,0:T(8,128)(2,1)}, bf16[272,512]{1,0:T(8,128)(2,1)S(1)}, u32[]{:S(2)}, u32[]{:S(2)}) %collective-permute-start.4) | collective-permute-done | bytes 278560 | tf_op jit(solution)/shard_map/ppermute | solution.py:618
  24.3 5.2 %front0.1 = (f32[16,512]{1,0:T(8,128)S(1)}, bf16[512,1536]{1,0:T(8,128)(2,1)S(1)}, bf16[512,512]{1,0:T(8,128)(2,1)S(1)}, bf16[384,512]{1,0:T(8,128)(2,1)S(1)}, b...) custom-call(bf16[2,384,512]{2,1,0:T(8,128)(2,1)S(1)} %bitcast.22, ...), custom_call_target="tpu_custom_call" | custom-call | flops 700000000 | tf_op jit(solution)/shard_map/front0/pallas_call | solution.py:305
  29.5 1.9 %collective-permute-done.8.refs_6_ = bf16[64,2048]{1,0:T(8,128)(2,1)S(1)} collective-permute-done((bf16[64,2048]{1,0:T(8,128)(2,1)S(1)}, bf16[64,2048]{1,0:T(8,128)(2,1)S(1)}, u32[]{:S(2)}, u32[]{:S(2)}) %collective-permute-start.8) | collective-permute-done | bytes 262176 | tf_op jit(solution)/shard_map/ppermute | solution.py:618
  34.0 5.0 %front1.1 = (bf16[384,512]{1,0:T(8,128)(2,1)S(1)}, bf16[432,512]{1,0:T(8,128)(2,1)S(1)}, bf16[432,512]{1,0:T(8,128)(2,1)S(1)}, bf16[512,432]{1,0:T(8,128)(2,1)S(...) custom-call(bf16[2,384,512]{2,1,0:T(8,128)(2,1)S(1)} %bitcast.23, ...), custom_call_target="tpu_custom_call" | custom-call | flops 700000000 | tf_op jit(solution)/shard_map/front1/pallas_call | solution.py:305
  41.9 6.2 %middle.1 = (bf16[768,2048]{1,0:T(8,128)(2,1)S(1)}, bf16[768,2048]{1,0:T(8,128)(2,1)S(1)}, bf16[512,2048]{1,0:T(8,128)(2,1)S(1)}, bf16[2,4,512,256]{3,2,1,0:T(8,128)(2,1)S(1)}) custom-call(bf16[384,512]{1,0:T(8,128)(2,1)S(1)} %get-tuple-element.151.refs_0_, bf16[384,512]{1,0:T(8,128)(2,1)S(1)} %get-tuple-element.152.refs_1_, ...), custom_call_target="tpu_custom_call" | custom-call | flops 800000000 | tf_op jit(solution)/shard_map/middle/pallas_call | solution.py:160
  50.3 2.1 %turn.1 = (bf16[768,2048]{1,0:T(8,128)(2,1)S(1)}, f32[4,512]{1,0:T(4,128)S(1)}, bf16[2048,512]{1,0:T(8,128)(2,1)S(1)}) custom-call(bf16[768,512]{1,0:T(8,128)(2,1)S(1)} %bitcast.25, bf16[768,2048]{1,0:T(8,128)(2,1)S(1)} %get-tuple-element.163.slopes, bf16[256,512]{1,0:T(8,128)(2,1)S(1)} %copy-done.6, bf16[256,512]{1,0:T(8,128)(2,1)S(1)} %collective-permute-done.16.refs_1_, ...), custom_call_target="tpu_custom_call" | custom-call | flops 500000000 | tf_op jit(solution)/shard_map/turn/pallas_call | solution.py:160
  52.7 1.8 %rise.1.both = bf16[2,4,64,2048]{3,2,1,0:T(8,128)(2,1)S(1)} custom-call(bf16[512,384]{1,0:T(8,128)(2,1)S(1)} %get-tuple-element.170.refs_0_, bf16[512,384]{1,0:T(8,128)(2,1)S(1)} %get-tuple-element.171.refs_1_, bf16[768,2048]{1,0:T(8,128)(2,1)S(1)} %get-tuple-element.174.refs_2_.refs_4_), custom_call_target="tpu_custom_call" | custom-call | flops 400000000 | tf_op jit(solution)/shard_map/rise/pallas_call | solution.py:160
  57.5 2.9 %back.1 = (f32[768,512]{1,0:T(8,128)S(1)}, bf16[768,512]{1,0:T(8,128)(2,1)S(1)}, f32[4,512]{1,0:T(4,128)S(1)}) custom-call(f32[384,512]{1,0:T(8,128)S(1)} %get-tuple-element.144.refs_0_, f32[384,512]{1,0:T(8,128)S(1)} %get-tuple-element.148.refs_1_, f32[384,128]{1,0:T(8,128)S(1)} %get-tuple-element.149.refs_2_, f32[384,128]{1,0:T(8,128)S(1)} %get-tuple-element.150.refs_3_, ...), custom_call_target="tpu_custom_call" | custom-call | flops 800000000 | tf_op jit(solution)/shard_map/back/pallas_call | solution.py:160
  62.9 3.5 %rear0.1 = (bf16[432,1536]{1,0:T(8,128)(2,1)S(1)}, f32[2,512]{1,0:T(2,128)S(1)}) custom-call(bf16[384,512]{1,0:T(8,128)(2,1)S(1)} %get-tuple-element.183.q, bf16[432,512]{1,0:T(8,128)(2,1)S(1)} %get-tuple-element.184.k, bf16[432,512]{1,0:T(8,128)(2,1)S(1)} %get-tuple-element.185.v, bf16[3,4,192,256]{3,2,1,0:T(8,128)(2,1)S(1)} %get-tuple-element.186.p, ...), custom_call_target="tpu_custom_call" | custom-call | flops 700000000 | tf_op jit(solution)/shard_map/rear0/pallas_call | solution.py:160
  68.5 3.2 %rear1.1 = (bf16[432,1536]{1,0:T(8,128)(2,1)S(1)}, f32[2,512]{1,0:T(2,128)S(1)}) custom-call(bf16[384,512]{1,0:T(8,128)(2,1)S(1)} %get-tuple-element.194.q, bf16[432,512]{1,0:T(8,128)(2,1)S(1)} %get-tuple-element.195.k, bf16[432,512]{1,0:T(8,128)(2,1)S(1)} %get-tuple-element.196.v, bf16[3,4,192,256]{3,2,1,0:T(8,128)(2,1)S(1)} %get-tuple-element.197.p, ...), custom_call_target="tpu_custom_call" | custom-call | flops 700000000 | tf_op jit(solution)/shard_map/rear1/pallas_call | solution.py:160
  77.3 4.8 %base.1 = (bf16[2,4,64,2176]{3,2,1,0:T(8,128)(2,1)S(1)}, f32[2,384,512]{2,1,0:T(8,128)S(1)}, f32[16,512]{1,0:T(8,128)}) custom-call(f32[2,384,512]{2,1,0:T(8,128)S(1)} %get-tuple-element.138.units, f32[768,512]{1,0:T(8,128)S(1)} %get-tuple-element.205.dresid, bf16[512,1536]{1,0:T(8,128)(2,1)S(1)} %get-tuple-element.146.w_in_in.w_in, ...), custom_call_target="tpu_custom_call" | custom-call | flops 600000000 | tf_op jit(solution)/shard_map/base/pallas_call | solution.py:160
  82.9 2.6 %collective-permute-start.43 = (bf16[256,256]{1,0:T(8,128)(2,1)S(1)}, bf16[256,256]{1,0:T(8,128)(2,1)S(1)}, u32[]{:S(2)}, u32[]{:S(2)}) collective-permute-start(bf16[256,256]{1,0:T(8,128)(2,1)S(1)} %plus.10.refs_0_), channel_id=1, source_target_pairs={{0,16},{8,24},{16,0},{24,8},{1,17},{9,25},{17,1},{25,9},{2,18},{10... | collective-permute-start | bytes 393224 | tf_op jit(solution)/shard_map/ppermute | solution.py:622
  89.4 1.7 %collective-permute-done.42.refs_1_ = bf16[32,2048]{1,0:T(8,128)(2,1)S(1)} collective-permute-done((bf16[32,2048]{1,0:T(8,128)(2,1)S(1)}, bf16[32,2048]{1,0:T(8,128)(2,1)S(1)}, u32[]{:S(2)}, u32[]{:S(2)}) %collective-permute-start.42) | collective-permute-done | bytes 131104 | tf_op jit(solution)/shard_map/ppermute | solution.py:622
  92.7 2.7 %finish.1 = bf16[768,512]{1,0:T(8,128)(2,1)} custom-call(f32[16,512]{1,0:T(8,128)S(1)} %get-tuple-element.226.vecs_in.refs_3_.refs_6_.vecs, bf16[768,2048]{1,0:T(8,128)(2,1)S(1)} %get-tuple-element.221.hidden, bf16[2048,512]{1,0:T(8,128)(2,1)S(1)} %get-tuple-element.222.down, f32[384,512]{1,0:T(8,128)S(1)} %get-tuple-element.223.refs_0_, ...), custom_call_target="tpu_custom_call" | custom-call | flops 400000000 | tf_op jit(solution)/shard_map/finish/pallas_call | solution.py:160
  95.4 1.9 %shed.1 = f32[2,384,512]{2,1,0:T(8,128)} custom-call(f32[2,384,512]{2,1,0:T(8,128)S(1)} %get-tuple-element.138.units, f32[2,384,128]{2,1,0:T(8,128)S(1)} %get-tuple-element.225.scales, f32[768,512]{1,0:T(8,128)S(1)} %get-tuple-element.205.dresid, f32[16,512]{1,0:T(8,128)S(1)} %get-tuple-element.226.vecs_in.refs_3_.refs_6_.vecs, ...), custom_call_target="tpu_custom_call" | custom-call | flops 200000000 | tf_op jit(solution)/shard_map/shed/pallas_call | solution.py:160
  97.2 2.8 %collective-permute-done.44.refs_1_ = bf16[32,2048]{1,0:T(8,128)(2,1)S(1)} collective-permute-done((bf16[32,2048]{1,0:T(8,128)(2,1)S(1)}, bf16[32,2048]{1,0:T(8,128)(2,1)S(1)}, u32[]{:S(2)}, u32[]{:S(2)}) %collective-permute-start.44) | collective-permute-done | bytes 131104 | tf_op jit(solution)/shard_map/ppermute | solution.py:622
  101.5 2.4 %collective-permute-start.36 = (bf16[16,2176]{1,0:T(8,128)(2,1)S(1)}, bf16[16,2176]{1,0:T(8,128)(2,1)S(1)}, u32[]{:S(2)}, u32[]{:S(2)}) collective-permute-start(bf16[16,2176]{1,0:T(8,128)(2,1)S(1)} %get-tuple-element.232), channel_id=1, source_target_pairs={{0,24},{8,16},{16,8},{24,0},{1,25},{9,17},{17,9},{25,1},{2,26},{10... | collective-permute-start | bytes 208904 | tf_op jit(solution)/shard_map/ppermute | solution.py:622
  108.1 3.2 %collective-permute-done.37.refs_2_ = bf16[16,2176]{1,0:T(8,128)(2,1)S(1)} collective-permute-done((bf16[16,2176]{1,0:T(8,128)(2,1)S(1)}, bf16[16,2176]{1,0:T(8,128)(2,1)S(1)}, u32[]{:S(2)}, u32[]{:S(2)}) %collective-permute-start.37) | collective-permute-done | bytes 69664 | tf_op jit(solution)/shard_map/ppermute | solution.py:622
  111.3 2.5 %collective-permute-start.41 = (bf16[16,2176]{1,0:T(8,128)(2,1)S(1)}, bf16[16,2176]{1,0:T(8,128)(2,1)S(1)}, u32[]{:S(2)}, u32[]{:S(2)}) collective-permute-start(bf16[16,2176]{1,0:T(8,128)(2,1)S(1)} %plus.12.refs_0_), channel_id=1, source_target_pairs={{0,24},{8,16},{16,8},{24,0},{1,25},{9,17},{17,9},{25,1},{2,26},{10... | collective-permute-start | bytes 208904 | tf_op jit(solution)/shard_map/ppermute | solution.py:622
  113.8 2.0 %collective-permute-start.39 = (bf16[16,2176]{1,0:T(8,128)(2,1)S(1)}, bf16[16,2176]{1,0:T(8,128)(2,1)S(1)}, u32[]{:S(2)}, u32[]{:S(2)}) collective-permute-start(bf16[16,2176]{1,0:T(8,128)(2,1)S(1)} %plus.12.refs_0_), channel_id=1, source_target_pairs={{0,8},{8,0},{16,24},{24,16},{1,9},{9,1},{17,25},{25,17},{2,10},{10... | collective-permute-start | bytes 208904 | tf_op jit(solution)/shard_map/ppermute | solution.py:622
  117.8 2.6 %collective-permute-done.40.refs_2_ = bf16[16,2176]{1,0:T(8,128)(2,1)S(1)} collective-permute-done((bf16[16,2176]{1,0:T(8,128)(2,1)S(1)}, bf16[16,2176]{1,0:T(8,128)(2,1)S(1)}, u32[]{:S(2)}, u32[]{:S(2)}) %collective-permute-start.40) | collective-permute-done | bytes 69664 | tf_op jit(solution)/shard_map/ppermute | solution.py:622
  (122 shorter events, 46.3 us)
Async XLA Ops:
  3.0 11.3 %collective-permute-start = (bf16[272,512]{1,0:T(8,128)(2,1)}, bf16[272,512]{1,0:T(8,128)(2,1)S(1)}, u32[]{:S(2)}, u32[]{:S(2)}) collective-permute-start(bf16[272,512]{1,0:T(8,128)(2,1)} %pack.1.refs_0_), channel_id=1, source_target_pairs={{0,6},{1,7},{2,4},{3,5},{4,2},{5,3},{6,0},{7,1},{8,14},{9,15},{10,... | collective-permute-start | bytes 835592 | tf_op jit(solution)/shard_map/ppermute | solution.py:618
  6.5 13.4 %collective-permute-start.4 = (bf16[272,512]{1,0:T(8,128)(2,1)}, bf16[272,512]{1,0:T(8,128)(2,1)S(1)}, u32[]{:S(2)}, u32[]{:S(2)}) collective-permute-start(bf16[272,512]{1,0:T(8,128)(2,1)} %pack.1.refs_0_), channel_id=1, source_target_pairs={{0,4},{1,5},{2,6},{3,7},{4,0},{5,1},{6,2},{7,3},{8,12},{9,13},{10,... | collective-permute-start | bytes 835592 | tf_op jit(solution)/shard_map/ppermute | solution.py:618
  7.0 13.2 %collective-permute-start.3 = (bf16[272,512]{1,0:T(8,128)(2,1)}, bf16[272,512]{1,0:T(8,128)(2,1)S(1)}, u32[]{:S(2)}, u32[]{:S(2)}) collective-permute-start(bf16[272,512]{1,0:T(8,128)(2,1)} %pack.1.refs_0_), channel_id=1, source_target_pairs={{0,2},{1,3},{2,0},{3,1},{4,6},{5,7},{6,4},{7,5},{8,10},{9,11},{10,... | collective-permute-start | bytes 835592 | tf_op jit(solution)/shard_map/ppermute | solution.py:618
  14.2 7.9 %collective-permute-start.2 = (bf16[64,2048]{1,0:T(8,128)(2,1)}, bf16[64,2048]{1,0:T(8,128)(2,1)S(1)}, u32[]{:S(2)}, u32[]{:S(2)}) collective-permute-start(bf16[64,2048]{1,0:T(8,128)(2,1)} %refs_4_.2), channel_id=1, source_target_pairs={{0,1},{1,0},{2,3},{3,2},{4,5},{5,4},{6,7},{7,6},{8,9},{9,8},{10,11... | collective-permute-start | bytes 786440 | tf_op jit(solution)/shard_map/ppermute | solution.py:618
  14.2 8.5 %collective-permute-start.7 = (bf16[272,512]{1,0:T(8,128)(2,1)S(1)}, bf16[272,512]{1,0:T(8,128)(2,1)S(1)}, u32[]{:S(2)}, u32[]{:S(2)}) collective-permute-start(bf16[272,512]{1,0:T(8,128)(2,1)S(1)} %collective-permute-done.refs_4_), channel_id=1, source_target_pairs={{0,1},{1,0},{2,3},{3,2},{4,5},{5,4},{6,7},{7,6},{8,9},{9,8},{10,11... | collective-permute-start | bytes 835592 | tf_op jit(solution)/shard_map/ppermute | solution.py:618
  20.7 8.7 %collective-permute-start.9 = (bf16[64,2048]{1,0:T(8,128)(2,1)S(1)}, bf16[64,2048]{1,0:T(8,128)(2,1)S(1)}, u32[]{:S(2)}, u32[]{:S(2)}) collective-permute-start(bf16[64,2048]{1,0:T(8,128)(2,1)S(1)} %copy-done.5), channel_id=1, source_target_pairs={{0,4},{1,5},{2,6},{3,7},{4,0},{5,1},{6,2},{7,3},{8,12},{9,13},{10,... | collective-permute-start | bytes 786440 | tf_op jit(solution)/shard_map/ppermute | solution.py:618
  22.2 9.2 %collective-permute-start.8 = (bf16[64,2048]{1,0:T(8,128)(2,1)S(1)}, bf16[64,2048]{1,0:T(8,128)(2,1)S(1)}, u32[]{:S(2)}, u32[]{:S(2)}) collective-permute-start(bf16[64,2048]{1,0:T(8,128)(2,1)S(1)} %copy-done.5), channel_id=1, source_target_pairs={{0,2},{1,3},{2,0},{3,1},{4,6},{5,7},{6,4},{7,5},{8,10},{9,11},{10,... | collective-permute-start | bytes 786440 | tf_op jit(solution)/shard_map/ppermute | solution.py:618
  22.8 16.3 %collective-permute-start.12 = (bf16[64,2048]{1,0:T(8,128)(2,1)S(1)}, bf16[64,2048]{1,0:T(8,128)(2,1)S(1)}, u32[]{:S(2)}, u32[]{:S(2)}) collective-permute-start(bf16[64,2048]{1,0:T(8,128)(2,1)S(1)} %copy-done.5), channel_id=1, source_target_pairs={{0,6},{1,7},{2,4},{3,5},{4,2},{5,3},{6,0},{7,1},{8,14},{9,15},{10,... | collective-permute-start | bytes 786440 | tf_op jit(solution)/shard_map/ppermute | solution.py:618
  31.9 9.5 %collective-permute-start.11 = (bf16[256,512]{1,0:T(8,128)(2,1)S(1)}, bf16[256,512]{1,0:T(8,128)(2,1)S(1)}, u32[]{:S(2)}, u32[]{:S(2)}) collective-permute-start(bf16[256,512]{1,0:T(8,128)(2,1)S(1)} %copy-done.6), channel_id=1, source_target_pairs={{0,4},{1,5},{2,6},{3,7},{4,0},{5,1},{6,2},{7,3},{8,12},{9,13},{10,... | collective-permute-start | bytes 786440 | tf_op jit(solution)/shard_map/ppermute | solution.py:618
  32.5 8.9 %collective-permute-start.10 = (bf16[256,512]{1,0:T(8,128)(2,1)S(1)}, bf16[256,512]{1,0:T(8,128)(2,1)S(1)}, u32[]{:S(2)}, u32[]{:S(2)}) collective-permute-start(bf16[256,512]{1,0:T(8,128)(2,1)S(1)} %copy-done.6), channel_id=1, source_target_pairs={{0,2},{1,3},{2,0},{3,1},{4,6},{5,7},{6,4},{7,5},{8,10},{9,11},{10,... | collective-permute-start | bytes 786440 | tf_op jit(solution)/shard_map/ppermute | solution.py:618
  39.2 9.6 %collective-permute-start.17 = (bf16[256,512]{1,0:T(8,128)(2,1)S(1)}, bf16[256,512]{1,0:T(8,128)(2,1)S(1)}, u32[]{:S(2)}, u32[]{:S(2)}) collective-permute-start(bf16[256,512]{1,0:T(8,128)(2,1)S(1)} %copy-done.6), channel_id=1, source_target_pairs={{0,6},{1,7},{2,4},{3,5},{4,2},{5,3},{6,0},{7,1},{8,14},{9,15},{10,... | collective-permute-start | bytes 786440 | tf_op jit(solution)/shard_map/ppermute | solution.py:618
  55.5 10.8 %collective-permute-start.26 = (bf16[2,256,256]{2,1,0:T(8,128)(2,1)S(1)}, bf16[2,256,256]{2,1,0:T(8,128)(2,1)S(1)}, u32[]{:S(2)}, u32[]{:S(2)}) collective-permute-start(bf16[2,256,256]{2,1,0:T(8,128)(2,1)S(1)} %get-tuple-element.181), channel_id=1, source_target_pairs={{0,4},{1,5},{2,6},{3,7},{4,0},{5,1},{6,2},{7,3},{8,12},{9,13},{10,... | collective-permute-start | bytes 786440 | tf_op jit(solution)/shard_map/ppermute | solution.py:618
  56.6 9.8 %collective-permute-start.25 = (bf16[2,256,256]{2,1,0:T(8,128)(2,1)S(1)}, bf16[2,256,256]{2,1,0:T(8,128)(2,1)S(1)}, u32[]{:S(2)}, u32[]{:S(2)}) collective-permute-start(bf16[2,256,256]{2,1,0:T(8,128)(2,1)S(1)} %get-tuple-element.173), channel_id=1, source_target_pairs={{0,2},{1,3},{2,0},{3,1},{4,6},{5,7},{6,4},{7,5},{8,10},{9,11},{10,... | collective-permute-start | bytes 786440 | tf_op jit(solution)/shard_map/ppermute | solution.py:618
  60.7 11.0 %collective-permute-start.24 = (bf16[2,32,2048]{2,1,0:T(8,128)(2,1)S(1)}, bf16[2,32,2048]{2,1,0:T(8,128)(2,1)S(1)}, u32[]{:S(2)}, u32[]{:S(2)}) collective-permute-start(bf16[2,32,2048]{2,1,0:T(8,128)(2,1)S(1)} %get-tuple-element.180), channel_id=1, source_target_pairs={{0,4},{1,5},{2,6},{3,7},{4,0},{5,1},{6,2},{7,3},{8,12},{9,13},{10,... | collective-permute-start | bytes 786440 | tf_op jit(solution)/shard_map/ppermute | solution.py:618
  61.9 9.9 %collective-permute-start.23 = (bf16[2,32,2048]{2,1,0:T(8,128)(2,1)S(1)}, bf16[2,32,2048]{2,1,0:T(8,128)(2,1)S(1)}, u32[]{:S(2)}, u32[]{:S(2)}) collective-permute-start(bf16[2,32,2048]{2,1,0:T(8,128)(2,1)S(1)} %get-tuple-element.179), channel_id=1, source_target_pairs={{0,2},{1,3},{2,0},{3,1},{4,6},{5,7},{6,4},{7,5},{8,10},{9,11},{10,... | collective-permute-start | bytes 786440 | tf_op jit(solution)/shard_map/ppermute | solution.py:618
  73.4 8.6 %collective-permute-start.31 = (bf16[256,256]{1,0:T(8,128)(2,1)S(1)}, bf16[256,256]{1,0:T(8,128)(2,1)S(1)}, u32[]{:S(2)}, u32[]{:S(2)}) collective-permute-start(bf16[256,256]{1,0:T(8,128)(2,1)S(1)} %get-tuple-element.204), channel_id=1, source_target_pairs={{0,8},{8,0},{16,24},{24,16},{1,9},{9,1},{17,25},{25,17},{2,10},{10... | collective-permute-start | bytes 393224 | tf_op jit(solution)/shard_map/ppermute | solution.py:622
  82.4 8.7 %collective-permute-start.42 = (bf16[32,2048]{1,0:T(8,128)(2,1)S(1)}, bf16[32,2048]{1,0:T(8,128)(2,1)S(1)}, u32[]{:S(2)}, u32[]{:S(2)}) collective-permute-start(bf16[32,2048]{1,0:T(8,128)(2,1)S(1)} %get-tuple-element.216), channel_id=1, source_target_pairs={{0,8},{8,0},{16,24},{24,16},{1,9},{9,1},{17,25},{25,17},{2,10},{10... | collective-permute-start | bytes 393224 | tf_op jit(solution)/shard_map/ppermute | solution.py:622
  82.9 8.2 %collective-permute-start.43 = (bf16[256,256]{1,0:T(8,128)(2,1)S(1)}, bf16[256,256]{1,0:T(8,128)(2,1)S(1)}, u32[]{:S(2)}, u32[]{:S(2)}) collective-permute-start(bf16[256,256]{1,0:T(8,128)(2,1)S(1)} %plus.10.refs_0_), channel_id=1, source_target_pairs={{0,16},{8,24},{16,0},{24,8},{1,17},{9,25},{17,1},{25,9},{2,18},{10... | collective-permute-start | bytes 393224 | tf_op jit(solution)/shard_map/ppermute | solution.py:622
  85.9 15.2 %collective-permute-start.35 = (bf16[64,2176]{1,0:T(8,128)(2,1)S(1)}, bf16[64,2176]{1,0:T(8,128)(2,1)S(1)}, u32[]{:S(2)}, u32[]{:S(2)}) collective-permute-start(bf16[64,2176]{1,0:T(8,128)(2,1)S(1)} %get-tuple-element.266), channel_id=1, source_target_pairs={{0,6},{1,7},{2,4},{3,5},{4,2},{5,3},{6,0},{7,1},{8,14},{9,15},{10,... | collective-permute-start | bytes 835592 | tf_op jit(solution)/shard_map/ppermute | solution.py:618
  87.4 13.9 %collective-permute-start.34 = (bf16[64,2176]{1,0:T(8,128)(2,1)S(1)}, bf16[64,2176]{1,0:T(8,128)(2,1)S(1)}, u32[]{:S(2)}, u32[]{:S(2)}) collective-permute-start(bf16[64,2176]{1,0:T(8,128)(2,1)S(1)} %get-tuple-element.267), channel_id=1, source_target_pairs={{0,4},{1,5},{2,6},{3,7},{4,0},{5,1},{6,2},{7,3},{8,12},{9,13},{10,... | collective-permute-start | bytes 835592 | tf_op jit(solution)/shard_map/ppermute | solution.py:618
  88.2 13.0 %collective-permute-start.33 = (bf16[64,2176]{1,0:T(8,128)(2,1)S(1)}, bf16[64,2176]{1,0:T(8,128)(2,1)S(1)}, u32[]{:S(2)}, u32[]{:S(2)}) collective-permute-start(bf16[64,2176]{1,0:T(8,128)(2,1)S(1)} %get-tuple-element.268), channel_id=1, source_target_pairs={{0,2},{1,3},{2,0},{3,1},{4,6},{5,7},{6,4},{7,5},{8,10},{9,11},{10,... | collective-permute-start | bytes 835592 | tf_op jit(solution)/shard_map/ppermute | solution.py:618
  91.2 8.8 %collective-permute-start.44 = (bf16[32,2048]{1,0:T(8,128)(2,1)S(1)}, bf16[32,2048]{1,0:T(8,128)(2,1)S(1)}, u32[]{:S(2)}, u32[]{:S(2)}) collective-permute-start(bf16[32,2048]{1,0:T(8,128)(2,1)S(1)} %plus.13.refs_0_), channel_id=1, source_target_pairs={{0,16},{8,24},{16,0},{24,8},{1,17},{9,25},{17,1},{25,9},{2,18},{10... | collective-permute-start | bytes 393224 | tf_op jit(solution)/shard_map/ppermute | solution.py:622
  100.1 15.7 %collective-permute-start.45 = (bf16[32,2048]{1,0:T(8,128)(2,1)S(1)}, bf16[32,2048]{1,0:T(8,128)(2,1)S(1)}, u32[]{:S(2)}, u32[]{:S(2)}) collective-permute-start(bf16[32,2048]{1,0:T(8,128)(2,1)S(1)} %plus.14.keep), channel_id=1, source_target_pairs={{0,8},{8,0},{16,24},{24,16},{1,9},{9,1},{17,25},{25,17},{2,10},{10... | collective-permute-start | bytes 393224 | tf_op jit(solution)/shard_map/ppermute | solution.py:622
  106.0 10.6 %collective-permute-start.46 = (bf16[256,256]{1,0:T(8,128)(2,1)S(1)}, bf16[256,256]{1,0:T(8,128)(2,1)S(1)}, u32[]{:S(2)}, u32[]{:S(2)}) collective-permute-start(bf16[256,256]{1,0:T(8,128)(2,1)S(1)} %plus.15.keep), channel_id=1, source_target_pairs={{0,8},{8,0},{16,24},{24,16},{1,9},{9,1},{17,25},{25,17},{2,10},{10... | collective-permute-start | bytes 393224 | tf_op jit(solution)/shard_map/ppermute | solution.py:622
  (31 other events, 196.3 us)
